TPU v7x, 32 devices: a whole 2x2x4 slice. The times are simulated.
32 devices in a mesh: dom: 4 (over y, core), orb: 8 (over z, x).
Axes of the slice: x: 2, y: 2, z: 4, core: 2. Of those that a mesh axis runs over, the one named last changes fastest.
Arguments:
- psi: float32 [12288, 2048], P('dom', 'orb'), may hold values from -6 to 6
- rot: float32 [2048, 2048], P(None, 'orb'), may hold values from -0.125 to 0.125
- occ: float32 [2048], P('orb'), may hold values from 0.1 to 2
- v_loc: float32 [12288], P('dom'), may hold values from -1 to 1
Outputs:
- rotated: float32 [12288, 2048], P('dom', 'orb')
- density: float32 [12288], P('dom')
- hpsi: float32 [12288, 2048], P('dom', 'orb')
- band: float32 [2048], P('orb')
All inputs are finite; a program needn't handle non-finite values.
Results may differ from a plain program's by a relative error of at most 0.000075.
Values sent between devices are 32-bit elements; how exact they have to be, the bound alone decides.
No kernel may reach another device: no remote copies, remote signals or barrier semaphores. Data moves between devices by JAX's collectives and lax.ppermute only.
A program may use at most 128 MiB of HBM per device.

v0:
```python
import jax
import jax.numpy as jnp
from jax import lax
from jax.sharding import PartitionSpec as P

M = 2048
PLANES_DEV = 3
NY = 8
NZ = 128


def with_halo(cells, sides, width):
    for axis, dim in sides:
        count = lax.axis_size(axis)
        head = lax.slice_in_dim(cells, 0, width, axis=dim)
        tail = lax.slice_in_dim(cells, cells.shape[dim] - width, cells.shape[dim], axis=dim)
        cells = jnp.concatenate(
            [
                lax.ppermute(tail, axis, [(i, (i + 1) % count) for i in range(count)]),
                cells,
                lax.ppermute(head, axis, [((i + 1) % count, i) for i in range(count)]),
            ],
            axis=dim,
        )
    return cells


def shards(psi, rot, occ, v_loc):
    points = psi.shape[0]
    local_m = psi.shape[1]
    point_share = lax.all_to_all(psi, "orb", split_axis=0, concat_axis=1, tiled=True)
    full_matrix = lax.all_gather(rot, "orb", axis=1, tiled=True)
    turned = jnp.dot(
        point_share,
        full_matrix,
        precision=lax.Precision.HIGHEST,
        preferred_element_type=jnp.float32,
    )
    rotated = lax.all_to_all(turned, "orb", split_axis=1, concat_axis=0, tiled=True)
    factor = (3.0 / jnp.pi) ** (1.0 / 3.0)
    part_density = jnp.sum(occ[None, :] * rotated * rotated, axis=1) / M
    density = lax.psum(part_density, "orb")
    potential = v_loc - factor * jnp.cbrt(density)
    field = rotated.reshape(PLANES_DEV, NY, NZ, local_m)
    padded = with_halo(field, (("dom", 0),), 1)
    beside = padded[2:] + padded[:-2]
    beside = beside + jnp.roll(field, 1, 1) + jnp.roll(field, -1, 1)
    beside = beside + jnp.roll(field, 1, 2) + jnp.roll(field, -1, 2)
    lap = (beside - 6.0 * field).reshape(points, local_m)
    hpsi = -0.5 * lap + potential[:, None] * rotated
    total_points = points * lax.axis_size("dom")
    band = lax.psum(jnp.sum(rotated * hpsi, axis=0) / total_points, "dom")
    return (rotated, density, hpsi, band)


def solution(mesh):
    placed = (P("dom", "orb"), P(None, "orb"), P("orb"), P("dom"))
    return jax.shard_map(
        shards,
        mesh=mesh,
        in_specs=placed,
        out_specs=(P("dom", "orb"), P("dom"), P("dom", "orb"), P("orb")),
        check_vma=False,
    )
```

profile of v0, /device:TPU:0, one launch (start us, length us, event | category | flops | bytes accessed | tf_op | source)
XLA Modules:
  0.0 501.9 jit_solution(10848311016970387077)
XLA Ops:
  7.2 0.0 all-gather.2.cloned.1.call-start
  7.2 0.7 all-gather.2.cloned.1.call-update
  7.9 142.6 %all_to_all.35 = f32[8,384,256]{2,1,0:T(8,128)S(1)} all-to-all(f32[8,384,256]{2,1,0:T(8,128)} %bitcast.35), channel_id=1, replica_groups=mesh['dom'=4,'orb'=8] {'orb'}, dimensions={0} | all-to-all | bytes 6291456 | tf_op jit(solution)/shard_map/all_to_all | solution.py:31
  150.5 3.5 copy.10
  154.0 2.8 reshape.40
  156.9 141.8 %all-gather.2.cloned.1.call-done = f32[2048,2048]{1,0:T(8,128)} async-done(((f32[2048,256]{1,0:T(8,128)}), f32[2048,2048]{1,0:T(8,128)}) %all-gather.2.cloned.1.call-update) | async-done | bytes 16777232 | tf_op jit(solution)/shard_map/all_gather | solution.py:32
  298.6 17.6 %copy.11 = f32[2048,2048]{1,0:T(8,128)} copy(f32[2048,2048]{0,1:T(8,128)} %bitcast.33) | data formatting | bytes 33554432 | tf_op jit(solution)/shard_map/dot_general | solution.py:33
  316.2 23.4 %fusion.15 = f32[384,8,256]{2,0,1:T(8,128)S(1)} fusion(f32[384,2048,1]{1,0,2:T(8,128)S(1)} %reshape.40, f32[8,256,2048]{2,1,0:T(8,128)} %bitcast.31), kind=kOutput, calls=%fused_computation.24 | convolution fusion | flops 19327352832 | bytes 23068672 | tf_op jit(solution)/shard_map/dot_general | solution.py:33
  339.6 73.4 %all_to_all.36 = f32[384,8,256]{2,0,1:T(8,128)S(1)} all-to-all(f32[384,8,256]{2,0,1:T(8,128)S(1)} %fusion.15), channel_id=1, replica_groups=mesh['dom'=4,'orb'=8] {'orb'}, dimensions={1} | all-to-all | bytes 6291456 | tf_op jit(solution)/shard_map/all_to_all | solution.py:39
  413.1 0.8 fusion.13
  413.9 1.5 fusion.14
  415.4 0.0 copy-done.3
  415.4 0.5 fusion
  415.9 0.6 div.16
  416.5 35.2 %psum.14 = f32[3072]{0:T(1024)} all-reduce(f32[3072]{0:T(1024)} %div.16), channel_id=1, replica_groups=mesh['dom'=4,'orb'=8] {'orb'}, use_global_device_ids=true, to_apply=%region_1.0 | all-reduce | flops 3072 | bytes 24576 | tf_op jit(solution)/shard_map/psum | solution.py:42
  451.7 0.7 multiply_subtract_fusion
  452.5 0.6 mul.70
  453.1 0.0 collective-permute-start
  453.1 0.5 collective-permute-start.1
  453.6 0.6 fusion.12
  454.2 0.0 copy-start.1
  454.2 0.7 fusion.10
  454.9 21.1 %collective-permute-done = f32[1,8,128,256]{3,2,1,0:T(8,128)S(1)} collective-permute-done((f32[1,8,128,256]{3,2,1,0:T(8,128)}, f32[1,8,128,256]{3,2,1,0:T(8,128)S(1)}, u32[]{:S(2)}, u32[]{:S(2)}) %collective-permute-start) | collective-permute-done | bytes 1048608 | tf_op jit(solution)/shard_map/ppermute | solution.py:21
  476.0 2.7 collective-permute-done.1
  478.7 0.0 copy-done.1
  478.7 2.5 fusion.7
  481.2 0.0 copy-start
  481.2 0.6 fusion.9
  481.8 1.1 copy-done
  482.9 6.5 %psum.15 = f32[256]{0:T(256)} all-reduce(f32[256]{0:T(256)S(1)} %broadcast_multiply_fusion.1), channel_id=1, replica_groups=mesh['dom'=4,'orb'=8] {'dom'}, use_global_device_ids=true, to_apply=%region_3.4 | all-reduce | flops 256 | bytes 2048 | tf_op jit(solution)/shard_map/psum | solution.py:52
  489.4 4.0 bitcast_add_fusion
  493.4 1.7 copy.13
  (6 shorter events, 0.0 us)
Async XLA Ops:
  7.2 291.4 %all-gather.2.cloned.1.call-start = ((), (), s32[]{:S(2)}) async-start(), calls=%async_computation.2 | async-start | bytes 18874368 | tf_op jit(solution)/shard_map/all_gather | solution.py:32
  413.1 2.4 copy-start.3
  453.1 23.0 %collective-permute-start = (f32[1,8,128,256]{3,2,1,0:T(8,128)}, f32[1,8,128,256]{3,2,1,0:T(8,128)S(1)}, u32[]{:S(2)}, u32[]{:S(2)}) collective-permute-start(f32[1,8,128,256]{3,2,1,0:T(8,128)} %get-tuple-element.12), channel_id=1, source_target_pairs={{8,0},{16,8},{24,16},{0,24},{9,1},{17,9},{25,17},{1,25},{10,2},{18... | collective-permute-start | bytes 3145736 | tf_op jit(solution)/shard_map/ppermute | solution.py:21
  453.1 25.6 %collective-permute-start.1 = (f32[1,8,128,256]{3,2,1,0:T(8,128)}, f32[1,8,128,256]{3,2,1,0:T(8,128)S(1)}, u32[]{:S(2)}, u32[]{:S(2)}) collective-permute-start(f32[1,8,128,256]{3,2,1,0:T(8,128)} %get-tuple-element.13), channel_id=1, source_target_pairs={{0,8},{8,16},{16,24},{24,0},{1,9},{9,17},{17,25},{25,1},{2,10},{10... | collective-permute-start | bytes 3145736 | tf_op jit(solution)/shard_map/ppermute | solution.py:19
  454.2 24.5 %copy-start.1 = (f32[3,1,128,256]{3,2,1,0:T(8,128)S(1)}, f32[3,1,128,256]{3,2,1,0:T(8,128)}, u32[]{:S(2)}) copy-start(f32[3,1,128,256]{3,2,1,0:T(8,128)} %get-tuple-element.11) | copy-start | bytes 1179652
  478.7 2.5 copy-start.2
  481.2 1.7 copy-start
Sparse Core Ops, SparseCore 0:
  10.0 288.5 all-gather.1
where the time goes:
time: 503 us; the launch traced here: 502 us
  blocking collectives  258 us (51%)
  waiting for transfers between devices  166 us (33%)
  local copies, waits for them, and re-layouts  31.6 us (6%)
  matrix products  23.4 us (5%)
  between operations  14.1 us (3%)
  other arithmetic  8.32 us (2%)
    all_to_all x1, blocking collectives, shards(): lax.all_to_all(psi, 'orb', split_axis=0, concat_axis=1, tiled=True)  143 us
    all_gather x1, waiting for transfers between devices, shards(): full_matrix = lax.all_gather(rot, 'orb', axis=1, tiled=True)  142 us
    all_to_all x1, blocking collectives, shards(): lax.all_to_all(turned, 'orb', split_axis=1, concat_axis=0, tiled=True)  73.4 us
    psum x1, blocking collectives, shards(): density = lax.psum(part_density, 'orb')  35.2 us
    dot_general x1, matrix products, shards(): jnp.dot(point_share, full_matrix, precision=lax.Precision.HIGHEST, prefer...  23.4 us
    ppermute x1, waiting for transfers between devices, with_halo(): lax.ppermute(head, axis, [((i + 1) % count, i) for i in range(count)])  21.1 us
    dot_general x1, local copies, waits for them, and re-layouts, shards(): jnp.dot(point_share, full_matrix, precision=lax.Precision.HIGHEST, prefer...  17.6 us
  transfers between devices with their start and end apart: 3, of which 3 were waited for; matrix products, arithmetic and copies ran while one was open for 2% of the time, Pallas kernels for 0%

commit v1 on v0

v1 whole, which is shorter than its diff:
```python
import jax
import jax.numpy as jnp
from jax import lax
from jax.experimental import pallas as pl
from jax.experimental.pallas import tpu as pltpu
from jax.sharding import PartitionSpec as P

NY = 8
NZ = 128
EXTRA = 8


def send(block, axis, size, step):
    return lax.ppermute(block, axis, [(a, step(a)) for a in range(size)])


def halves(x):
    high = x.astype(jnp.bfloat16)
    return high, (x - high.astype(jnp.float32)).astype(jnp.bfloat16)


def split_rot(pieces, places):
    group, rows, cols = pieces[0].shape
    rows -= EXTRA
    depth = rows * len(pieces)

    def body(place, *refs):
        ins, (high, low) = refs[: len(pieces)], refs[len(pieces) :]
        for k, piece in enumerate(ins):
            at = pl.ds(pl.multiple_of(place[k] * rows, rows), rows)
            high[0, at, :], low[0, at, :] = halves(piece[0, :rows, :])

    block = pl.BlockSpec((1, rows + EXTRA, cols), lambda s, _: (s, 0, 0))
    out = pl.BlockSpec((1, depth, cols), lambda s, _: (s, 0, 0))
    shape = jax.ShapeDtypeStruct((group, depth, cols), jnp.bfloat16)
    return pl.pallas_call(
        body,
        grid_spec=pltpu.PrefetchScalarGridSpec(
            num_scalar_prefetch=1,
            grid=(group,),
            in_specs=[block] * len(pieces),
            out_specs=[out, out],
        ),
        out_shape=[shape, shape],
        compiler_params=pltpu.CompilerParams(vmem_limit_bytes=32 << 20),
        name="split_rot",
    )(places, *pieces)


def turn(blocks, sources, high, low, occ_piece, scale):
    group, depth, cols = high.shape
    rows = blocks[0].shape[0]
    count = len(blocks)
    lines = rows // NZ
    occ_row = occ_piece.shape[1] // EXTRA - 1

    def body(source, *refs):
        ins = refs[:count]
        high_ref, low_ref, occ_ref = refs[count : count + 3]
        outs = refs[count + 3 : count + 3 + group]
        x_high, x_low, dens = refs[count + 3 + group :]
        step = pl.program_id(0)

        @pl.when(step == 0)
        def _():
            for k, block in enumerate(ins):
                at = pl.ds(pl.multiple_of(source[k] * cols, cols), cols)
                x_high[:, at], x_low[:, at] = halves(block[...])

        def dot(a, b):
            return jnp.dot(a, b, preferred_element_type=jnp.float32)

        value = dot(x_low[...], high_ref[0])
        value += dot(x_high[...], low_ref[0])
        value += dot(x_high[...], high_ref[0])
        part = value * value * occ_ref[0, :1, :]
        folded = part[:, :NZ]
        for k in range(1, cols // NZ):
            folded += part[:, k * NZ : (k + 1) * NZ]

        @pl.when(step == 0)
        def _():
            dens[...] = folded

        @pl.when(step > 0)
        def _():
            dens[...] += folded

        for k, out in enumerate(outs):

            @pl.when(step == k)
            def _():
                out[:rows, :] = value

        @pl.when(step == group - 1)
        def _():
            for line in range(lines):
                sums = jnp.sum(dens[line * NZ : (line + 1) * NZ, :].T, axis=0, keepdims=True) * scale
                for out in outs:
                    out[rows + line : rows + line + 1, :NZ] = sums

    whole = pl.BlockSpec((rows, cols), lambda s, _: (0, 0))
    weight = pl.BlockSpec((1, depth, cols), lambda s, _: (s, 0, 0))
    out = pl.BlockSpec((rows + EXTRA, cols), lambda s, _: (0, 0))
    return pl.pallas_call(
        body,
        grid_spec=pltpu.PrefetchScalarGridSpec(
            num_scalar_prefetch=1,
            grid=(group,),
            in_specs=[whole] * count + [weight, weight, pl.BlockSpec((1, EXTRA, cols), lambda s, _: (s, occ_row, 0))],
            out_specs=[out] * group,
            scratch_shapes=[
                pltpu.VMEM((rows, depth), jnp.bfloat16),
                pltpu.VMEM((rows, depth), jnp.bfloat16),
                pltpu.VMEM((rows, NZ), jnp.float32),
            ],
        ),
        out_shape=[jax.ShapeDtypeStruct((rows + EXTRA, cols), jnp.float32)] * group,
        compiler_params=pltpu.CompilerParams(vmem_limit_bytes=32 << 20),
        cost_estimate=pl.CostEstimate(flops=6 * rows * depth * cols * group, bytes_accessed=4 * depth * cols * group + 8 * rows * depth, transcendentals=0),
        name="turn",
    )(sources, *blocks, high, low, occ_piece)


def finish(planes, before, after, others, v_loc, turned, group):
    cols = before.shape[-1]
    lines = NY // group
    flat = [array for plane in planes for array in plane[0]]
    kinds = [plane[1] for plane in planes]
    count = len(planes)
    points = count * NY * NZ
    factor = (3.0 / jnp.pi) ** (1.0 / 3.0)
    width = NZ

    def body(turned_ref, *refs):
        refs = list(refs)
        pieces = []
        for plane in planes:
            pieces.append([refs.pop(0) for _ in plane[0]])
        before_ref, after_ref = refs.pop(0), refs.pop(0)
        other = [[refs.pop(0) for _ in plane] for plane in others]
        v_ref, rotated, density, hpsi, band = refs
        shift = turned_ref[0]

        def tile(p, y):
            y = y % NY
            r, h = y // lines, y % lines
            if p < 0 or p == count:
                ref = before_ref if p < 0 else after_ref
                return ref[r, h * NZ : (h + 1) * NZ, :]
            if kinds[p] == "whole":
                return pieces[p][0][r, h * NZ : (h + 1) * NZ, :]
            return pieces[p][h][r, :NZ, :]

        def density_line(p, y):
            r, h = y // lines, y % lines
            if kinds[p] == "whole":
                row = other[p][0][0, r, h : h + 1, :]
                return row + other[p][0][1, r, h : h + 1, :]
            return other[p][h][0, r, :1, :] + other[p][h][1, r, :1, :]

        total = jnp.zeros((8, width), jnp.float32)
        for p in range(count):
            dens = jnp.concatenate([density_line(p, y) for y in range(NY)], axis=0)
            dens = pltpu.roll(dens, shift, 0)
            density[p * NY : (p + 1) * NY, :] = dens
            pot = v_ref[p * NY : (p + 1) * NY, :] - factor * jnp.exp(jnp.log(dens) * (1.0 / 3.0))
            pot = pltpu.roll(pot, lax.rem(NY - shift, NY), 0)
            pot = jnp.concatenate([pot, jnp.zeros((NZ - NY, NZ), jnp.float32)], axis=0).T
            for y in range(NY):
                here = tile(p, y)
                beside = tile(p - 1, y) + tile(p + 1, y) + tile(p, y - 1) + tile(p, y + 1)
                beside += pltpu.roll(here, 1, 0) + pltpu.roll(here, NZ - 1, 0)
                value = (pot[:, y : y + 1] + 3.0) * here - 0.5 * beside
                line = lax.rem(y + shift, NY)
                at = pl.ds(pl.multiple_of(p * NY * NZ + line * NZ, NZ), NZ)
                rotated[at, :] = here
                hpsi[at, :] = value
                total += jnp.sum((here * value).reshape(NZ // 8, 8, width), axis=0)
        band[...] = jnp.sum(total, axis=0, keepdims=True)

    def column(array):
        shape = array.shape
        return pl.BlockSpec(shape[:-1] + (width,), lambda c, _: (0,) * (len(shape) - 1) + (c,))

    def fixed(array):
        shape = array.shape
        return pl.BlockSpec(shape, lambda c, _: (0,) * len(shape))

    small = [array for plane in others for array in plane]
    v_lines = v_loc.reshape(count * NY, NZ)
    out_column = pl.BlockSpec((points, width), lambda c, _: (0, c))
    return pl.pallas_call(
        body,
        grid_spec=pltpu.PrefetchScalarGridSpec(
            num_scalar_prefetch=1,
            grid=(cols // width,),
            in_specs=[column(a) for a in flat] + [column(before), column(after)] + [fixed(a) for a in small] + [fixed(v_lines)],
            out_specs=[
                out_column,
                pl.BlockSpec((count * NY, NZ), lambda c, _: (0, 0)),
                out_column,
                pl.BlockSpec((1, width), lambda c, _: (0, c)),
            ],
        ),
        out_shape=[
            jax.ShapeDtypeStruct((points, cols), jnp.float32),
            jax.ShapeDtypeStruct((count * NY, NZ), jnp.float32),
            jax.ShapeDtypeStruct((points, cols), jnp.float32),
            jax.ShapeDtypeStruct((1, cols), jnp.float32),
        ],
        compiler_params=pltpu.CompilerParams(vmem_limit_bytes=40 << 20),
        name="finish",
    )(turned, *flat, before, after, *small, v_lines)


def shards(psi, rot, occ, v_loc):
    points, cols = psi.shape
    depth = rot.shape[0]
    n = lax.axis_size("orb")
    doms = lax.axis_size("dom")
    group = n // 2
    me = lax.axis_index("orb")
    dom = lax.axis_index("dom")
    pos = lax.rem(me, group)
    lines = NY // group
    plane_points = NY * NZ
    planes = points // plane_points

    rows = depth // 4
    quarter = 2 * (dom // (doms // 2)) + lax.rem(dom, 2)
    own = lax.dynamic_slice_in_dim(rot, quarter * rows, rows)
    own = jnp.concatenate([own, jnp.broadcast_to(occ[None, :], (EXTRA, cols))], axis=0)
    parts = [own]
    for s in range(1, group):
        parts.append(send(own, "orb", n, lambda a, s=s: a // group * group + (a + s) % group))
    first = jnp.stack(parts)
    second = send(first, "dom", doms, lambda a: (a + doms // 2) % doms)
    third = send(first, "dom", doms, lambda a: a ^ 1)
    fourth = send(second, "dom", doms, lambda a: a ^ 1)
    places = jnp.stack([quarter, quarter ^ 2, quarter ^ 1, quarter ^ 3]).astype(jnp.int32)
    high, low = split_rot([first, second, third, fourth], places)

    order = [0, planes - 1]
    chunks = [(p, 0, lines) for p in order]
    for p in range(1, planes - 1):
        chunks += [(p, h, 1) for h in range(lines)]
    sources = jnp.stack([lax.rem(me - s + n, n) for s in range(n)]).astype(jnp.int32)

    gathered = []
    for p, h, count in chunks:
        blocks = []
        for s in range(n):
            share = lax.rem(me + s, group)
            start = p * plane_points + (share * lines + h) * NZ
            block = lax.dynamic_slice_in_dim(psi, start, count * NZ)
            if s:
                block = send(block, "orb", n, lambda a, s=s: (a + s) % n)
            blocks.append(block)
        gathered.append(blocks)

    plane_pieces = [[] for _ in range(planes)]
    plane_others = [[] for _ in range(planes)]
    edges = {}
    for (p, h, count), blocks in zip(chunks, gathered):
        outs = turn(blocks, sources, high, low, first, 1.0 / depth)
        back = [outs[0]]
        for r in range(1, group):
            back.append(send(outs[r], "orb", n, lambda a, r=r: a // group * group + (a - r) % group))
        stack = jnp.stack(back)
        dens = stack[:, count * NZ :, :NZ]
        far = send(dens, "orb", n, lambda a: (a + group) % n)
        plane_pieces[p].append(stack)
        plane_others[p].append(jnp.stack([dens, far]))
        if p == planes - 1:
            edges["before"] = send(stack, "dom", doms, lambda a: (a + 1) % doms)
        if p == 0:
            edges["after"] = send(stack, "dom", doms, lambda a: (a - 1) % doms)

    kinds = ["whole" if p in (0, planes - 1) else "lines" for p in range(planes)]
    turned = (pos * lines).astype(jnp.int32).reshape(1)
    rotated, density, hpsi, band = finish(
        list(zip(plane_pieces, kinds)), edges["before"], edges["after"], plane_others, v_loc, turned, group
    )
    band = lax.psum(band.reshape(cols), "dom") / (points * doms)
    return rotated, density.reshape(points), hpsi, band


def solution(mesh):
    placed = (P("dom", "orb"), P(None, "orb"), P("orb"), P("dom"))
    return jax.shard_map(
        shards,
        mesh=mesh,
        in_specs=placed,
        out_specs=(P("dom", "orb"), P("dom"), P("dom", "orb"), P("orb")),
        check_vma=False,
    )
```

time: 503 us -> 314 us (0.62)
  blocking collectives: 258 us -> 7.53 us
  starting transfers between devices: 0.55 us -> 114 us
  Pallas kernels: 0 us -> 30.8 us
  waiting for transfers between devices: 166 us -> 140 us
  matrix products: 23.4 us -> 0 us
  local copies, waits for them, and re-layouts: 31.6 us -> 16.6 us
  between operations: 14.1 us -> 1.06 us
  other arithmetic: 8.32 us -> 2.41 us
    all_to_all x2 -> x0, blocking collectives: 216 us -> none  [the longest x1 143 us: shards(): lax.all_to_all(psi, 'orb', split_axis=0, concat_axis=1, tiled=True)]
    all_gather x1 -> x0, waiting for transfers between devices: 142 us -> none  [shards(): full_matrix = lax.all_gather(rot, 'orb', axis=1, tiled=True)]
    ppermute x2 -> x52, waiting for transfers between devices: 23.8 us -> 140 us  [send(): return lax.ppermute(block, axis, [(a, step(a)) for a in range(size)])]
    ppermute x2 -> x52, starting transfers between devices: 0.51 us -> 114 us  [send(): return lax.ppermute(block, axis, [(a, step(a)) for a in range(size)])]
    psum x2 -> x1, blocking collectives: 41.7 us -> 7.53 us  [shards(): band = lax.psum(band.reshape(cols), 'dom') / (points * doms)]
    pallas_call x0 -> x6, Pallas kernels: none -> 30.8 us  [the longest x4 21.3 us: turn(): pl.pallas_call(body, grid_spec=pltpu.PrefetchScalarGridSpec(num_scalar_pr...]
    dot_general x1 -> x0, matrix products: 23.4 us -> none  [shards(): jnp.dot(point_share, full_matrix, precision=lax.Precision.HIGHEST, prefer...]
    dot_general x1 -> x0, local copies, waits for them, and re-layouts: 17.6 us -> none  [shards(): jnp.dot(point_share, full_matrix, precision=lax.Precision.HIGHEST, prefer...]
  transfers between devices with their start and end apart: 3 -> 52, of which waited for: 3 -> 21; matrix products, arithmetic and copies ran while one was open for 2% -> 2% of each run, Pallas kernels for 0% -> 9%
where the time goes in v1:
time: 314 us; the launch traced here: 312 us
  waiting for transfers between devices  140 us (45%)
  starting transfers between devices  114 us (36%)
  Pallas kernels  30.8 us (10%)
  local copies, waits for them, and re-layouts  16.6 us (5%)
  blocking collectives  7.53 us (2%)
    ppermute x52, waiting for transfers between devices, send(): return lax.ppermute(block, axis, [(a, step(a)) for a in range(size)])  140 us
    ppermute x52, starting transfers between devices, send(): return lax.ppermute(block, axis, [(a, step(a)) for a in range(size)])  114 us
    pallas_call x4, Pallas kernels, turn(): pl.pallas_call(body, grid_spec=pltpu.PrefetchScalarGridSpec(num_scalar_pr...  21.3 us
    unnamed x70, local copies, waits for them, and re-layouts  9.45 us
    psum x1, blocking collectives, shards(): band = lax.psum(band.reshape(cols), 'dom') / (points * doms)  7.53 us
    dynamic_slice x2, local copies, waits for them, and re-layouts, shards(): block = lax.dynamic_slice_in_dim(psi, start, count * NZ)  6.34 us
  transfers between devices with their start and end apart: 52, of which 21 were waited for; matrix products, arithmetic and copies ran while one was open for 2% of the time, Pallas kernels for 9%

profile of v1, /device:TPU:0, one launch (start us, length us, event | category | flops | bytes accessed | tf_op | source)
XLA Modules:
  0.0 312.0 jit_solution(15304068384949224930)
XLA Ops:
  3.0 3.0 collective-permute-start.7
  9.0 11.0 %collective-permute-done.7 = f32[520,256]{1,0:T(8,128)S(1)} collective-permute-done((f32[520,256]{1,0:T(8,128)S(1)}, f32[520,256]{1,0:T(8,128)S(1)}, u32[]{:S(2)}, u32[]{:S(2)}) %collective-permute-start.7) | collective-permute-done | bytes 532512 | tf_op jit(solution)/shard_map/ppermute | solution.py:14
  21.0 9.5 %collective-permute-done.9 = f32[520,256]{1,0:T(8,128)S(1)} collective-permute-done((f32[520,256]{1,0:T(8,128)S(1)}, f32[520,256]{1,0:T(8,128)S(1)}, u32[]{:S(2)}, u32[]{:S(2)}) %collective-permute-start.9) | collective-permute-done | bytes 532512 | tf_op jit(solution)/shard_map/ppermute | solution.py:14
  33.7 46.9 %collective-permute-done.10.refs_1_ = f32[4,520,256]{2,1,0:T(8,128)} collective-permute-done((f32[4,520,256]{2,1,0:T(8,128)}, f32[4,520,256]{2,1,0:T(8,128)}, u32[]{:S(2)}, u32[]{:S(2)}) %collective-permute-start.10) | collective-permute-done | bytes 2129952 | tf_op jit(solution)/shard_map/ppermute | solution.py:14
  85.2 3.6 %collective-permute-start.28 = (f32[128,256]{1,0:T(8,128)S(1)}, f32[128,256]{1,0:T(8,128)S(1)}, u32[]{:S(2)}, u32[]{:S(2)}) collective-permute-start(f32[128,256]{1,0:T(8,128)S(1)} %get-tuple-element.68), channel_id=1, source_target_pairs={{0,3},{1,4},{2,5},{3,6},{4,7},{5,0},{6,1},{7,2},{8,11},{9,12},{10,... | collective-permute-start | bytes 393224 | tf_op jit(solution)/shard_map/ppermute | solution.py:14
  88.8 3.3 %collective-permute-done.26.refs_1_ = f32[128,256]{1,0:T(8,128)S(1)} collective-permute-done((f32[128,256]{1,0:T(8,128)S(1)}, f32[128,256]{1,0:T(8,128)S(1)}, u32[]{:S(2)}, u32[]{:S(2)}) %collective-permute-start.26) | collective-permute-done | bytes 131104 | tf_op jit(solution)/shard_map/ppermute | solution.py:14
  93.7 14.0 %collective-permute-start.30 = (f32[128,256]{1,0:T(8,128)S(1)}, f32[128,256]{1,0:T(8,128)S(1)}, u32[]{:S(2)}, u32[]{:S(2)}) collective-permute-start(f32[128,256]{1,0:T(8,128)S(1)} %get-tuple-element.66), channel_id=1, source_target_pairs={{0,5},{1,6},{2,7},{3,0},{4,1},{5,2},{6,3},{7,4},{8,13},{9,14},{10,... | collective-permute-start | bytes 393224 | tf_op jit(solution)/shard_map/ppermute | solution.py:14
  108.4 3.0 collective-permute-start.31
  118.4 5.3 %collective-permute-done.16.refs_1_ = f32[128,256]{1,0:T(8,128)S(1)} collective-permute-done((f32[128,256]{1,0:T(8,128)S(1)}, f32[128,256]{1,0:T(8,128)S(1)}, u32[]{:S(2)}, u32[]{:S(2)}) %collective-permute-start.16) | collective-permute-done | bytes 131104 | tf_op jit(solution)/shard_map/ppermute | solution.py:14
  125.5 3.9 %constant_dynamic-slice_fusion = (f32[256,256]{1,0:T(8,128)}, f32[256,256]{1,0:T(8,128)}, f32[256,256]{1,0:T(8,128)}, f32[256,256]{1,0:T(8,128)}, f32[256,256]{1...) fusion(f32[3072,256]{1,0:T(8,128)} %param.4, ...), kind=kLoop, calls=%fused_computation.10 | loop fusion | bytes 8388672 | tf_op jit(solution)/shard_map/dynamic_slice | solution.py:256
  129.3 4.1 %collective-permute-done.18.refs_3_ = f32[128,256]{1,0:T(8,128)S(1)} collective-permute-done((f32[128,256]{1,0:T(8,128)S(1)}, f32[128,256]{1,0:T(8,128)S(1)}, u32[]{:S(2)}, u32[]{:S(2)}) %collective-permute-start.18) | collective-permute-done | bytes 131104 | tf_op jit(solution)/shard_map/ppermute | solution.py:14
  139.2 16.9 %collective-permute-done.21.refs_6_ = f32[128,256]{1,0:T(8,128)S(1)} collective-permute-done((f32[128,256]{1,0:T(8,128)S(1)}, f32[128,256]{1,0:T(8,128)S(1)}, u32[]{:S(2)}, u32[]{:S(2)}) %collective-permute-start.21) | collective-permute-done | bytes 131104 | tf_op jit(solution)/shard_map/ppermute | solution.py:14
  157.5 3.8 %collective-permute-start.40 = (f32[256,256]{1,0:T(8,128)}, f32[256,256]{1,0:T(8,128)}, u32[]{:S(2)}, u32[]{:S(2)}) collective-permute-start(f32[256,256]{1,0:T(8,128)} %get-tuple-element.49), channel_id=1, source_target_pairs={{0,5},{1,6},{2,7},{3,0},{4,1},{5,2},{6,3},{7,4},{8,13},{9,14},{10,... | collective-permute-start | bytes 786440 | tf_op jit(solution)/shard_map/ppermute | solution.py:14
  161.3 3.4 %collective-permute-start.41 = (f32[256,256]{1,0:T(8,128)}, f32[256,256]{1,0:T(8,128)}, u32[]{:S(2)}, u32[]{:S(2)}) collective-permute-start(f32[256,256]{1,0:T(8,128)} %get-tuple-element.63), channel_id=1, source_target_pairs={{0,6},{1,7},{2,0},{3,1},{4,2},{5,3},{6,4},{7,5},{8,14},{9,15},{10,... | collective-permute-start | bytes 786440 | tf_op jit(solution)/shard_map/ppermute | solution.py:14
  164.9 5.2 %split_rot.1 = (bf16[4,2048,256]{2,1,0:T(8,128)(2,1)S(1)}, bf16[4,2048,256]{2,1,0:T(8,128)(2,1)S(1)}) custom-call(s32[4]{0:T(128)S(1)} %pad_add_fusion.place, f32[4,520,256]{2,1,0:T(8,128)} %pad_maximum_fusion.refs_0_.refs_10_, f32[4,520,256]{2,1,0:T(8,128)} %collective-permute-done.10.refs_1_, f32[4,520,256]{2,1,0:T(8,128)} %collective-permute-done.11.refs_2_, ...), custom_call_target="tpu_custom_call" | custom-call | tf_op jit(solution)/shard_map/split_rot/pallas_call | solution.py:36
  170.1 8.8 %collective-permute-done.38.refs_3_ = f32[256,256]{1,0:T(8,128)} collective-permute-done((f32[256,256]{1,0:T(8,128)}, f32[256,256]{1,0:T(8,128)}, u32[]{:S(2)}, u32[]{:S(2)}) %collective-permute-start.38) | collective-permute-done | bytes 262176 | tf_op jit(solution)/shard_map/ppermute | solution.py:14
  181.4 3.6 %collective-permute-start = (f32[256,256]{1,0:T(8,128)S(1)}, f32[256,256]{1,0:T(8,128)S(1)}, u32[]{:S(2)}, u32[]{:S(2)}) collective-permute-start(f32[256,256]{1,0:T(8,128)S(1)} %copy-done.32), channel_id=1, source_target_pairs={{0,1},{1,2},{2,3},{3,4},{4,5},{5,6},{6,7},{7,0},{8,9},{9,10},{10,1... | collective-permute-start | bytes 786440 | tf_op jit(solution)/shard_map/ppermute | solution.py:14
  185.1 16.4 %collective-permute-start.1 = (f32[256,256]{1,0:T(8,128)S(1)}, f32[256,256]{1,0:T(8,128)S(1)}, u32[]{:S(2)}, u32[]{:S(2)}) collective-permute-start(f32[256,256]{1,0:T(8,128)S(1)} %copy-done.31), channel_id=1, source_target_pairs={{0,2},{1,3},{2,4},{3,5},{4,6},{5,7},{6,0},{7,1},{8,10},{9,11},{10,... | collective-permute-start | bytes 786440 | tf_op jit(solution)/shard_map/ppermute | solution.py:14
  201.5 4.3 %collective-permute-start.3 = (f32[256,256]{1,0:T(8,128)S(1)}, f32[256,256]{1,0:T(8,128)S(1)}, u32[]{:S(2)}, u32[]{:S(2)}) collective-permute-start(f32[256,256]{1,0:T(8,128)S(1)} %copy-done.29), channel_id=1, source_target_pairs={{0,4},{1,5},{2,6},{3,7},{4,0},{5,1},{6,2},{7,3},{8,12},{9,13},{10,... | collective-permute-start | bytes 786440 | tf_op jit(solution)/shard_map/ppermute | solution.py:14
  205.9 6.8 %turn.7 = (f32[264,256]{1,0:T(8,128)S(1)}, f32[264,256]{1,0:T(8,128)S(1)}, f32[264,256]{1,0:T(8,128)S(1)}, f32[264,256]{1,0:T(8,128)S(1)}) custom-call(s32[8]{0:T(128)S(1)} %stack.161.source, f32[256,256]{1,0:T(8,128)S(1)} %get-tuple-element.54.refs_0_, f32[256,256]{1,0:T(8,128)S(1)} %collective-permute-done.36.refs_1_, ...), custom_call_target="tpu_custom_call" | custom-call | flops 3221225472 | bytes 12582912 | tf_op jit(solution)/shard_map/turn/pallas_call | solution.py:105
  212.8 13.1 %collective-permute-start.5 = (f32[256,256]{1,0:T(8,128)S(1)}, f32[256,256]{1,0:T(8,128)S(1)}, u32[]{:S(2)}, u32[]{:S(2)}) collective-permute-start(f32[256,256]{1,0:T(8,128)S(1)} %copy-done.27), channel_id=1, source_target_pairs={{0,6},{1,7},{2,0},{3,1},{4,2},{5,3},{6,4},{7,5},{8,14},{9,15},{10,... | collective-permute-start | bytes 786440 | tf_op jit(solution)/shard_map/ppermute | solution.py:14
  226.1 4.2 %turn.6 = (f32[136,256]{1,0:T(8,128)S(1)}, f32[136,256]{1,0:T(8,128)S(1)}, f32[136,256]{1,0:T(8,128)S(1)}, f32[136,256]{1,0:T(8,128)S(1)}) custom-call(s32[8]{0:T(128)S(1)} %stack.161.source, f32[128,256]{1,0:T(8,128)S(1)} %get-tuple-element.71.refs_0_, f32[128,256]{1,0:T(8,128)S(1)} %collective-permute-done.26.refs_1_, f32[128,256]{1,0:T(8,128)S(1)} %copy-done.2, ...), custom_call_target="tpu_custom_call" | custom-call | flops 1610612736 | bytes 10485760 | tf_op jit(solution)/shard_map/turn/pallas_call | solution.py:105
  230.4 4.2 %collective-permute-start.33 = (f32[136,256]{1,0:T(8,128)S(1)}, f32[136,256]{1,0:T(8,128)S(1)}, u32[]{:S(2)}, u32[]{:S(2)}) collective-permute-start(f32[136,256]{1,0:T(8,128)S(1)} %get-tuple-element.37), channel_id=1, source_target_pairs={{0,3},{1,0},{2,1},{3,2},{4,7},{5,4},{6,5},{7,6},{8,11},{9,8},{10,9... | collective-permute-start | bytes 417800 | tf_op jit(solution)/shard_map/ppermute | solution.py:14
  234.6 7.3 %collective-permute-start.34 = (f32[136,256]{1,0:T(8,128)S(1)}, f32[136,256]{1,0:T(8,128)S(1)}, u32[]{:S(2)}, u32[]{:S(2)}) collective-permute-start(f32[136,256]{1,0:T(8,128)S(1)} %get-tuple-element.38), channel_id=1, source_target_pairs={{0,2},{1,3},{2,0},{3,1},{4,6},{5,7},{6,4},{7,5},{8,10},{9,11},{10,... | collective-permute-start | bytes 417800 | tf_op jit(solution)/shard_map/ppermute | solution.py:14
  242.0 4.2 %turn.5 = (f32[136,256]{1,0:T(8,128)S(1)}, f32[136,256]{1,0:T(8,128)S(1)}, f32[136,256]{1,0:T(8,128)S(1)}, f32[136,256]{1,0:T(8,128)S(1)}) custom-call(s32[8]{0:T(128)S(1)} %stack.161.source, f32[128,256]{1,0:T(8,128)S(1)} %get-tuple-element.79.refs_0_, f32[128,256]{1,0:T(8,128)S(1)} %copy-done.8, f32[128,256]{1,0:T(8,128)S(1)} %copy-done.12, ...), custom_call_target="tpu_custom_call" | custom-call | flops 1610612736 | bytes 10485760 | tf_op jit(solution)/shard_map/turn/pallas_call | solution.py:105
  250.4 6.1 %turn.4 = (f32[264,256]{1,0:T(8,128)S(1)}, f32[264,256]{1,0:T(8,128)S(1)}, f32[264,256]{1,0:T(8,128)S(1)}, f32[264,256]{1,0:T(8,128)S(1)}) custom-call(s32[8]{0:T(128)S(1)} %stack.161.source, f32[256,256]{1,0:T(8,128)S(1)} %get-tuple-element.62.refs_0_, f32[256,256]{1,0:T(8,128)S(1)} %collective-permute-done.refs_1_, ...), custom_call_target="tpu_custom_call" | custom-call | flops 3221225472 | bytes 12582912 | tf_op jit(solution)/shard_map/turn/pallas_call | solution.py:105
  266.1 4.8 %collective-permute-start.50 = (f32[4,8,128]{2,1,0:T(8,128)S(1)}, f32[4,8,128]{2,1,0:T(8,128)S(1)}, u32[]{:S(2)}, u32[]{:S(2)}) collective-permute-start(f32[4,8,128]{2,1,0:T(8,128)S(1)} %get-tuple-element.85), channel_id=1, source_target_pairs={{0,4},{1,5},{2,6},{3,7},{4,0},{5,1},{6,2},{7,3},{8,12},{9,13},{10,... | collective-permute-start | bytes 49160 | tf_op jit(solution)/shard_map/ppermute | solution.py:14
  270.9 3.4 %collective-permute-done.45 = f32[264,256]{1,0:T(8,128)S(1)} collective-permute-done((f32[264,256]{1,0:T(8,128)S(1)}, f32[264,256]{1,0:T(8,128)S(1)}, u32[]{:S(2)}, u32[]{:S(2)}) %collective-permute-start.45) | collective-permute-done | bytes 270368 | tf_op jit(solution)/shard_map/ppermute | solution.py:14
  276.0 7.8 %collective-permute-done.15 = f32[264,256]{1,0:T(8,128)S(1)} collective-permute-done((f32[264,256]{1,0:T(8,128)S(1)}, f32[264,256]{1,0:T(8,128)S(1)}, u32[]{:S(2)}, u32[]{:S(2)}) %collective-permute-start.15) | collective-permute-done | bytes 270368 | tf_op jit(solution)/shard_map/ppermute | solution.py:14
  295.5 4.1 %collective-permute-done.47.refs_5_ = f32[4,264,256]{2,1,0:T(8,128)S(1)} collective-permute-done((f32[4,264,256]{2,1,0:T(8,128)S(1)}, f32[4,264,256]{2,1,0:T(8,128)S(1)}, u32[]{:S(2)}, u32[]{:S(2)}) %collective-permute-start.47) | collective-permute-done | bytes 1081376 | tf_op jit(solution)/shard_map/ppermute | solution.py:14
  299.6 4.3 %finish.1 = (f32[3072,256]{1,0:T(8,128)}, f32[24,128]{1,0:T(8,128)}, f32[3072,256]{1,0:T(8,128)}, f32[1,256]{1,0:T(1,128)S(1)}) custom-call(s32[1]{0:T(128)} %bitcast.turned_ref, f32[4,264,256]{2,1,0:T(8,128)S(1)} %pad_maximum_fusion.1.refs_0_, f32[4,136,256]{2,1,0:T(8,128)S(1)} %pad_maximum_fusion.3.refs_1_, f32[4,136,256]{2,1,0:T(8,128)S(1)} %pad_maximum_fusion.4.refs_2_, ...), custom_call_target="tpu_custom_call" | custom-call | tf_op jit(solution)/shard_map/finish/pallas_call | solution.py:193
  303.9 7.5 %psum.7 = f32[256]{0:T(256)S(1)} all-reduce(f32[256]{0:T(256)S(1)} %bitcast.54), channel_id=1, replica_groups=mesh['dom'=4,'orb'=8] {'dom'}, use_global_device_ids=true, to_apply=%region_0.1 | all-reduce | flops 256 | bytes 2048 | tf_op jit(solution)/shard_map/psum | solution.py:285
  (170 shorter events, 62.9 us)
Async XLA Ops:
  3.0 17.0 %collective-permute-start.7 = (f32[520,256]{1,0:T(8,128)S(1)}, f32[520,256]{1,0:T(8,128)S(1)}, u32[]{:S(2)}, u32[]{:S(2)}) collective-permute-start(f32[520,256]{1,0:T(8,128)S(1)} %get-tuple-element.89), channel_id=1, source_target_pairs={{0,1},{1,2},{2,3},{3,0},{4,5},{5,6},{6,7},{7,4},{8,9},{9,10},{10,1... | collective-permute-start | bytes 1597448 | tf_op jit(solution)/shard_map/ppermute | solution.py:14
  7.6 22.9 %collective-permute-start.9 = (f32[520,256]{1,0:T(8,128)S(1)}, f32[520,256]{1,0:T(8,128)S(1)}, u32[]{:S(2)}, u32[]{:S(2)}) collective-permute-start(f32[520,256]{1,0:T(8,128)S(1)} %get-tuple-element.89), channel_id=1, source_target_pairs={{0,3},{1,0},{2,1},{3,2},{4,7},{5,4},{6,5},{7,6},{8,11},{9,8},{10,9... | collective-permute-start | bytes 1597448 | tf_op jit(solution)/shard_map/ppermute | solution.py:14
  32.0 48.6 %collective-permute-start.10 = (f32[4,520,256]{2,1,0:T(8,128)}, f32[4,520,256]{2,1,0:T(8,128)}, u32[]{:S(2)}, u32[]{:S(2)}) collective-permute-start(f32[4,520,256]{2,1,0:T(8,128)} %pad_maximum_fusion.refs_0_.refs_10_), channel_id=1, source_target_pairs={{0,16},{8,24},{16,0},{24,8},{1,17},{9,25},{17,1},{25,9},{2,18},{10... | collective-permute-start | bytes 6389768 | tf_op jit(solution)/shard_map/ppermute | solution.py:14
  33.7 127.6 %collective-permute-start.11 = (f32[4,520,256]{2,1,0:T(8,128)}, f32[4,520,256]{2,1,0:T(8,128)}, u32[]{:S(2)}, u32[]{:S(2)}) collective-permute-start(f32[4,520,256]{2,1,0:T(8,128)} %pad_maximum_fusion.refs_0_.refs_10_), channel_id=1, source_target_pairs={{0,8},{8,0},{16,24},{24,16},{1,9},{9,1},{17,25},{25,17},{2,10},{10... | collective-permute-start | bytes 6389768 | tf_op jit(solution)/shard_map/ppermute | solution.py:14
  80.6 84.1 %collective-permute-start.12 = (f32[4,520,256]{2,1,0:T(8,128)}, f32[4,520,256]{2,1,0:T(8,128)}, u32[]{:S(2)}, u32[]{:S(2)}) collective-permute-start(f32[4,520,256]{2,1,0:T(8,128)} %collective-permute-done.10.refs_1_), channel_id=1, source_target_pairs={{0,8},{8,0},{16,24},{24,16},{1,9},{9,1},{17,25},{25,17},{2,10},{10... | collective-permute-start | bytes 6389768 | tf_op jit(solution)/shard_map/ppermute | solution.py:14
  85.2 22.5 %collective-permute-start.28 = (f32[128,256]{1,0:T(8,128)S(1)}, f32[128,256]{1,0:T(8,128)S(1)}, u32[]{:S(2)}, u32[]{:S(2)}) collective-permute-start(f32[128,256]{1,0:T(8,128)S(1)} %get-tuple-element.68), channel_id=1, source_target_pairs={{0,3},{1,4},{2,5},{3,6},{4,7},{5,0},{6,1},{7,2},{8,11},{9,12},{10,... | collective-permute-start | bytes 393224 | tf_op jit(solution)/shard_map/ppermute | solution.py:14
  92.2 19.2 %collective-permute-start.29 = (f32[128,256]{1,0:T(8,128)S(1)}, f32[128,256]{1,0:T(8,128)S(1)}, u32[]{:S(2)}, u32[]{:S(2)}) collective-permute-start(f32[128,256]{1,0:T(8,128)S(1)} %get-tuple-element.67), channel_id=1, source_target_pairs={{0,4},{1,5},{2,6},{3,7},{4,0},{5,1},{6,2},{7,3},{8,12},{9,13},{10,... | collective-permute-start | bytes 393224 | tf_op jit(solution)/shard_map/ppermute | solution.py:14
  93.7 20.1 %collective-permute-start.30 = (f32[128,256]{1,0:T(8,128)S(1)}, f32[128,256]{1,0:T(8,128)S(1)}, u32[]{:S(2)}, u32[]{:S(2)}) collective-permute-start(f32[128,256]{1,0:T(8,128)S(1)} %get-tuple-element.66), channel_id=1, source_target_pairs={{0,5},{1,6},{2,7},{3,0},{4,1},{5,2},{6,3},{7,4},{8,13},{9,14},{10,... | collective-permute-start | bytes 393224 | tf_op jit(solution)/shard_map/ppermute | solution.py:14
  134.1 22.7 %collective-permute-start.36 = (f32[256,256]{1,0:T(8,128)S(1)}, f32[256,256]{1,0:T(8,128)S(1)}, u32[]{:S(2)}, u32[]{:S(2)}) collective-permute-start(f32[256,256]{1,0:T(8,128)S(1)} %get-tuple-element.53), channel_id=1, source_target_pairs={{0,1},{1,2},{2,3},{3,4},{4,5},{5,6},{6,7},{7,0},{8,9},{9,10},{10,1... | collective-permute-start | bytes 786440 | tf_op jit(solution)/shard_map/ppermute | solution.py:14
  134.7 22.7 %collective-permute-start.37 = (f32[256,256]{1,0:T(8,128)S(1)}, f32[256,256]{1,0:T(8,128)S(1)}, u32[]{:S(2)}, u32[]{:S(2)}) collective-permute-start(f32[256,256]{1,0:T(8,128)S(1)} %get-tuple-element.52), channel_id=1, source_target_pairs={{0,2},{1,3},{2,4},{3,5},{4,6},{5,7},{6,0},{7,1},{8,10},{9,11},{10,... | collective-permute-start | bytes 786440 | tf_op jit(solution)/shard_map/ppermute | solution.py:14
  137.1 19.0 %collective-permute-start.21 = (f32[128,256]{1,0:T(8,128)S(1)}, f32[128,256]{1,0:T(8,128)S(1)}, u32[]{:S(2)}, u32[]{:S(2)}) collective-permute-start(f32[128,256]{1,0:T(8,128)S(1)} %copy-done.34), channel_id=1, source_target_pairs={{0,6},{1,7},{2,0},{3,1},{4,2},{5,3},{6,4},{7,5},{8,14},{9,15},{10,... | collective-permute-start | bytes 393224 | tf_op jit(solution)/shard_map/ppermute | solution.py:14
  156.7 22.2 %collective-permute-start.38 = (f32[256,256]{1,0:T(8,128)}, f32[256,256]{1,0:T(8,128)}, u32[]{:S(2)}, u32[]{:S(2)}) collective-permute-start(f32[256,256]{1,0:T(8,128)} %get-tuple-element.51), channel_id=1, source_target_pairs={{0,3},{1,4},{2,5},{3,6},{4,7},{5,0},{6,1},{7,2},{8,11},{9,12},{10,... | collective-permute-start | bytes 786440 | tf_op jit(solution)/shard_map/ppermute | solution.py:14
  156.8 24.7 %collective-permute-start.39 = (f32[256,256]{1,0:T(8,128)}, f32[256,256]{1,0:T(8,128)}, u32[]{:S(2)}, u32[]{:S(2)}) collective-permute-start(f32[256,256]{1,0:T(8,128)} %get-tuple-element.50), channel_id=1, source_target_pairs={{0,4},{1,5},{2,6},{3,7},{4,0},{5,1},{6,2},{7,3},{8,12},{9,13},{10,... | collective-permute-start | bytes 786440 | tf_op jit(solution)/shard_map/ppermute | solution.py:14
  157.5 27.6 %collective-permute-start.40 = (f32[256,256]{1,0:T(8,128)}, f32[256,256]{1,0:T(8,128)}, u32[]{:S(2)}, u32[]{:S(2)}) collective-permute-start(f32[256,256]{1,0:T(8,128)} %get-tuple-element.49), channel_id=1, source_target_pairs={{0,5},{1,6},{2,7},{3,0},{4,1},{5,2},{6,3},{7,4},{8,13},{9,14},{10,... | collective-permute-start | bytes 786440 | tf_op jit(solution)/shard_map/ppermute | solution.py:14
  161.3 40.1 %collective-permute-start.41 = (f32[256,256]{1,0:T(8,128)}, f32[256,256]{1,0:T(8,128)}, u32[]{:S(2)}, u32[]{:S(2)}) collective-permute-start(f32[256,256]{1,0:T(8,128)} %get-tuple-element.63), channel_id=1, source_target_pairs={{0,6},{1,7},{2,0},{3,1},{4,2},{5,3},{6,4},{7,5},{8,14},{9,15},{10,... | collective-permute-start | bytes 786440 | tf_op jit(solution)/shard_map/ppermute | solution.py:14
  164.7 36.8 %collective-permute-start.42 = (f32[256,256]{1,0:T(8,128)}, f32[256,256]{1,0:T(8,128)}, u32[]{:S(2)}, u32[]{:S(2)}) collective-permute-start(f32[256,256]{1,0:T(8,128)} %get-tuple-element.48), channel_id=1, source_target_pairs={{0,7},{1,0},{2,1},{3,2},{4,3},{5,4},{6,5},{7,6},{8,15},{9,8},{10,9... | collective-permute-start | bytes 786440 | tf_op jit(solution)/shard_map/ppermute | solution.py:14
  178.9 33.7 %collective-permute-start.22 = (f32[128,256]{1,0:T(8,128)S(1)}, f32[128,256]{1,0:T(8,128)S(1)}, u32[]{:S(2)}, u32[]{:S(2)}) collective-permute-start(f32[128,256]{1,0:T(8,128)S(1)} %copy-done.33), channel_id=1, source_target_pairs={{0,7},{1,0},{2,1},{3,2},{4,3},{5,4},{6,5},{7,6},{8,15},{9,8},{10,9... | collective-permute-start | bytes 393224 | tf_op jit(solution)/shard_map/ppermute | solution.py:14
  181.4 31.3 %collective-permute-start = (f32[256,256]{1,0:T(8,128)S(1)}, f32[256,256]{1,0:T(8,128)S(1)}, u32[]{:S(2)}, u32[]{:S(2)}) collective-permute-start(f32[256,256]{1,0:T(8,128)S(1)} %copy-done.32), channel_id=1, source_target_pairs={{0,1},{1,2},{2,3},{3,4},{4,5},{5,6},{6,7},{7,0},{8,9},{9,10},{10,1... | collective-permute-start | bytes 786440 | tf_op jit(solution)/shard_map/ppermute | solution.py:14
  185.1 40.9 %collective-permute-start.1 = (f32[256,256]{1,0:T(8,128)S(1)}, f32[256,256]{1,0:T(8,128)S(1)}, u32[]{:S(2)}, u32[]{:S(2)}) collective-permute-start(f32[256,256]{1,0:T(8,128)S(1)} %copy-done.31), channel_id=1, source_target_pairs={{0,2},{1,3},{2,4},{3,5},{4,6},{5,7},{6,0},{7,1},{8,10},{9,11},{10,... | collective-permute-start | bytes 786440 | tf_op jit(solution)/shard_map/ppermute | solution.py:14
  201.4 28.9 %collective-permute-start.2 = (f32[256,256]{1,0:T(8,128)S(1)}, f32[256,256]{1,0:T(8,128)S(1)}, u32[]{:S(2)}, u32[]{:S(2)}) collective-permute-start(f32[256,256]{1,0:T(8,128)S(1)} %copy-done.30), channel_id=1, source_target_pairs={{0,3},{1,4},{2,5},{3,6},{4,7},{5,0},{6,1},{7,2},{8,11},{9,12},{10,... | collective-permute-start | bytes 786440 | tf_op jit(solution)/shard_map/ppermute | solution.py:14
  201.5 33.1 %collective-permute-start.3 = (f32[256,256]{1,0:T(8,128)S(1)}, f32[256,256]{1,0:T(8,128)S(1)}, u32[]{:S(2)}, u32[]{:S(2)}) collective-permute-start(f32[256,256]{1,0:T(8,128)S(1)} %copy-done.29), channel_id=1, source_target_pairs={{0,4},{1,5},{2,6},{3,7},{4,0},{5,1},{6,2},{7,3},{8,12},{9,13},{10,... | collective-permute-start | bytes 786440 | tf_op jit(solution)/shard_map/ppermute | solution.py:14
  212.6 33.6 %collective-permute-start.4 = (f32[256,256]{1,0:T(8,128)S(1)}, f32[256,256]{1,0:T(8,128)S(1)}, u32[]{:S(2)}, u32[]{:S(2)}) collective-permute-start(f32[256,256]{1,0:T(8,128)S(1)} %copy-done.28), channel_id=1, source_target_pairs={{0,5},{1,6},{2,7},{3,0},{4,1},{5,2},{6,3},{7,4},{8,13},{9,14},{10,... | collective-permute-start | bytes 786440 | tf_op jit(solution)/shard_map/ppermute | solution.py:14
  212.8 33.5 %collective-permute-start.5 = (f32[256,256]{1,0:T(8,128)S(1)}, f32[256,256]{1,0:T(8,128)S(1)}, u32[]{:S(2)}, u32[]{:S(2)}) collective-permute-start(f32[256,256]{1,0:T(8,128)S(1)} %copy-done.27), channel_id=1, source_target_pairs={{0,6},{1,7},{2,0},{3,1},{4,2},{5,3},{6,4},{7,5},{8,14},{9,15},{10,... | collective-permute-start | bytes 786440 | tf_op jit(solution)/shard_map/ppermute | solution.py:14
  225.9 22.4 %collective-permute-start.6 = (f32[256,256]{1,0:T(8,128)S(1)}, f32[256,256]{1,0:T(8,128)S(1)}, u32[]{:S(2)}, u32[]{:S(2)}) collective-permute-start(f32[256,256]{1,0:T(8,128)S(1)} %copy-done.26), channel_id=1, source_target_pairs={{0,7},{1,0},{2,1},{3,2},{4,3},{5,4},{6,5},{7,6},{8,15},{9,8},{10,9... | collective-permute-start | bytes 786440 | tf_op jit(solution)/shard_map/ppermute | solution.py:14
  230.4 19.3 %collective-permute-start.33 = (f32[136,256]{1,0:T(8,128)S(1)}, f32[136,256]{1,0:T(8,128)S(1)}, u32[]{:S(2)}, u32[]{:S(2)}) collective-permute-start(f32[136,256]{1,0:T(8,128)S(1)} %get-tuple-element.37), channel_id=1, source_target_pairs={{0,3},{1,0},{2,1},{3,2},{4,7},{5,4},{6,5},{7,6},{8,11},{9,8},{10,9... | collective-permute-start | bytes 417800 | tf_op jit(solution)/shard_map/ppermute | solution.py:14
  234.6 15.2 %collective-permute-start.34 = (f32[136,256]{1,0:T(8,128)S(1)}, f32[136,256]{1,0:T(8,128)S(1)}, u32[]{:S(2)}, u32[]{:S(2)}) collective-permute-start(f32[136,256]{1,0:T(8,128)S(1)} %get-tuple-element.38), channel_id=1, source_target_pairs={{0,2},{1,3},{2,0},{3,1},{4,6},{5,7},{6,4},{7,5},{8,10},{9,11},{10,... | collective-permute-start | bytes 417800 | tf_op jit(solution)/shard_map/ppermute | solution.py:14
  246.2 17.4 %collective-permute-start.43 = (f32[264,256]{1,0:T(8,128)S(1)}, f32[264,256]{1,0:T(8,128)S(1)}, u32[]{:S(2)}, u32[]{:S(2)}) collective-permute-start(f32[264,256]{1,0:T(8,128)S(1)} %get-tuple-element.41), channel_id=1, source_target_pairs={{0,3},{1,0},{2,1},{3,2},{4,7},{5,4},{6,5},{7,6},{8,11},{9,8},{10,9... | collective-permute-start | bytes 811016 | tf_op jit(solution)/shard_map/ppermute | solution.py:14
  259.2 15.2 %collective-permute-start.45 = (f32[264,256]{1,0:T(8,128)S(1)}, f32[264,256]{1,0:T(8,128)S(1)}, u32[]{:S(2)}, u32[]{:S(2)}) collective-permute-start(f32[264,256]{1,0:T(8,128)S(1)} %get-tuple-element.43), channel_id=1, source_target_pairs={{0,1},{1,2},{2,3},{3,0},{4,5},{5,6},{6,7},{7,4},{8,9},{9,10},{10,1... | collective-permute-start | bytes 811016 | tf_op jit(solution)/shard_map/ppermute | solution.py:14
  263.7 20.2 %collective-permute-start.15 = (f32[264,256]{1,0:T(8,128)S(1)}, f32[264,256]{1,0:T(8,128)S(1)}, u32[]{:S(2)}, u32[]{:S(2)}) collective-permute-start(f32[264,256]{1,0:T(8,128)S(1)} %get-tuple-element.31), channel_id=1, source_target_pairs={{0,1},{1,2},{2,3},{3,0},{4,5},{5,6},{6,7},{7,4},{8,9},{9,10},{10,1... | collective-permute-start | bytes 811016 | tf_op jit(solution)/shard_map/ppermute | solution.py:14
  266.1 20.1 %collective-permute-start.50 = (f32[4,8,128]{2,1,0:T(8,128)S(1)}, f32[4,8,128]{2,1,0:T(8,128)S(1)}, u32[]{:S(2)}, u32[]{:S(2)}) collective-permute-start(f32[4,8,128]{2,1,0:T(8,128)S(1)} %get-tuple-element.85), channel_id=1, source_target_pairs={{0,4},{1,5},{2,6},{3,7},{4,0},{5,1},{6,2},{7,3},{8,12},{9,13},{10,... | collective-permute-start | bytes 49160 | tf_op jit(solution)/shard_map/ppermute | solution.py:14
  274.4 21.1 %collective-permute-start.46 = (f32[4,264,256]{2,1,0:T(8,128)S(1)}, f32[4,264,256]{2,1,0:T(8,128)S(1)}, u32[]{:S(2)}, u32[]{:S(2)}) collective-permute-start(f32[4,264,256]{2,1,0:T(8,128)S(1)} %pad_maximum_fusion.2.refs_3_), channel_id=1, source_target_pairs={{0,8},{8,16},{16,24},{24,0},{1,9},{9,17},{17,25},{25,1},{2,10},{10... | collective-permute-start | bytes 3244040 | tf_op jit(solution)/shard_map/ppermute | solution.py:14
  283.9 15.8 %collective-permute-start.47 = (f32[4,264,256]{2,1,0:T(8,128)S(1)}, f32[4,264,256]{2,1,0:T(8,128)S(1)}, u32[]{:S(2)}, u32[]{:S(2)}) collective-permute-start(f32[4,264,256]{2,1,0:T(8,128)S(1)} %pad_maximum_fusion.1.refs_0_), channel_id=1, source_target_pairs={{0,24},{8,0},{16,8},{24,16},{1,25},{9,1},{17,9},{25,17},{2,26},{10... | collective-permute-start | bytes 3244040 | tf_op jit(solution)/shard_map/ppermute | solution.py:14
  (55 other events, 616.3 us)

commit v2 on v1

v2 whole, which is shorter than its diff:
```python
import jax
import jax.numpy as jnp
from jax import lax
from jax.experimental import pallas as pl
from jax.experimental.pallas import tpu as pltpu
from jax.sharding import PartitionSpec as P

NY = 8
NZ = 128
EXTRA = 8
VMEM = 20 << 20
MARK = 40


def send(block, axis, size, step):
    return lax.ppermute(block, axis, [(a, step(a)) for a in range(size)])


def halves(x):
    high = x.astype(jnp.bfloat16)
    return high, (x - high.astype(jnp.float32)).astype(jnp.bfloat16)


def after(array, others):
    return lax.optimization_barrier((array, *others))[0] if others else array


def collect(pieces, span):
    rows, cols = pieces[0].shape
    count = len(pieces)

    def body(*refs):
        for k in range(count):

            @pl.when(pl.program_id(0) == k)
            def _():
                refs[-1][0] = refs[k][...]

    return pl.pallas_call(
        body,
        grid=(count,),
        in_specs=[pl.BlockSpec((rows, cols), lambda s: (0, 0))] * count,
        out_specs=pl.BlockSpec((1, rows, cols), lambda s: (s, 0, 0)),
        out_shape=jax.ShapeDtypeStruct((count, rows, cols), pieces[0].dtype),
        cost_estimate=pl.CostEstimate(flops=span * 10**9, bytes_accessed=8 * count * rows * cols, transcendentals=0),
        name="collect",
    )(*pieces)


def split_rot(sets, places):
    half, rows, cols = sets[0][0].shape
    rows -= EXTRA
    parts = len(sets[0])
    depth = rows * parts
    group = half * len(sets)

    def body(place, *refs):
        ins, (high, low, occ) = refs[: parts * len(sets)], refs[parts * len(sets) :]
        for number in range(len(sets)):

            @pl.when(pl.program_id(0) // half == number)
            def _():
                for k in range(parts):
                    piece = ins[number * parts + k]
                    at = pl.ds(pl.multiple_of(place[k] * rows, rows), rows)
                    high[0, at, :], low[0, at, :] = halves(piece[0, :rows, :])
                occ[0] = ins[number * parts][0, rows:, :]

    def block(number):
        return pl.BlockSpec((1, rows + EXTRA, cols), lambda s, _: (jnp.clip(s - number * half, 0, half - 1), 0, 0))

    def out(height):
        return pl.BlockSpec((1, height, cols), lambda s, _: (s, 0, 0))

    return pl.pallas_call(
        body,
        grid_spec=pltpu.PrefetchScalarGridSpec(
            num_scalar_prefetch=1,
            grid=(group,),
            in_specs=[block(number) for number, pieces in enumerate(sets) for _ in pieces],
            out_specs=[out(depth), out(depth), out(EXTRA)],
        ),
        out_shape=[
            jax.ShapeDtypeStruct((group, depth, cols), jnp.bfloat16),
            jax.ShapeDtypeStruct((group, depth, cols), jnp.bfloat16),
            jax.ShapeDtypeStruct((group, EXTRA, cols), jnp.float32),
        ],
        compiler_params=pltpu.CompilerParams(vmem_limit_bytes=VMEM),
        name="split_rot",
    )(places, *[piece for pieces in sets for piece in pieces])


def turn(blocks, high, low, occ, scale):
    count, rows, cols = blocks.shape
    group, depth, _ = high.shape
    lines = rows // NZ

    def body(x_ref, high_ref, low_ref, occ_ref, *refs):
        outs = refs[:group]
        dens_out, x_high, x_low, dens = refs[group:]
        step = pl.program_id(0)

        @pl.when(step == 0)
        def _():
            for k in range(count):
                at = slice(k * cols, (k + 1) * cols)
                x_high[:, at], x_low[:, at] = halves(x_ref[k])
            dens[...] = jnp.zeros_like(dens)

        def dot(a, b):
            return jnp.dot(a, b, preferred_element_type=jnp.float32)

        value = dot(x_low[...], high_ref[0])
        value += dot(x_high[...], low_ref[0])
        value += dot(x_high[...], high_ref[0])
        squares = value * value * occ_ref[0, :1, :]
        folded = squares[:, :NZ]
        for c in range(1, cols // NZ):
            folded += squares[:, c * NZ : (c + 1) * NZ]
        dens[...] += folded
        for k, out in enumerate(outs):

            @pl.when(step == k)
            def _():
                out[:rows, :] = value

        @pl.when(step == group - 1)
        def _():
            dens_out[...] = jnp.zeros_like(dens_out)
            for line in range(lines):
                sums = jnp.sum(dens[line * NZ : (line + 1) * NZ, :].T, axis=0, keepdims=True) * scale
                dens_out[line : line + 1, :] = sums
            for out in outs:
                for c in range(cols // NZ):
                    out[rows:, c * NZ : (c + 1) * NZ] = dens_out[...]

    weight = pl.BlockSpec((1, depth, cols), lambda s: (s, 0, 0))
    out = jax.ShapeDtypeStruct((rows + EXTRA, cols), jnp.float32)
    return pl.pallas_call(
        body,
        grid=(group,),
        in_specs=[pl.BlockSpec(blocks.shape, lambda s: (0, 0, 0)), weight, weight, pl.BlockSpec((1, EXTRA, cols), lambda s: (s, 0, 0))],
        out_specs=[pl.BlockSpec((rows + EXTRA, cols), lambda s: (0, 0))] * group + [pl.BlockSpec((EXTRA, NZ), lambda s: (0, 0))],
        out_shape=[out] * group + [jax.ShapeDtypeStruct((EXTRA, NZ), jnp.float32)],
        scratch_shapes=[
            pltpu.VMEM((rows, depth), jnp.bfloat16),
            pltpu.VMEM((rows, depth), jnp.bfloat16),
            pltpu.VMEM((rows, NZ), jnp.float32),
        ],
        compiler_params=pltpu.CompilerParams(vmem_limit_bytes=VMEM),
        cost_estimate=pl.CostEstimate(flops=6 * rows * depth * cols * group, bytes_accessed=4 * depth * cols * group + 8 * rows * depth, transcendentals=0),
        name="turn",
    )(blocks, high, low, occ)


def finish(planes, before, after, v_loc, places, group):
    rows, cols = before.shape[-2:]
    lines = NY // group
    count = len(planes)
    points = count * NY * NZ
    factor = (3.0 / jnp.pi) ** (1.0 / 3.0)
    width = NZ
    flat, layout, scratch = [], [], []
    for plane in planes:
        for part, shape in zip(plane, ((group, rows, width), (group, EXTRA, NZ))):
            many = isinstance(part, list)
            layout.append(len(part) if many else 0)
            flat += part if many else [part]
            if many:
                scratch.append(pltpu.VMEM(shape, jnp.float32))

    def body(place, *refs):
        refs = list(refs)
        held = refs[len(refs) - len(scratch) :]
        got = []
        for many in layout:
            if many:
                kept = held.pop(0)
                for k in range(many):
                    kept[k] = refs.pop(0)[...]
                got.append(kept)
            else:
                got.append(refs.pop(0))
        before_ref, after_ref, v_ref, rotated, density, hpsi, band = refs[:7]
        near, far = got[0::2], got[1::2]

        def tile(p, y):
            y = y % NY
            r, h = place[y // lines], y % lines
            ref = before_ref if p < 0 else after_ref if p == count else near[p]
            return ref[r, h * NZ : (h + 1) * NZ, :]

        def density_line(p, y):
            r, h = place[y // lines], y % lines
            row = rows - EXTRA + h
            return near[p][r, row : row + 1, :] + far[p][r, h : h + 1, :]

        total = jnp.zeros((8, width), jnp.float32)
        for p in range(count):
            dens = jnp.concatenate([density_line(p, y) for y in range(NY)], axis=0)
            density[p * NY : (p + 1) * NY, :] = dens
            pot = v_ref[p * NY : (p + 1) * NY, :] - factor * jnp.exp(jnp.log(dens) * (1.0 / 3.0))
            pot = jnp.concatenate([pot, jnp.zeros((NZ - NY, NZ), jnp.float32)], axis=0).T
            for y in range(NY):
                here = tile(p, y)
                beside = tile(p - 1, y) + tile(p + 1, y) + tile(p, y - 1) + tile(p, y + 1)
                beside += pltpu.roll(here, 1, 0) + pltpu.roll(here, NZ - 1, 0)
                value = (pot[:, y : y + 1] + 3.0) * here - 0.5 * beside
                at = slice((p * NY + y) * NZ, (p * NY + y + 1) * NZ)
                rotated[at, :] = here
                hpsi[at, :] = value
                total += jnp.sum((here * value).reshape(NZ // 8, 8, width), axis=0)
        band[...] = jnp.sum(total, axis=0, keepdims=True)

    def column(array):
        shape = array.shape
        if shape[-1] == cols and shape[-2] == rows:
            return pl.BlockSpec(shape[:-1] + (width,), lambda c, _: (0,) * (len(shape) - 1) + (c,))
        return pl.BlockSpec(shape, lambda c, _: (0,) * len(shape))

    v_lines = v_loc.reshape(count * NY, NZ)
    ins = [*flat, before, after, v_lines]
    out_column = pl.BlockSpec((points, width), lambda c, _: (0, c))
    return pl.pallas_call(
        body,
        grid_spec=pltpu.PrefetchScalarGridSpec(
            num_scalar_prefetch=1,
            grid=(cols // width,),
            in_specs=[column(a) for a in ins],
            out_specs=[
                out_column,
                pl.BlockSpec((count * NY, NZ), lambda c, _: (0, 0)),
                out_column,
                pl.BlockSpec((1, width), lambda c, _: (0, c)),
            ],
            scratch_shapes=scratch,
        ),
        out_shape=[
            jax.ShapeDtypeStruct((points, cols), jnp.float32),
            jax.ShapeDtypeStruct((count * NY, NZ), jnp.float32),
            jax.ShapeDtypeStruct((points, cols), jnp.float32),
            jax.ShapeDtypeStruct((1, cols), jnp.float32),
        ],
        compiler_params=pltpu.CompilerParams(vmem_limit_bytes=VMEM),
        name="finish",
    )(places, *ins)


def shards(psi, rot, occ, v_loc):
    points, cols = psi.shape
    depth = rot.shape[0]
    n = lax.axis_size("orb")
    doms = lax.axis_size("dom")
    group = n // 2
    me = lax.axis_index("orb")
    pos = lax.rem(me, group)
    dom = lax.axis_index("dom")
    plane_points = NY * NZ
    planes = points // plane_points
    shares = jnp.stack([pos ^ s for s in range(group)]).astype(jnp.int32)

    def swap(block, s):
        return send(block, "orb", n, lambda a: a ^ s)

    def across(block):
        return send(block, "dom", doms, lambda a: (a + doms // 2) % doms)

    def beside(block):
        return send(block, "dom", doms, lambda a: a ^ 1)

    rows = depth // 4
    quarter = 2 * (dom // (doms // 2)) + lax.rem(dom, 2)
    own = lax.dynamic_slice_in_dim(rot, quarter * rows, rows)
    own = jnp.concatenate([own, jnp.broadcast_to(occ[None, :], (EXTRA, cols))], axis=0)
    first = collect([own] + [swap(own, s) for s in range(1, group)], MARK)
    places = jnp.stack([quarter, quarter ^ 2, quarter ^ 1, quarter ^ 3]).astype(jnp.int32)
    second = across(first)
    third = beside(first)
    fourth = beside(second)
    high, low, occ_rows = split_rot([(first, second, third, fourth)], places)

    order = [0, planes - 1] + list(range(1, planes - 1))
    gates = [[], [first], [second, third]] + [[] for _ in order]
    done = {}
    edges = {}
    for index, p in enumerate(order):
        lot = psi[p * plane_points : (p + 1) * plane_points]
        lot = after(jnp.concatenate([lot, lot]), gates[index])
        lot = lax.all_to_all(lot, "orb", split_axis=0, concat_axis=0, tiled=True)
        gates[index + 1].append(lot)
        if index == 2:
            lot = after(lot, [done[order[1]][0]])
        *outs, dens = turn(lot.reshape(n, plane_points // group, cols), high, low, occ_rows, 1.0 / depth)
        back = [outs[0]] + [swap(outs[s], s) for s in range(1, group)]
        if index == len(order) - 1 and index > 1:
            done[p] = (back, [swap(dens, group + s) for s in range(group)])
            continue
        stack = jnp.stack(back)
        done[p] = (stack, swap(stack[:, -EXTRA:, :NZ], group))
        if p == planes - 1:
            edges["before"] = send(stack, "dom", doms, lambda a: (a + 1) % doms)
        if p == 0:
            edges["after"] = send(stack, "dom", doms, lambda a: (a - 1) % doms)

    rotated, density, hpsi, band = finish(
        [done[p] for p in range(planes)], edges["before"], edges["after"], v_loc, shares, group
    )
    band = lax.psum(band.reshape(cols), "dom") / (points * doms)
    return rotated, density.reshape(points), hpsi, band


def solution(mesh):
    placed = (P("dom", "orb"), P(None, "orb"), P("orb"), P("dom"))
    return jax.shard_map(
        shards,
        mesh=mesh,
        in_specs=placed,
        out_specs=(P("dom", "orb"), P("dom"), P("dom", "orb"), P("orb")),
        check_vma=False,
    )
```

time: 314 us -> 243 us (0.77)
  starting transfers between devices: 114 us -> 44.4 us
  waiting for transfers between devices: 140 us -> 132 us
  other arithmetic: 2.41 us -> 8.72 us
  Pallas kernels: 30.8 us -> 36 us
    ppermute x52 -> x23, starting transfers between devices: 114 us -> 27.9 us  [send(): return lax.ppermute(block, axis, [(a, step(a)) for a in range(size)])]
    ppermute x52 -> x23, waiting for transfers between devices: 140 us -> 104 us  [send(): return lax.ppermute(block, axis, [(a, step(a)) for a in range(size)])]
    all_to_all x0 -> x3, waiting for transfers between devices: none -> 27.7 us  [shards(): lot = lax.all_to_all(lot, 'orb', split_axis=0, concat_axis=0, tiled=True)]
    all_to_all x0 -> x3, starting transfers between devices: none -> 16.5 us  [shards(): lot = lax.all_to_all(lot, 'orb', split_axis=0, concat_axis=0, tiled=True)]
    concatenate x0 -> x4, other arithmetic: none -> 6.84 us  [the longest x3 6.02 us: shards(): lot = after(jnp.concatenate([lot, lot]), gates[index])]
    dynamic_slice x2 -> x0, local copies, waits for them, and re-layouts: 6.34 us -> none  [shards(): block = lax.dynamic_slice_in_dim(psi, start, count * NZ)]
    slice x0 -> x3, local copies, waits for them, and re-layouts: none -> 4.35 us  [the longest x1 3.03 us: shards(): lot = psi[p * plane_points:(p + 1) * plane_points]]
    pallas_call x4, Pallas kernels: 21.3 us -> 25.5 us  [the longest x3 22.1 us: turn(): pl.pallas_call(body, grid=(group,), in_specs=[pl.BlockSpec(blocks.shape,...]
  transfers between devices with their start and end apart: 52 -> 26, of which waited for: 21 -> 10; matrix products, arithmetic and copies ran while one was open for 2% -> 5% of each run, Pallas kernels for 9% -> 12%
where the time goes in v2:
time: 243 us
  waiting for transfers between devices  132 us (54%)
  starting transfers between devices  44.4 us (18%)
  Pallas kernels  36 us (15%)
  local copies, waits for them, and re-layouts  15.6 us (6%)
  other arithmetic  8.72 us (4%)
  blocking collectives  5.64 us (2%)
    ppermute x23, waiting for transfers between devices, send(): return lax.ppermute(block, axis, [(a, step(a)) for a in range(size)])  104 us
    ppermute x23, starting transfers between devices, send(): return lax.ppermute(block, axis, [(a, step(a)) for a in range(size)])  27.9 us
    all_to_all x3, waiting for transfers between devices, shards(): lot = lax.all_to_all(lot, 'orb', split_axis=0, concat_axis=0, tiled=True)  27.7 us
    pallas_call x3, Pallas kernels, turn(): pl.pallas_call(body, grid=(group,), in_specs=[pl.BlockSpec(blocks.shape,...  22.1 us
    all_to_all x3, starting transfers between devices, shards(): lot = lax.all_to_all(lot, 'orb', split_axis=0, concat_axis=0, tiled=True)  16.5 us
    unnamed x18, local copies, waits for them, and re-layouts  10.5 us
    pallas_call x1, Pallas kernels, finish(): pl.pallas_call(body, grid_spec=pltpu.PrefetchScalarGridSpec(num_scalar_pr...  6.27 us
    concatenate x3, other arithmetic, shards(): lot = after(jnp.concatenate([lot, lot]), gates[index])  6.02 us
  transfers between devices with their start and end apart: 26, of which 10 were waited for; matrix products, arithmetic and copies ran while one was open for 5% of the time, Pallas kernels for 12%

profile of v2, /device:TPU:0, one launch (start us, length us, event | category | flops | bytes accessed | tf_op | source)
XLA Modules:
  0.0 242.7 jit_solution(5927863545945410603)
XLA Ops:
  3.8 2.9 %collective-permute-start = (f32[520,256]{1,0:T(8,128)}, f32[520,256]{1,0:T(8,128)}, u32[]{:S(2)}, u32[]{:S(2)}) collective-permute-start(f32[520,256]{1,0:T(8,128)} %pad_maximum_fusion.5.refs_0_), channel_id=1, source_target_pairs={{0,1},{1,0},{2,3},{3,2},{4,5},{5,4},{6,7},{7,6},{8,9},{9,8},{10,11... | collective-permute-start | bytes 1597448 | tf_op jit(solution)/shard_map/ppermute | solution.py:16
  8.3 3.0 %fusion = (f32[1024,256]{1,0:T(8,128)}, f32[1024,256]{1,0:T(8,128)S(1)}, f32[1024,256]{1,0:T(8,128)S(1)}) fusion(f32[3072,256]{1,0:T(8,128)} %param.4), kind=kLoop, calls=%fused_computation.10 | loop fusion | bytes 6291456 | tf_op jit(solution)/shard_map/slice | solution.py:287
  12.8 6.2 %all-to-all-start = ((f32[8,256,256]{2,1,0:T(8,128)}), f32[8,256,256]{2,1,0:T(8,128)}, u32[]{:S(2)}, u32[]{:S(2)}) async-start(f32[8,256,256]{2,1,0:T(8,128)} %bitcast.30), calls=%async_computation | async-start | bytes 4194304 | tf_op jit(solution)/shard_map/all_to_all | solution.py:289
  19.0 3.0 %pad_maximum_fusion.2 = f32[2048,256]{1,0:T(8,128)} fusion(f32[1024,256]{1,0:T(8,128)} %get-tuple-element.50), kind=kLoop, calls=%fused_computation.2 | loop fusion | flops 524288 | bytes 3145728 | tf_op jit(solution)/shard_map/concatenate | solution.py:288
  22.1 16.6 %collective-permute-done.2.refs_3_ = f32[520,256]{1,0:T(8,128)} collective-permute-done((f32[520,256]{1,0:T(8,128)}, f32[520,256]{1,0:T(8,128)}, u32[]{:S(2)}, u32[]{:S(2)}) %collective-permute-start.2) | collective-permute-done | bytes 532512 | tf_op jit(solution)/shard_map/ppermute | solution.py:16
  38.6 3.4 %collect.1.refs_0_ = f32[4,520,256]{2,1,0:T(8,128)} custom-call(f32[520,256]{1,0:T(8,128)} %pad_maximum_fusion.5.refs_0_, f32[520,256]{1,0:T(8,128)} %collective-permute-done.refs_1_, f32[520,256]{1,0:T(8,128)} %collective-permute-done.1.refs_2_, f32[520,256]{1,0:T(8,128)} %collective-permute-done.2.refs_3_), custom_call_target="tpu_custom_call" | custom-call | flops 40000000000 | bytes 4259840 | tf_op jit(solution)/shard_map/collect/pallas_call | solution.py:39
  42.0 27.7 %all-to-all-done.x_ref = f32[8,256,256]{2,1,0:T(8,128)} async-done(((f32[8,256,256]{2,1,0:T(8,128)}), f32[8,256,256]{2,1,0:T(8,128)}, u32[]{:S(2)}, u32[]{:S(2)}) %all-to-all-start) | async-done | bytes 2097184 | tf_op jit(solution)/shard_map/all_to_all | solution.py:289
  69.7 4.7 %all-to-all-start.2 = ((f32[8,256,256]{2,1,0:T(8,128)}), f32[8,256,256]{2,1,0:T(8,128)}, u32[]{:S(2)}, u32[]{:S(2)}) async-start(f32[8,256,256]{2,1,0:T(8,128)} %bitcast.29), calls=%async_computation.2 | async-start | bytes 4194304 | tf_op jit(solution)/shard_map/all_to_all | solution.py:289
  75.9 45.4 %collective-permute-done.3.refs_1_ = f32[4,520,256]{2,1,0:T(8,128)} collective-permute-done((f32[4,520,256]{2,1,0:T(8,128)}, f32[4,520,256]{2,1,0:T(8,128)}, u32[]{:S(2)}, u32[]{:S(2)}) %collective-permute-start.3) | collective-permute-done | bytes 2129952 | tf_op jit(solution)/shard_map/ppermute | solution.py:16
  124.2 5.7 %all-to-all-start.1 = ((f32[8,256,256]{2,1,0:T(8,128)}), f32[8,256,256]{2,1,0:T(8,128)}, u32[]{:S(2)}, u32[]{:S(2)}) async-start(f32[8,256,256]{2,1,0:T(8,128)} %bitcast.28), calls=%async_computation.1 | async-start | bytes 4194304 | tf_op jit(solution)/shard_map/all_to_all | solution.py:289
  129.9 1.6 copy-done.1
  131.5 1.6 copy-done.3
  133.1 4.2 %split_rot.1 = (bf16[4,2048,256]{2,1,0:T(8,128)(2,1)S(1)}, bf16[4,2048,256]{2,1,0:T(8,128)(2,1)S(1)}, f32[4,8,256]{2,1,0:T(8,128)S(1)}) custom-call(s32[4]{0:T(128)S(1)} %pad_add_fusion.1.place, f32[4,520,256]{2,1,0:T(8,128)S(1)} %copy-done.1, f32[4,520,256]{2,1,0:T(8,128)} %collective-permute-done.3.refs_1_, f32[4,520,256]{2,1,0:T(8,128)S(1)} %copy-done.3, ...), custom_call_target="tpu_custom_call" | custom-call | tf_op jit(solution)/shard_map/split_rot/pallas_call | solution.py:75
  137.4 8.3 %turn.4 = (f32[264,256]{1,0:T(8,128)S(1)}, f32[264,256]{1,0:T(8,128)S(1)}, f32[264,256]{1,0:T(8,128)S(1)}, f32[264,256]{1,0:T(8,128)S(1)}, f32[8,128]{1,0:T(8,128)}) custom-call(f32[8,256,256]{2,1,0:T(8,128)} %all-to-all-done.2.x_ref, bf16[4,2048,256]{2,1,0:T(8,128)(2,1)S(1)} %get-tuple-element.27.high_ref, ...), custom_call_target="tpu_custom_call" | custom-call | flops 3221225472 | bytes 12582912 | tf_op jit(solution)/shard_map/turn/pallas_call | solution.py:139
  145.7 2.0 collective-permute-start.10
  149.2 6.7 %turn.3 = (f32[264,256]{1,0:T(8,128)S(1)}, f32[264,256]{1,0:T(8,128)S(1)}, f32[264,256]{1,0:T(8,128)S(1)}, f32[264,256]{1,0:T(8,128)S(1)}, f32[8,128]{1,0:T(8,128)}) custom-call(f32[8,256,256]{2,1,0:T(8,128)} %all-to-all-done.x_ref, bf16[4,2048,256]{2,1,0:T(8,128)(2,1)S(1)} %get-tuple-element.27.high_ref, ...), custom_call_target="tpu_custom_call" | custom-call | flops 3221225472 | bytes 12582912 | tf_op jit(solution)/shard_map/turn/pallas_call | solution.py:139
  155.9 2.0 collective-permute-start.6
  159.4 12.5 %collective-permute-done.11 = f32[264,256]{1,0:T(8,128)S(1)} collective-permute-done((f32[264,256]{1,0:T(8,128)S(1)}, f32[264,256]{1,0:T(8,128)S(1)}, u32[]{:S(2)}, u32[]{:S(2)}) %collective-permute-start.11) | collective-permute-done | bytes 270368 | tf_op jit(solution)/shard_map/ppermute | solution.py:16
  171.9 7.9 %collective-permute-done.12 = f32[264,256]{1,0:T(8,128)S(1)} collective-permute-done((f32[264,256]{1,0:T(8,128)S(1)}, f32[264,256]{1,0:T(8,128)S(1)}, u32[]{:S(2)}, u32[]{:S(2)}) %collective-permute-start.12) | collective-permute-done | bytes 270368 | tf_op jit(solution)/shard_map/ppermute | solution.py:16
  180.0 4.9 %collective-permute-done.7 = f32[264,256]{1,0:T(8,128)S(1)} collective-permute-done((f32[264,256]{1,0:T(8,128)S(1)}, f32[264,256]{1,0:T(8,128)S(1)}, u32[]{:S(2)}, u32[]{:S(2)}) %collective-permute-start.7) | collective-permute-done | bytes 270368 | tf_op jit(solution)/shard_map/ppermute | solution.py:16
  184.9 5.9 %collective-permute-done.8 = f32[264,256]{1,0:T(8,128)S(1)} collective-permute-done((f32[264,256]{1,0:T(8,128)S(1)}, f32[264,256]{1,0:T(8,128)S(1)}, u32[]{:S(2)}, u32[]{:S(2)}) %collective-permute-start.8) | collective-permute-done | bytes 270368 | tf_op jit(solution)/shard_map/ppermute | solution.py:16
  193.7 2.5 %collective-permute-start.20 = (f32[4,8,128]{2,1,0:T(8,128)}, f32[4,8,128]{2,1,0:T(8,128)S(1)}, u32[]{:S(2)}, u32[]{:S(2)}) collective-permute-start(f32[4,8,128]{2,1,0:T(8,128)} %slice.21), channel_id=1, source_target_pairs={{0,4},{1,5},{2,6},{3,7},{4,0},{5,1},{6,2},{7,3},{8,12},{9,13},{10,... | collective-permute-start | bytes 49160 | tf_op jit(solution)/shard_map/ppermute | solution.py:16
  196.6 2.2 copy-done.6
  198.8 2.2 copy-done.8
  201.0 7.1 %turn.5 = (f32[264,256]{1,0:T(8,128)S(1)}, f32[264,256]{1,0:T(8,128)}, f32[264,256]{1,0:T(8,128)}, f32[264,256]{1,0:T(8,128)}, f32[8,128]{1,0:T(8,128)S(1)}) custom-call(f32[8,256,256]{2,1,0:T(8,128)} %bitcast.20.x_ref, bf16[4,2048,256]{2,1,0:T(8,128)(2,1)S(1)} %copy-done.6, bf16[4,2048,256]{2,1,0:T(8,128)(2,1)S(1)} %copy-done.8, ...), custom_call_target="tpu_custom_call" | custom-call | flops 3221225472 | bytes 12582912 | tf_op jit(solution)/shard_map/turn/pallas_call | solution.py:139
  211.6 2.5 %collective-permute-start.16 = (f32[8,128]{1,0:T(8,128)S(1)}, f32[8,128]{1,0:T(8,128)S(1)}, u32[]{:S(2)}, u32[]{:S(2)}) collective-permute-start(f32[8,128]{1,0:T(8,128)S(1)} %get-tuple-element.45), channel_id=1, source_target_pairs={{0,4},{1,5},{2,6},{3,7},{4,0},{5,1},{6,2},{7,3},{8,12},{9,13},{10,... | collective-permute-start | bytes 12296 | tf_op jit(solution)/shard_map/ppermute | solution.py:16
  214.8 6.6 %collective-permute-done.16.refs_6_ = f32[8,128]{1,0:T(8,128)S(1)} collective-permute-done((f32[8,128]{1,0:T(8,128)S(1)}, f32[8,128]{1,0:T(8,128)S(1)}, u32[]{:S(2)}, u32[]{:S(2)}) %collective-permute-start.16) | collective-permute-done | bytes 4128 | tf_op jit(solution)/shard_map/ppermute | solution.py:16
  221.4 2.4 collective-permute-start.18
  223.9 2.2 collective-permute-start.19
  226.8 3.3 %collective-permute-done.19.refs_9_ = f32[8,128]{1,0:T(8,128)S(1)} collective-permute-done((f32[8,128]{1,0:T(8,128)S(1)}, f32[8,128]{1,0:T(8,128)S(1)}, u32[]{:S(2)}, u32[]{:S(2)}) %collective-permute-start.19) | collective-permute-done | bytes 4128 | tf_op jit(solution)/shard_map/ppermute | solution.py:16
  230.2 6.3 %finish.1 = (f32[3072,256]{1,0:T(8,128)}, f32[24,128]{1,0:T(8,128)}, f32[3072,256]{1,0:T(8,128)}, f32[1,256]{1,0:T(1,128)S(1)}) custom-call(s32[4]{0:T(128)S(1)} %pad_add_fusion.place, f32[4,264,256]{2,1,0:T(8,128)} %pad_maximum_fusion.3.refs_0_, f32[4,8,128]{2,1,0:T(8,128)S(1)} %collective-permute-done.9.refs_1_, f32[264,256]{1,0:T(8,128)S(1)} %get-tuple-element.41.refs_2_, ...), custom_call_target="tpu_custom_call" | custom-call | tf_op jit(solution)/shard_map/finish/pallas_call | solution.py:224
  236.5 5.6 %psum.7 = f32[256]{0:T(256)S(1)} all-reduce(f32[256]{0:T(256)S(1)} %bitcast.27), channel_id=1, replica_groups=mesh['dom'=4,'orb'=8] {'dom'}, use_global_device_ids=true, to_apply=%region_0.1 | all-reduce | flops 256 | bytes 2048 | tf_op jit(solution)/shard_map/psum | solution.py:308
  (59 shorter events, 22.7 us)
Async XLA Ops:
  3.8 18.3 %collective-permute-start = (f32[520,256]{1,0:T(8,128)}, f32[520,256]{1,0:T(8,128)}, u32[]{:S(2)}, u32[]{:S(2)}) collective-permute-start(f32[520,256]{1,0:T(8,128)} %pad_maximum_fusion.5.refs_0_), channel_id=1, source_target_pairs={{0,1},{1,0},{2,3},{3,2},{4,5},{5,4},{6,7},{7,6},{8,9},{9,8},{10,11... | collective-permute-start | bytes 1597448 | tf_op jit(solution)/shard_map/ppermute | solution.py:16
  6.7 15.4 %collective-permute-start.1 = (f32[520,256]{1,0:T(8,128)}, f32[520,256]{1,0:T(8,128)}, u32[]{:S(2)}, u32[]{:S(2)}) collective-permute-start(f32[520,256]{1,0:T(8,128)} %pad_maximum_fusion.5.refs_0_), channel_id=1, source_target_pairs={{0,2},{1,3},{2,0},{3,1},{4,6},{5,7},{6,4},{7,5},{8,10},{9,11},{10,... | collective-permute-start | bytes 1597448 | tf_op jit(solution)/shard_map/ppermute | solution.py:16
  8.3 30.4 %collective-permute-start.2 = (f32[520,256]{1,0:T(8,128)}, f32[520,256]{1,0:T(8,128)}, u32[]{:S(2)}, u32[]{:S(2)}) collective-permute-start(f32[520,256]{1,0:T(8,128)} %pad_maximum_fusion.5.refs_0_), channel_id=1, source_target_pairs={{0,3},{1,2},{2,1},{3,0},{4,7},{5,6},{6,5},{7,4},{8,11},{9,10},{10,... | collective-permute-start | bytes 1597448 | tf_op jit(solution)/shard_map/ppermute | solution.py:16
  12.8 56.9 %all-to-all-start = ((f32[8,256,256]{2,1,0:T(8,128)}), f32[8,256,256]{2,1,0:T(8,128)}, u32[]{:S(2)}, u32[]{:S(2)}) async-start(f32[8,256,256]{2,1,0:T(8,128)} %bitcast.30), calls=%async_computation | async-start | bytes 4194304 | tf_op jit(solution)/shard_map/all_to_all | solution.py:289
  69.7 54.5 %all-to-all-start.2 = ((f32[8,256,256]{2,1,0:T(8,128)}), f32[8,256,256]{2,1,0:T(8,128)}, u32[]{:S(2)}, u32[]{:S(2)}) async-start(f32[8,256,256]{2,1,0:T(8,128)} %bitcast.29), calls=%async_computation.2 | async-start | bytes 4194304 | tf_op jit(solution)/shard_map/all_to_all | solution.py:289
  74.4 47.0 %collective-permute-start.3 = (f32[4,520,256]{2,1,0:T(8,128)}, f32[4,520,256]{2,1,0:T(8,128)}, u32[]{:S(2)}, u32[]{:S(2)}) collective-permute-start(f32[4,520,256]{2,1,0:T(8,128)} %collect.1.refs_0_), channel_id=1, source_target_pairs={{0,16},{8,24},{16,0},{24,8},{1,17},{9,25},{17,1},{25,9},{2,18},{10... | collective-permute-start | bytes 6389768 | tf_op jit(solution)/shard_map/ppermute | solution.py:16
  75.9 46.9 %collective-permute-start.4 = (f32[4,520,256]{2,1,0:T(8,128)}, f32[4,520,256]{2,1,0:T(8,128)S(1)}, u32[]{:S(2)}, u32[]{:S(2)}) collective-permute-start(f32[4,520,256]{2,1,0:T(8,128)} %collect.1.refs_0_), channel_id=1, source_target_pairs={{0,8},{8,0},{16,24},{24,16},{1,9},{9,1},{17,25},{25,17},{2,10},{10... | collective-permute-start | bytes 6389768 | tf_op jit(solution)/shard_map/ppermute | solution.py:16
  121.4 8.6 %collective-permute-start.5 = (f32[4,520,256]{2,1,0:T(8,128)}, f32[4,520,256]{2,1,0:T(8,128)}, u32[]{:S(2)}, u32[]{:S(2)}) collective-permute-start(f32[4,520,256]{2,1,0:T(8,128)} %collective-permute-done.3.refs_1_), channel_id=1, source_target_pairs={{0,8},{8,0},{16,24},{24,16},{1,9},{9,1},{17,25},{25,17},{2,10},{10... | collective-permute-start | bytes 6389768 | tf_op jit(solution)/shard_map/ppermute | solution.py:16
  124.2 72.4 %all-to-all-start.1 = ((f32[8,256,256]{2,1,0:T(8,128)}), f32[8,256,256]{2,1,0:T(8,128)}, u32[]{:S(2)}, u32[]{:S(2)}) async-start(f32[8,256,256]{2,1,0:T(8,128)} %bitcast.28), calls=%async_computation.1 | async-start | bytes 4194304 | tf_op jit(solution)/shard_map/all_to_all | solution.py:289
  129.9 1.6 copy-start.1
  137.4 11.8 %copy-start.5 = (bf16[4,2048,256]{2,1,0:T(8,128)(2,1)}, bf16[4,2048,256]{2,1,0:T(8,128)(2,1)S(1)}, u32[]{:S(2)}) copy-start(bf16[4,2048,256]{2,1,0:T(8,128)(2,1)S(1)} %get-tuple-element.27.high_ref) | copy-start | bytes 12582916
  137.4 11.8 %copy-start.7 = (bf16[4,2048,256]{2,1,0:T(8,128)(2,1)}, bf16[4,2048,256]{2,1,0:T(8,128)(2,1)S(1)}, u32[]{:S(2)}) copy-start(bf16[4,2048,256]{2,1,0:T(8,128)(2,1)S(1)} %get-tuple-element.28.low_ref) | copy-start | bytes 12582916
  145.7 13.7 %collective-permute-start.10 = (f32[264,256]{1,0:T(8,128)S(1)}, f32[264,256]{1,0:T(8,128)S(1)}, u32[]{:S(2)}, u32[]{:S(2)}) collective-permute-start(f32[264,256]{1,0:T(8,128)S(1)} %get-tuple-element.37), channel_id=1, source_target_pairs={{0,1},{1,0},{2,3},{3,2},{4,5},{5,4},{6,7},{7,6},{8,9},{9,8},{10,11... | collective-permute-start | bytes 811016 | tf_op jit(solution)/shard_map/ppermute | solution.py:16
  147.7 24.2 %collective-permute-start.11 = (f32[264,256]{1,0:T(8,128)S(1)}, f32[264,256]{1,0:T(8,128)S(1)}, u32[]{:S(2)}, u32[]{:S(2)}) collective-permute-start(f32[264,256]{1,0:T(8,128)S(1)} %get-tuple-element.38), channel_id=1, source_target_pairs={{0,2},{1,3},{2,0},{3,1},{4,6},{5,7},{6,4},{7,5},{8,10},{9,11},{10,... | collective-permute-start | bytes 811016 | tf_op jit(solution)/shard_map/ppermute | solution.py:16
  149.2 30.7 %collective-permute-start.12 = (f32[264,256]{1,0:T(8,128)S(1)}, f32[264,256]{1,0:T(8,128)S(1)}, u32[]{:S(2)}, u32[]{:S(2)}) collective-permute-start(f32[264,256]{1,0:T(8,128)S(1)} %get-tuple-element.39), channel_id=1, source_target_pairs={{0,3},{1,2},{2,1},{3,0},{4,7},{5,6},{6,5},{7,4},{8,11},{9,10},{10,... | collective-permute-start | bytes 811016 | tf_op jit(solution)/shard_map/ppermute | solution.py:16
  155.9 24.1 %collective-permute-start.6 = (f32[264,256]{1,0:T(8,128)S(1)}, f32[264,256]{1,0:T(8,128)S(1)}, u32[]{:S(2)}, u32[]{:S(2)}) collective-permute-start(f32[264,256]{1,0:T(8,128)S(1)} %get-tuple-element.31), channel_id=1, source_target_pairs={{0,1},{1,0},{2,3},{3,2},{4,5},{5,4},{6,7},{7,6},{8,9},{9,8},{10,11... | collective-permute-start | bytes 811016 | tf_op jit(solution)/shard_map/ppermute | solution.py:16
  158.0 26.9 %collective-permute-start.7 = (f32[264,256]{1,0:T(8,128)S(1)}, f32[264,256]{1,0:T(8,128)S(1)}, u32[]{:S(2)}, u32[]{:S(2)}) collective-permute-start(f32[264,256]{1,0:T(8,128)S(1)} %get-tuple-element.32), channel_id=1, source_target_pairs={{0,2},{1,3},{2,0},{3,1},{4,6},{5,7},{6,4},{7,5},{8,10},{9,11},{10,... | collective-permute-start | bytes 811016 | tf_op jit(solution)/shard_map/ppermute | solution.py:16
  159.4 31.3 %collective-permute-start.8 = (f32[264,256]{1,0:T(8,128)S(1)}, f32[264,256]{1,0:T(8,128)S(1)}, u32[]{:S(2)}, u32[]{:S(2)}) collective-permute-start(f32[264,256]{1,0:T(8,128)S(1)} %get-tuple-element.33), channel_id=1, source_target_pairs={{0,3},{1,2},{2,1},{3,0},{4,7},{5,6},{6,5},{7,4},{8,11},{9,10},{10,... | collective-permute-start | bytes 811016 | tf_op jit(solution)/shard_map/ppermute | solution.py:16
  179.9 31.6 %collective-permute-start.21 = (f32[4,264,256]{2,1,0:T(8,128)S(1)}, f32[4,264,256]{2,1,0:T(8,128)}, u32[]{:S(2)}, u32[]{:S(2)}) collective-permute-start(f32[4,264,256]{2,1,0:T(8,128)S(1)} %pad_maximum_fusion.4.refs_10_), channel_id=1, source_target_pairs={{0,8},{8,16},{16,24},{24,0},{1,9},{9,17},{17,25},{25,1},{2,10},{10... | collective-permute-start | bytes 3244040 | tf_op jit(solution)/shard_map/ppermute | solution.py:16
  191.8 22.2 %collective-permute-start.22 = (f32[4,264,256]{2,1,0:T(8,128)}, f32[4,264,256]{2,1,0:T(8,128)}, u32[]{:S(2)}, u32[]{:S(2)}) collective-permute-start(f32[4,264,256]{2,1,0:T(8,128)} %pad_maximum_fusion.3.refs_0_), channel_id=1, source_target_pairs={{0,24},{8,0},{16,8},{24,16},{1,25},{9,1},{17,9},{25,17},{2,26},{10... | collective-permute-start | bytes 3244040 | tf_op jit(solution)/shard_map/ppermute | solution.py:16
  193.7 15.2 %collective-permute-start.20 = (f32[4,8,128]{2,1,0:T(8,128)}, f32[4,8,128]{2,1,0:T(8,128)S(1)}, u32[]{:S(2)}, u32[]{:S(2)}) collective-permute-start(f32[4,8,128]{2,1,0:T(8,128)} %slice.21), channel_id=1, source_target_pairs={{0,4},{1,5},{2,6},{3,7},{4,0},{5,1},{6,2},{7,3},{8,12},{9,13},{10,... | collective-permute-start | bytes 49160 | tf_op jit(solution)/shard_map/ppermute | solution.py:16
  196.2 14.4 %collective-permute-start.9 = (f32[4,8,128]{2,1,0:T(8,128)S(1)}, f32[4,8,128]{2,1,0:T(8,128)S(1)}, u32[]{:S(2)}, u32[]{:S(2)}) collective-permute-start(f32[4,8,128]{2,1,0:T(8,128)S(1)} %slice.20), channel_id=1, source_target_pairs={{0,4},{1,5},{2,6},{3,7},{4,0},{5,1},{6,2},{7,3},{8,12},{9,13},{10,... | collective-permute-start | bytes 49160 | tf_op jit(solution)/shard_map/ppermute | solution.py:16
  196.6 2.2 copy-start.6
  198.8 2.2 copy-start.8
  201.0 29.2 %copy-start.4 = (f32[3072]{0:T(1024)S(1)}, f32[3072]{0:T(1024)}, u32[]{:S(2)}) copy-start(f32[3072]{0:T(1024)} %param.7) | copy-start | bytes 36868
  208.1 22.1 %collective-permute-start.13 = (f32[264,256]{1,0:T(8,128)}, f32[264,256]{1,0:T(8,128)}, u32[]{:S(2)}, u32[]{:S(2)}) collective-permute-start(f32[264,256]{1,0:T(8,128)} %get-tuple-element.42), channel_id=1, source_target_pairs={{0,1},{1,0},{2,3},{3,2},{4,5},{5,4},{6,7},{7,6},{8,9},{9,8},{10,11... | collective-permute-start | bytes 811016 | tf_op jit(solution)/shard_map/ppermute | solution.py:16
  208.9 21.2 %collective-permute-start.14 = (f32[264,256]{1,0:T(8,128)}, f32[264,256]{1,0:T(8,128)}, u32[]{:S(2)}, u32[]{:S(2)}) collective-permute-start(f32[264,256]{1,0:T(8,128)} %get-tuple-element.43), channel_id=1, source_target_pairs={{0,2},{1,3},{2,0},{3,1},{4,6},{5,7},{6,4},{7,5},{8,10},{9,11},{10,... | collective-permute-start | bytes 811016 | tf_op jit(solution)/shard_map/ppermute | solution.py:16
  210.5 19.7 %collective-permute-start.15 = (f32[264,256]{1,0:T(8,128)}, f32[264,256]{1,0:T(8,128)}, u32[]{:S(2)}, u32[]{:S(2)}) collective-permute-start(f32[264,256]{1,0:T(8,128)} %get-tuple-element.44), channel_id=1, source_target_pairs={{0,3},{1,2},{2,1},{3,0},{4,7},{5,6},{6,5},{7,4},{8,11},{9,10},{10,... | collective-permute-start | bytes 811016 | tf_op jit(solution)/shard_map/ppermute | solution.py:16
  211.6 9.9 %collective-permute-start.16 = (f32[8,128]{1,0:T(8,128)S(1)}, f32[8,128]{1,0:T(8,128)S(1)}, u32[]{:S(2)}, u32[]{:S(2)}) collective-permute-start(f32[8,128]{1,0:T(8,128)S(1)} %get-tuple-element.45), channel_id=1, source_target_pairs={{0,4},{1,5},{2,6},{3,7},{4,0},{5,1},{6,2},{7,3},{8,12},{9,13},{10,... | collective-permute-start | bytes 12296 | tf_op jit(solution)/shard_map/ppermute | solution.py:16
  214.0 9.8 %collective-permute-start.17 = (f32[8,128]{1,0:T(8,128)S(1)}, f32[8,128]{1,0:T(8,128)S(1)}, u32[]{:S(2)}, u32[]{:S(2)}) collective-permute-start(f32[8,128]{1,0:T(8,128)S(1)} %get-tuple-element.45), channel_id=1, source_target_pairs={{0,5},{1,4},{2,7},{3,6},{4,1},{5,0},{6,3},{7,2},{8,13},{9,12},{10,... | collective-permute-start | bytes 12296 | tf_op jit(solution)/shard_map/ppermute | solution.py:16
  221.4 5.4 %collective-permute-start.18 = (f32[8,128]{1,0:T(8,128)S(1)}, f32[8,128]{1,0:T(8,128)S(1)}, u32[]{:S(2)}, u32[]{:S(2)}) collective-permute-start(f32[8,128]{1,0:T(8,128)S(1)} %get-tuple-element.45), channel_id=1, source_target_pairs={{0,6},{1,7},{2,4},{3,5},{4,2},{5,3},{6,0},{7,1},{8,14},{9,15},{10,... | collective-permute-start | bytes 12296 | tf_op jit(solution)/shard_map/ppermute | solution.py:16
  223.9 6.3 %collective-permute-start.19 = (f32[8,128]{1,0:T(8,128)S(1)}, f32[8,128]{1,0:T(8,128)S(1)}, u32[]{:S(2)}, u32[]{:S(2)}) collective-permute-start(f32[8,128]{1,0:T(8,128)S(1)} %get-tuple-element.45), channel_id=1, source_target_pairs={{0,7},{1,6},{2,5},{3,4},{4,3},{5,2},{6,1},{7,0},{8,15},{9,14},{10,... | collective-permute-start | bytes 12296 | tf_op jit(solution)/shard_map/ppermute | solution.py:16
  (3 other events, 4.5 us)

commit v3 on v2

--- a/solution.py
+++ b/solution.py
@@ -8,7 +8,8 @@
 NY = 8
 NZ = 128
 EXTRA = 8
-VMEM = 20 << 20
+VMEM = 32 << 20
+MOST = 60 << 20
 MARK = 40
 
 
@@ -23,6 +24,32 @@
 
 def after(array, others):
     return lax.optimization_barrier((array, *others))[0] if others else array
+
+
+def load(psi, parts, group):
+    cols = psi.shape[1]
+    heights = [rows for _, rows, _ in parts]
+    total = sum(heights)
+
+    def body(*refs):
+        at = 0
+        for ref, height in zip(refs, heights):
+            for twice in range(2):
+                refs[-1][twice, 0, at : at + height, :] = ref[...]
+            at += height
+
+    def part(first, rows, step):
+        return pl.BlockSpec((rows, cols), lambda s: (first + s * step, 0))
+
+    return pl.pallas_call(
+        body,
+        grid=(group,),
+        in_specs=[part(*p) for p in parts],
+        out_specs=pl.BlockSpec((2, 1, total, cols), lambda s: (0, s, 0, 0)),
+        out_shape=jax.ShapeDtypeStruct((2, group, total, cols), psi.dtype),
+        compiler_params=pltpu.CompilerParams(vmem_limit_bytes=VMEM),
+        name="load",
+    )(*[psi] * len(parts))
 
 
 def collect(pieces, span):
@@ -48,17 +75,20 @@
 
 
 def split_rot(sets, places):
-    half, rows, cols = sets[0][0].shape
+    _, rows, cols = sets[0][0].shape
     rows -= EXTRA
     parts = len(sets[0])
     depth = rows * parts
-    group = half * len(sets)
+    sizes = [pieces[0].shape[0] for pieces in sets]
+    starts = [sum(sizes[:number]) for number in range(len(sets))]
+    group = sum(sizes)
 
     def body(place, *refs):
         ins, (high, low, occ) = refs[: parts * len(sets)], refs[parts * len(sets) :]
-        for number in range(len(sets)):
-
-            @pl.when(pl.program_id(0) // half == number)
+        step = pl.program_id(0)
+        for number, (start, size) in enumerate(zip(starts, sizes)):
+
+            @pl.when((step >= start) & (step < start + size))
             def _():
                 for k in range(parts):
                     piece = ins[number * parts + k]
@@ -67,7 +97,7 @@
                 occ[0] = ins[number * parts][0, rows:, :]
 
     def block(number):
-        return pl.BlockSpec((1, rows + EXTRA, cols), lambda s, _: (jnp.clip(s - number * half, 0, half - 1), 0, 0))
+        return pl.BlockSpec((1, rows + EXTRA, cols), lambda s, _: (jnp.clip(s - starts[number], 0, sizes[number] - 1), 0, 0))
 
     def out(height):
         return pl.BlockSpec((1, height, cols), lambda s, _: (s, 0, 0))
@@ -97,11 +127,20 @@
 
     def body(x_ref, high_ref, low_ref, occ_ref, *refs):
         outs = refs[:group]
-        dens_out, x_high, x_low, dens = refs[group:]
+        dens_out, x_high, x_low, dens, high_here, low_here, sems = refs[group:]
         step = pl.program_id(0)
+
+        def copies(s):
+            return (
+                pltpu.make_async_copy(high_ref.at[s], high_here.at[s], sems.at[0, s]),
+                pltpu.make_async_copy(low_ref.at[s], low_here.at[s], sems.at[1, s]),
+            )
 
         @pl.when(step == 0)
         def _():
+            for s in range(group):
+                for copy in copies(s):
+                    copy.start()
             for k in range(count):
                 at = slice(k * cols, (k + 1) * cols)
                 x_high[:, at], x_low[:, at] = halves(x_ref[k])
@@ -110,9 +149,11 @@
         def dot(a, b):
             return jnp.dot(a, b, preferred_element_type=jnp.float32)
 
-        value = dot(x_low[...], high_ref[0])
-        value += dot(x_high[...], low_ref[0])
-        value += dot(x_high[...], high_ref[0])
+        for copy in copies(step):
+            copy.wait()
+        value = dot(x_low[...], high_here[step])
+        value += dot(x_high[...], low_here[step])
+        value += dot(x_high[...], high_here[step])
         squares = value * value * occ_ref[0, :1, :]
         folded = squares[:, :NZ]
         for c in range(1, cols // NZ):
@@ -134,7 +175,7 @@
                 for c in range(cols // NZ):
                     out[rows:, c * NZ : (c + 1) * NZ] = dens_out[...]
 
-    weight = pl.BlockSpec((1, depth, cols), lambda s: (s, 0, 0))
+    weight = pl.BlockSpec(memory_space=pltpu.HBM)
     out = jax.ShapeDtypeStruct((rows + EXTRA, cols), jnp.float32)
     return pl.pallas_call(
         body,
@@ -146,54 +187,40 @@
             pltpu.VMEM((rows, depth), jnp.bfloat16),
             pltpu.VMEM((rows, depth), jnp.bfloat16),
             pltpu.VMEM((rows, NZ), jnp.float32),
+            pltpu.VMEM((group, depth, cols), jnp.bfloat16),
+            pltpu.VMEM((group, depth, cols), jnp.bfloat16),
+            pltpu.SemaphoreType.DMA((2, group)),
         ],
-        compiler_params=pltpu.CompilerParams(vmem_limit_bytes=VMEM),
+        compiler_params=pltpu.CompilerParams(vmem_limit_bytes=MOST),
         cost_estimate=pl.CostEstimate(flops=6 * rows * depth * cols * group, bytes_accessed=4 * depth * cols * group + 8 * rows * depth, transcendentals=0),
         name="turn",
     )(blocks, high, low, occ)
 
 
-def finish(planes, before, after, v_loc, places, group):
-    rows, cols = before.shape[-2:]
-    lines = NY // group
-    count = len(planes)
+def finish(near, far, where, before, after, v_loc, places, scale):
+    cols = before.shape[-1]
+    lines = len(where[0])
+    count = len(where)
     points = count * NY * NZ
     factor = (3.0 / jnp.pi) ** (1.0 / 3.0)
     width = NZ
-    flat, layout, scratch = [], [], []
-    for plane in planes:
-        for part, shape in zip(plane, ((group, rows, width), (group, EXTRA, NZ))):
-            many = isinstance(part, list)
-            layout.append(len(part) if many else 0)
-            flat += part if many else [part]
-            if many:
-                scratch.append(pltpu.VMEM(shape, jnp.float32))
+    chunks = len(near)
 
     def body(place, *refs):
-        refs = list(refs)
-        held = refs[len(refs) - len(scratch) :]
-        got = []
-        for many in layout:
-            if many:
-                kept = held.pop(0)
-                for k in range(many):
-                    kept[k] = refs.pop(0)[...]
-                got.append(kept)
-            else:
-                got.append(refs.pop(0))
-        before_ref, after_ref, v_ref, rotated, density, hpsi, band = refs[:7]
-        near, far = got[0::2], got[1::2]
+        near_refs, far_refs = refs[:chunks], refs[chunks : 2 * chunks]
+        before_ref, after_ref, v_ref, rotated, density, hpsi, band = refs[2 * chunks :]
 
         def tile(p, y):
-            y = y % NY
-            r, h = place[y // lines], y % lines
-            ref = before_ref if p < 0 else after_ref if p == count else near[p]
-            return ref[r, h * NZ : (h + 1) * NZ, :]
+            r, h = place[y % NY // lines], y % lines
+            if p < 0 or p == count:
+                return (before_ref if p < 0 else after_ref)[r, h * NZ : (h + 1) * NZ, :]
+            chunk, line = where[p][h]
+            return near_refs[chunk][r, line * NZ : (line + 1) * NZ, :]
 
         def density_line(p, y):
-            r, h = place[y // lines], y % lines
-            row = rows - EXTRA + h
-            return near[p][r, row : row + 1, :] + far[p][r, h : h + 1, :]
+            r, (chunk, line) = place[y // lines], where[p][y % lines]
+            row = near[chunk].shape[1] - EXTRA + line
+            return near_refs[chunk][r, row : row + 1, :] + far_refs[chunk][r, line : line + 1, :]
 
         total = jnp.zeros((8, width), jnp.float32)
         for p in range(count):
@@ -210,30 +237,30 @@
                 rotated[at, :] = here
                 hpsi[at, :] = value
                 total += jnp.sum((here * value).reshape(NZ // 8, 8, width), axis=0)
-        band[...] = jnp.sum(total, axis=0, keepdims=True)
+        band[...] = jnp.sum(total, axis=0, keepdims=True) * scale
 
     def column(array):
         shape = array.shape
-        if shape[-1] == cols and shape[-2] == rows:
-            return pl.BlockSpec(shape[:-1] + (width,), lambda c, _: (0,) * (len(shape) - 1) + (c,))
+        return pl.BlockSpec(shape[:-1] + (width,), lambda c, _: (0,) * (len(shape) - 1) + (c,))
+
+    def fixed(array):
+        shape = array.shape
         return pl.BlockSpec(shape, lambda c, _: (0,) * len(shape))
 
     v_lines = v_loc.reshape(count * NY, NZ)
-    ins = [*flat, before, after, v_lines]
     out_column = pl.BlockSpec((points, width), lambda c, _: (0, c))
     return pl.pallas_call(
         body,
         grid_spec=pltpu.PrefetchScalarGridSpec(
             num_scalar_prefetch=1,
             grid=(cols // width,),
-            in_specs=[column(a) for a in ins],
+            in_specs=[column(a) for a in near] + [fixed(a) for a in far] + [column(before), column(after), fixed(v_lines)],
             out_specs=[
                 out_column,
                 pl.BlockSpec((count * NY, NZ), lambda c, _: (0, 0)),
                 out_column,
                 pl.BlockSpec((1, width), lambda c, _: (0, c)),
             ],
-            scratch_shapes=scratch,
         ),
         out_shape=[
             jax.ShapeDtypeStruct((points, cols), jnp.float32),
@@ -241,9 +268,9 @@
             jax.ShapeDtypeStruct((points, cols), jnp.float32),
             jax.ShapeDtypeStruct((1, cols), jnp.float32),
         ],
-        compiler_params=pltpu.CompilerParams(vmem_limit_bytes=VMEM),
+        compiler_params=pltpu.CompilerParams(vmem_limit_bytes=MOST),
         name="finish",
-    )(places, *ins)
+    )(places, *near, *far, before, after, v_lines)
 
 
 def shards(psi, rot, occ, v_loc):
@@ -272,41 +299,43 @@
     quarter = 2 * (dom // (doms // 2)) + lax.rem(dom, 2)
     own = lax.dynamic_slice_in_dim(rot, quarter * rows, rows)
     own = jnp.concatenate([own, jnp.broadcast_to(occ[None, :], (EXTRA, cols))], axis=0)
-    first = collect([own] + [swap(own, s) for s in range(1, group)], MARK)
+    firsts = [own[None], collect([swap(own, s) for s in range(1, group)], MARK)]
     places = jnp.stack([quarter, quarter ^ 2, quarter ^ 1, quarter ^ 3]).astype(jnp.int32)
-    second = across(first)
-    third = beside(first)
-    fourth = beside(second)
-    high, low, occ_rows = split_rot([(first, second, third, fourth)], places)
-
-    order = [0, planes - 1] + list(range(1, planes - 1))
-    gates = [[], [first], [second, third]] + [[] for _ in order]
-    done = {}
-    edges = {}
-    for index, p in enumerate(order):
-        lot = psi[p * plane_points : (p + 1) * plane_points]
-        lot = after(jnp.concatenate([lot, lot]), gates[index])
-        lot = lax.all_to_all(lot, "orb", split_axis=0, concat_axis=0, tiled=True)
+    seconds = [across(first) for first in firsts]
+    thirds = [beside(first) for first in firsts]
+    fourths = [beside(second) for second in seconds]
+    high, low, occ_rows = split_rot(list(zip(firsts, seconds, thirds, fourths)), places)
+
+    lines = NY // group
+    ends = [(0, 0, lines), (planes - 1, 0, lines)]
+    chunks = [ends] + [[(p, 0, lines)] for p in range(1, planes - 1)]
+    gates = [[], [high]] + [[] for _ in chunks]
+    where = [[None] * lines for _ in range(planes)]
+    near, far = [], []
+    for index, chunk in enumerate(chunks):
+        height = 0
+        lot = []
+        for p, h, count in chunk:
+            for k in range(count):
+                where[p][h + k] = (index, height + k)
+            height += count
+            lot.append(((p * NY + h) // count, count * NZ, lines // count))
+        lot = load(psi, lot, group).reshape(n * height * NZ, cols)
+        lot = lax.all_to_all(after(lot, gates[index]), "orb", split_axis=0, concat_axis=0, tiled=True)
         gates[index + 1].append(lot)
-        if index == 2:
-            lot = after(lot, [done[order[1]][0]])
-        *outs, dens = turn(lot.reshape(n, plane_points // group, cols), high, low, occ_rows, 1.0 / depth)
-        back = [outs[0]] + [swap(outs[s], s) for s in range(1, group)]
-        if index == len(order) - 1 and index > 1:
-            done[p] = (back, [swap(dens, group + s) for s in range(group)])
-            continue
-        stack = jnp.stack(back)
-        done[p] = (stack, swap(stack[:, -EXTRA:, :NZ], group))
-        if p == planes - 1:
-            edges["before"] = send(stack, "dom", doms, lambda a: (a + 1) % doms)
-        if p == 0:
-            edges["after"] = send(stack, "dom", doms, lambda a: (a - 1) % doms)
+        if index == 1:
+            lot = after(lot, near)
+        *outs, dens = turn(lot.reshape(n, height * NZ, cols), high, low, occ_rows, 1.0 / depth)
+        near.append(jnp.stack([outs[0]] + [swap(outs[s], s) for s in range(1, group)]))
+        far.append(swap(near[-1][:, -EXTRA:, :NZ], group))
+        if index == 0:
+            first, last = near[0][:, : lines * NZ], near[0][:, lines * NZ : 2 * lines * NZ]
+            edges = [send(last, "dom", doms, lambda a: (a + 1) % doms), send(first, "dom", doms, lambda a: (a - 1) % doms)]
 
     rotated, density, hpsi, band = finish(
-        [done[p] for p in range(planes)], edges["before"], edges["after"], v_loc, shares, group
+        near, far, where, *edges, v_loc, shares, 1.0 / (points * doms)
     )
-    band = lax.psum(band.reshape(cols), "dom") / (points * doms)
-    return rotated, density.reshape(points), hpsi, band
+    return rotated, density.reshape(points), hpsi, lax.psum(band.reshape(cols), "dom")
 
 
 def solution(mesh):

time: 243 us -> 232 us (0.955)
  starting transfers between devices: 44.4 us -> 32.4 us
  other arithmetic: 8.72 us -> 2.97 us
  local copies, waits for them, and re-layouts: 15.6 us -> 19.5 us
    ppermute x23 -> x19, waiting for transfers between devices: 104 us -> 123 us  [send(): return lax.ppermute(block, axis, [(a, step(a)) for a in range(size)])]
    all_to_all x3 -> x2, waiting for transfers between devices: 27.7 us -> 9.52 us  [shards(): lax.all_to_all(after(lot, gates[index]), 'orb', split_axis=0, concat_axis...]
    ppermute x23 -> x19, starting transfers between devices: 27.9 us -> 21.8 us  [send(): return lax.ppermute(block, axis, [(a, step(a)) for a in range(size)])]
    unnamed x18 -> x26, local copies, waits for them, and re-layouts: 10.5 us -> 16.6 us
    concatenate x3 -> x0, other arithmetic: 6.02 us -> none  [shards(): lot = after(jnp.concatenate([lot, lot]), gates[index])]
    all_to_all x3 -> x2, starting transfers between devices: 16.5 us -> 10.6 us  [shards(): lax.all_to_all(after(lot, gates[index]), 'orb', split_axis=0, concat_axis...]
    pallas_call x3 -> x2, Pallas kernels: 22.1 us -> 21.2 us  [turn(): pl.pallas_call(body, grid=(group,), in_specs=[pl.BlockSpec(blocks.shape,...]
  transfers between devices with their start and end apart: 26 -> 21, of which waited for: 10 -> 11; matrix products, arithmetic and copies ran while one was open for 5% -> 2% of each run, Pallas kernels for 12% -> 13%
where the time goes in v3:
time: 232 us; the launch traced here: 231 us
  waiting for transfers between devices  132 us (57%)
  Pallas kernels  36.7 us (16%)
  starting transfers between devices  32.4 us (14%)
  local copies, waits for them, and re-layouts  19.5 us (8%)
  blocking collectives  6.55 us (3%)
  other arithmetic  2.97 us (1%)
    ppermute x19, waiting for transfers between devices, send(): return lax.ppermute(block, axis, [(a, step(a)) for a in range(size)])  123 us
    ppermute x19, starting transfers between devices, send(): return lax.ppermute(block, axis, [(a, step(a)) for a in range(size)])  21.8 us
    pallas_call x2, Pallas kernels, turn(): pl.pallas_call(body, grid=(group,), in_specs=[pl.BlockSpec(blocks.shape,...  21.2 us
    unnamed x26, local copies, waits for them, and re-layouts  16.6 us
    all_to_all x2, starting transfers between devices, shards(): lax.all_to_all(after(lot, gates[index]), 'orb', split_axis=0, concat_axis...  10.6 us
    all_to_all x2, waiting for transfers between devices, shards(): lax.all_to_all(after(lot, gates[index]), 'orb', split_axis=0, concat_axis...  9.52 us
    pallas_call x1, Pallas kernels, finish(): pl.pallas_call(body, grid_spec=pltpu.PrefetchScalarGridSpec(num_scalar_pr...  6.58 us
    psum x1, blocking collectives, shards(): lax.psum(band.reshape(cols), 'dom')  6.55 us
  transfers between devices with their start and end apart: 21, of which 11 were waited for; matrix products, arithmetic and copies ran while one was open for 2% of the time, Pallas kernels for 13%

profile of v3, /device:TPU:0, one launch (start us, length us, event | category | flops | bytes accessed | tf_op | source)
XLA Modules:
  0.0 231.4 jit_solution(3379320202680656061)
XLA Ops:
  3.0 3.0 %collective-permute-start.3 = (f32[520,256]{1,0:T(8,128)S(1)}, f32[520,256]{1,0:T(8,128)}, u32[]{:S(2)}, u32[]{:S(2)}) collective-permute-start(f32[520,256]{1,0:T(8,128)S(1)} %get-tuple-element.40), channel_id=1, source_target_pairs={{0,1},{1,0},{2,3},{3,2},{4,5},{5,4},{6,7},{7,6},{8,9},{9,8},{10,11... | collective-permute-start | bytes 1597448 | tf_op jit(solution)/shard_map/ppermute | solution.py:17
  6.0 1.6 collective-permute-start.4
  7.6 1.9 copy-done.1
  10.1 2.0 copy-done.3
  12.1 6.2 %all-to-all-start = ((f32[8,512,256]{2,1,0:T(8,128)}), f32[8,512,256]{2,1,0:T(8,128)}, u32[]{:S(2)}, u32[]{:S(2)}) async-start(f32[8,512,256]{2,1,0:T(8,128)} %bitcast.26), calls=%async_computation | async-start | bytes 8388608 | tf_op jit(solution)/shard_map/all_to_all | solution.py:324
  18.4 2.8 %collective-permute-done.4.refs_1_ = f32[520,256]{1,0:T(8,128)} collective-permute-done((f32[520,256]{1,0:T(8,128)S(1)}, f32[520,256]{1,0:T(8,128)}, u32[]{:S(2)}, u32[]{:S(2)}) %collective-permute-start.4) | collective-permute-done | bytes 532512 | tf_op jit(solution)/shard_map/ppermute | solution.py:17
  21.2 21.1 %collective-permute-done.5.refs_2_ = f32[520,256]{1,0:T(8,128)} collective-permute-done((f32[520,256]{1,0:T(8,128)S(1)}, f32[520,256]{1,0:T(8,128)}, u32[]{:S(2)}, u32[]{:S(2)}) %collective-permute-start.5) | collective-permute-done | bytes 532512 | tf_op jit(solution)/shard_map/ppermute | solution.py:17
  42.3 3.0 %collect.1.refs_4_ = f32[3,520,256]{2,1,0:T(8,128)} custom-call(f32[520,256]{1,0:T(8,128)} %collective-permute-done.3.refs_0_, f32[520,256]{1,0:T(8,128)} %collective-permute-done.4.refs_1_, f32[520,256]{1,0:T(8,128)} %collective-permute-done.5.refs_2_), custom_call_target="tpu_custom_call" | custom-call | flops 40000000000 | bytes 3194880 | tf_op jit(solution)/shard_map/collect/pallas_call | solution.py:66
  45.3 2.0 collective-permute-start.6
  47.3 32.9 %collective-permute-done.6.refs_5_ = f32[3,520,256]{2,1,0:T(8,128)} collective-permute-done((f32[3,520,256]{2,1,0:T(8,128)}, f32[3,520,256]{2,1,0:T(8,128)}, u32[]{:S(2)}, u32[]{:S(2)}) %collective-permute-start.6) | collective-permute-done | bytes 1597472 | tf_op jit(solution)/shard_map/ppermute | solution.py:17
  81.9 12.9 %collective-permute-done.refs_1_ = f32[1,520,256]{2,1,0:T(8,128)S(1)} collective-permute-done((f32[1,520,256]{2,1,0:T(8,128)S(1)}, f32[1,520,256]{2,1,0:T(8,128)S(1)}, u32[]{:S(2)}, u32[]{:S(2)}) %collective-permute-start) | collective-permute-done | bytes 532512 | tf_op jit(solution)/shard_map/ppermute | solution.py:17
  94.8 1.9 copy-done.2
  99.9 5.0 %split_rot.1 = (bf16[4,2048,256]{2,1,0:T(8,128)(2,1)S(1)}, bf16[4,2048,256]{2,1,0:T(8,128)(2,1)S(1)}, f32[4,8,256]{2,1,0:T(8,128)S(1)}) custom-call(s32[4]{0:T(128)S(1)} %pad_add_fusion.1.place, f32[1,520,256]{2,1,0:T(8,128)S(1)} %get-tuple-element.41.refs_0_, f32[1,520,256]{2,1,0:T(8,128)S(1)} %collective-permute-done.refs_1_, ...), custom_call_target="tpu_custom_call" | custom-call | tf_op jit(solution)/shard_map/split_rot/pallas_call | solution.py:105
  104.9 2.0 copy-done.6
  106.9 1.9 copy-done.7
  109.4 9.5 %all-to-all-done.x_ref = f32[8,512,256]{2,1,0:T(8,128)} async-done(((f32[8,512,256]{2,1,0:T(8,128)}), f32[8,512,256]{2,1,0:T(8,128)}, u32[]{:S(2)}, u32[]{:S(2)}) %all-to-all-start) | async-done | bytes 4194336 | tf_op jit(solution)/shard_map/all_to_all | solution.py:324
  118.9 4.4 %all-to-all-start.1 = ((f32[8,256,256]{2,1,0:T(8,128)}), f32[8,256,256]{2,1,0:T(8,128)}, u32[]{:S(2)}, u32[]{:S(2)}) async-start(f32[8,256,256]{2,1,0:T(8,128)} %bitcast.27), calls=%async_computation.1 | async-start | bytes 4194304 | tf_op jit(solution)/shard_map/all_to_all | solution.py:324
  123.3 12.7 %turn.2 = (f32[520,256]{1,0:T(8,128)}, f32[520,256]{1,0:T(8,128)}, f32[520,256]{1,0:T(8,128)}, f32[520,256]{1,0:T(8,128)}, f32[8,128]{1,0:T(8,128)}) custom-call(f32[8,512,256]{2,1,0:T(8,128)} %all-to-all-done.x_ref, bf16[4,2048,256]{2,1,0:T(8,128)(2,1)} %copy-done.6, bf16[4,2048,256]{2,1,0:T(8,128)(2,1)} %copy-done.7, f32[4,8,256]{2,1,0:T(8,128)} %copy-done.8), custom_call_target="tpu_custom_call" | custom-call | flops 6442450944 | bytes 16777216 | tf_op jit(solution)/shard_map/turn/pallas_call | solution.py:180
  136.0 1.9 collective-permute-start.9
  139.6 19.9 %collective-permute-done.9 = f32[520,256]{1,0:T(8,128)S(1)} collective-permute-done((f32[520,256]{1,0:T(8,128)}, f32[520,256]{1,0:T(8,128)S(1)}, u32[]{:S(2)}, u32[]{:S(2)}) %collective-permute-start.9) | collective-permute-done | bytes 532512 | tf_op jit(solution)/shard_map/ppermute | solution.py:17
  159.5 11.7 %collective-permute-done.10 = f32[520,256]{1,0:T(8,128)S(1)} collective-permute-done((f32[520,256]{1,0:T(8,128)}, f32[520,256]{1,0:T(8,128)S(1)}, u32[]{:S(2)}, u32[]{:S(2)}) %collective-permute-start.10) | collective-permute-done | bytes 532512 | tf_op jit(solution)/shard_map/ppermute | solution.py:17
  171.2 10.5 %collective-permute-done.11 = f32[520,256]{1,0:T(8,128)S(1)} collective-permute-done((f32[520,256]{1,0:T(8,128)}, f32[520,256]{1,0:T(8,128)S(1)}, u32[]{:S(2)}, u32[]{:S(2)}) %collective-permute-start.11) | collective-permute-done | bytes 532512 | tf_op jit(solution)/shard_map/ppermute | solution.py:17
  185.8 1.7 collective-permute-start.18
  187.5 8.5 %turn.3 = (f32[264,256]{1,0:T(8,128)}, f32[264,256]{1,0:T(8,128)}, f32[264,256]{1,0:T(8,128)}, f32[264,256]{1,0:T(8,128)}, f32[8,128]{1,0:T(8,128)}) custom-call(f32[8,256,256]{2,1,0:T(8,128)} %bitcast.17.x_ref, bf16[4,2048,256]{2,1,0:T(8,128)(2,1)} %copy-done.6, bf16[4,2048,256]{2,1,0:T(8,128)(2,1)} %copy-done.7, f32[4,8,256]{2,1,0:T(8,128)} %copy-done.8), custom_call_target="tpu_custom_call" | custom-call | flops 3221225472 | bytes 12582912 | tf_op jit(solution)/shard_map/turn/pallas_call | solution.py:180
  197.0 2.5 %collective-permute-start.14 = (f32[264,256]{1,0:T(8,128)}, f32[264,256]{1,0:T(8,128)S(1)}, u32[]{:S(2)}, u32[]{:S(2)}) collective-permute-start(f32[264,256]{1,0:T(8,128)} %get-tuple-element.33), channel_id=1, source_target_pairs={{0,3},{1,2},{2,1},{3,0},{4,7},{5,6},{6,5},{7,4},{8,11},{9,10},{10,... | collective-permute-start | bytes 811016 | tf_op jit(solution)/shard_map/ppermute | solution.py:17
  200.3 4.5 %collective-permute-done.12 = f32[264,256]{1,0:T(8,128)S(1)} collective-permute-done((f32[264,256]{1,0:T(8,128)}, f32[264,256]{1,0:T(8,128)S(1)}, u32[]{:S(2)}, u32[]{:S(2)}) %collective-permute-start.12) | collective-permute-done | bytes 270368 | tf_op jit(solution)/shard_map/ppermute | solution.py:17
  204.8 2.4 %collective-permute-start.15 = (f32[4,8,128]{2,1,0:T(8,128)S(1)}, f32[4,8,128]{2,1,0:T(8,128)S(1)}, u32[]{:S(2)}, u32[]{:S(2)}) collective-permute-start(f32[4,8,128]{2,1,0:T(8,128)S(1)} %slice.16), channel_id=1, source_target_pairs={{0,4},{1,5},{2,6},{3,7},{4,0},{5,1},{6,2},{7,3},{8,12},{9,13},{10,... | collective-permute-start | bytes 49160 | tf_op jit(solution)/shard_map/ppermute | solution.py:17
  207.2 4.7 %collective-permute-done.14 = f32[264,256]{1,0:T(8,128)S(1)} collective-permute-done((f32[264,256]{1,0:T(8,128)}, f32[264,256]{1,0:T(8,128)S(1)}, u32[]{:S(2)}, u32[]{:S(2)}) %collective-permute-start.14) | collective-permute-done | bytes 270368 | tf_op jit(solution)/shard_map/ppermute | solution.py:17
  213.0 2.3 %collective-permute-start.16 = (f32[4,8,128]{2,1,0:T(8,128)S(1)}, f32[4,8,128]{2,1,0:T(8,128)S(1)}, u32[]{:S(2)}, u32[]{:S(2)}) collective-permute-start(f32[4,8,128]{2,1,0:T(8,128)S(1)} %slice.17), channel_id=1, source_target_pairs={{0,4},{1,5},{2,6},{3,7},{4,0},{5,1},{6,2},{7,3},{8,12},{9,13},{10,... | collective-permute-start | bytes 49160 | tf_op jit(solution)/shard_map/ppermute | solution.py:17
  215.9 1.8 collective-permute-done.16.refs_3_
  218.3 6.6 %finish.1 = (f32[3072,256]{1,0:T(8,128)}, f32[24,128]{1,0:T(8,128)}, f32[3072,256]{1,0:T(8,128)}, f32[1,256]{1,0:T(1,128)}) custom-call(s32[4]{0:T(128)} %pad_add_fusion.place, f32[4,520,256]{2,1,0:T(8,128)} %copy-done.9, f32[4,264,256]{2,1,0:T(8,128)} %copy-done.10, f32[4,8,128]{2,1,0:T(8,128)} %copy-done.11, f32[4,8,128]{2,1,0:T(8,128)} %copy-done.12, ...), custom_call_target="tpu_custom_call" | custom-call | tf_op jit(solution)/shard_map/finish/pallas_call | solution.py:252
  224.9 6.6 %psum.7 = f32[256]{0:T(256)} all-reduce(f32[256]{0:T(256)} %bitcast.37), channel_id=1, replica_groups=mesh['dom'=4,'orb'=8] {'dom'}, use_global_device_ids=true, to_apply=%region_0.1 | all-reduce | flops 256 | bytes 2048 | tf_op jit(solution)/shard_map/psum | solution.py:338
  (54 shorter events, 18.0 us)
Async XLA Ops:
  0.6 1.6 copy-start
  3.0 15.3 %collective-permute-start.3 = (f32[520,256]{1,0:T(8,128)S(1)}, f32[520,256]{1,0:T(8,128)}, u32[]{:S(2)}, u32[]{:S(2)}) collective-permute-start(f32[520,256]{1,0:T(8,128)S(1)} %get-tuple-element.40), channel_id=1, source_target_pairs={{0,1},{1,0},{2,3},{3,2},{4,5},{5,4},{6,7},{7,6},{8,9},{9,8},{10,11... | collective-permute-start | bytes 1597448 | tf_op jit(solution)/shard_map/ppermute | solution.py:17
  6.0 15.1 %collective-permute-start.4 = (f32[520,256]{1,0:T(8,128)S(1)}, f32[520,256]{1,0:T(8,128)}, u32[]{:S(2)}, u32[]{:S(2)}) collective-permute-start(f32[520,256]{1,0:T(8,128)S(1)} %get-tuple-element.40), channel_id=1, source_target_pairs={{0,2},{1,3},{2,0},{3,1},{4,6},{5,7},{6,4},{7,5},{8,10},{9,11},{10,... | collective-permute-start | bytes 1597448 | tf_op jit(solution)/shard_map/ppermute | solution.py:17
  7.6 34.7 %collective-permute-start.5 = (f32[520,256]{1,0:T(8,128)S(1)}, f32[520,256]{1,0:T(8,128)}, u32[]{:S(2)}, u32[]{:S(2)}) collective-permute-start(f32[520,256]{1,0:T(8,128)S(1)} %get-tuple-element.40), channel_id=1, source_target_pairs={{0,3},{1,2},{2,1},{3,0},{4,7},{5,6},{6,5},{7,4},{8,11},{9,10},{10,... | collective-permute-start | bytes 1597448 | tf_op jit(solution)/shard_map/ppermute | solution.py:17
  7.6 1.9 copy-start.1
  10.1 2.0 copy-start.3
  12.1 106.8 %all-to-all-start = ((f32[8,512,256]{2,1,0:T(8,128)}), f32[8,512,256]{2,1,0:T(8,128)}, u32[]{:S(2)}, u32[]{:S(2)}) async-start(f32[8,512,256]{2,1,0:T(8,128)} %bitcast.26), calls=%async_computation | async-start | bytes 8388608 | tf_op jit(solution)/shard_map/all_to_all | solution.py:324
  45.3 35.0 %collective-permute-start.6 = (f32[3,520,256]{2,1,0:T(8,128)}, f32[3,520,256]{2,1,0:T(8,128)}, u32[]{:S(2)}, u32[]{:S(2)}) collective-permute-start(f32[3,520,256]{2,1,0:T(8,128)} %collect.1.refs_4_), channel_id=1, source_target_pairs={{0,16},{8,24},{16,0},{24,8},{1,17},{9,25},{17,1},{25,9},{2,18},{10... | collective-permute-start | bytes 4792328 | tf_op jit(solution)/shard_map/ppermute | solution.py:17
  47.3 51.1 %collective-permute-start.7 = (f32[3,520,256]{2,1,0:T(8,128)}, f32[3,520,256]{2,1,0:T(8,128)}, u32[]{:S(2)}, u32[]{:S(2)}) collective-permute-start(f32[3,520,256]{2,1,0:T(8,128)} %collect.1.refs_4_), channel_id=1, source_target_pairs={{0,8},{8,0},{16,24},{24,16},{1,9},{9,1},{17,25},{25,17},{2,10},{10... | collective-permute-start | bytes 4792328 | tf_op jit(solution)/shard_map/ppermute | solution.py:17
  80.3 18.2 %collective-permute-start.8 = (f32[3,520,256]{2,1,0:T(8,128)}, f32[3,520,256]{2,1,0:T(8,128)}, u32[]{:S(2)}, u32[]{:S(2)}) collective-permute-start(f32[3,520,256]{2,1,0:T(8,128)} %collective-permute-done.6.refs_5_), channel_id=1, source_target_pairs={{0,8},{8,0},{16,24},{24,16},{1,9},{9,1},{17,25},{25,17},{2,10},{10... | collective-permute-start | bytes 4792328 | tf_op jit(solution)/shard_map/ppermute | solution.py:17
  80.3 14.5 %collective-permute-start = (f32[1,520,256]{2,1,0:T(8,128)S(1)}, f32[1,520,256]{2,1,0:T(8,128)S(1)}, u32[]{:S(2)}, u32[]{:S(2)}) collective-permute-start(f32[1,520,256]{2,1,0:T(8,128)S(1)} %get-tuple-element.41.refs_0_), channel_id=1, source_target_pairs={{0,16},{8,24},{16,0},{24,8},{1,17},{9,25},{17,1},{25,9},{2,18},{10... | collective-permute-start | bytes 1597448 | tf_op jit(solution)/shard_map/ppermute | solution.py:17
  81.7 16.8 %collective-permute-start.1 = (f32[1,520,256]{2,1,0:T(8,128)S(1)}, f32[1,520,256]{2,1,0:T(8,128)}, u32[]{:S(2)}, u32[]{:S(2)}) collective-permute-start(f32[1,520,256]{2,1,0:T(8,128)S(1)} %get-tuple-element.41.refs_0_), channel_id=1, source_target_pairs={{0,8},{8,0},{16,24},{24,16},{1,9},{9,1},{17,25},{25,17},{2,10},{10... | collective-permute-start | bytes 1597448 | tf_op jit(solution)/shard_map/ppermute | solution.py:17
  94.8 3.6 %collective-permute-start.2 = (f32[1,520,256]{2,1,0:T(8,128)S(1)}, f32[1,520,256]{2,1,0:T(8,128)}, u32[]{:S(2)}, u32[]{:S(2)}) collective-permute-start(f32[1,520,256]{2,1,0:T(8,128)S(1)} %collective-permute-done.refs_1_), channel_id=1, source_target_pairs={{0,8},{8,0},{16,24},{24,16},{1,9},{9,1},{17,25},{25,17},{2,10},{10... | collective-permute-start | bytes 1597448 | tf_op jit(solution)/shard_map/ppermute | solution.py:17
  94.8 1.9 copy-start.2
  97.0 1.3 copy-start.4
  98.5 1.4 copy-start.5
  104.9 2.0 copy-start.6
  106.9 1.9 copy-start.7
  118.9 68.6 %all-to-all-start.1 = ((f32[8,256,256]{2,1,0:T(8,128)}), f32[8,256,256]{2,1,0:T(8,128)}, u32[]{:S(2)}, u32[]{:S(2)}) async-start(f32[8,256,256]{2,1,0:T(8,128)} %bitcast.27), calls=%async_computation.1 | async-start | bytes 4194304 | tf_op jit(solution)/shard_map/all_to_all | solution.py:324
  136.0 23.4 %collective-permute-start.9 = (f32[520,256]{1,0:T(8,128)}, f32[520,256]{1,0:T(8,128)S(1)}, u32[]{:S(2)}, u32[]{:S(2)}) collective-permute-start(f32[520,256]{1,0:T(8,128)} %get-tuple-element.25), channel_id=1, source_target_pairs={{0,1},{1,0},{2,3},{3,2},{4,5},{5,4},{6,7},{7,6},{8,9},{9,8},{10,11... | collective-permute-start | bytes 1597448 | tf_op jit(solution)/shard_map/ppermute | solution.py:17
  138.0 33.2 %collective-permute-start.10 = (f32[520,256]{1,0:T(8,128)}, f32[520,256]{1,0:T(8,128)S(1)}, u32[]{:S(2)}, u32[]{:S(2)}) collective-permute-start(f32[520,256]{1,0:T(8,128)} %get-tuple-element.26), channel_id=1, source_target_pairs={{0,2},{1,3},{2,0},{3,1},{4,6},{5,7},{6,4},{7,5},{8,10},{9,11},{10,... | collective-permute-start | bytes 1597448 | tf_op jit(solution)/shard_map/ppermute | solution.py:17
  139.5 42.2 %collective-permute-start.11 = (f32[520,256]{1,0:T(8,128)}, f32[520,256]{1,0:T(8,128)S(1)}, u32[]{:S(2)}, u32[]{:S(2)}) collective-permute-start(f32[520,256]{1,0:T(8,128)} %get-tuple-element.27), channel_id=1, source_target_pairs={{0,3},{1,2},{2,1},{3,0},{4,7},{5,6},{6,5},{7,4},{8,11},{9,10},{10,... | collective-permute-start | bytes 1597448 | tf_op jit(solution)/shard_map/ppermute | solution.py:17
  182.9 1.4 copy-start.9
  185.8 31.9 %collective-permute-start.17 = (f32[4,256,256]{2,1,0:T(8,128)}, f32[4,256,256]{2,1,0:T(8,128)}, u32[]{:S(2)}, u32[]{:S(2)}) collective-permute-start(f32[4,256,256]{2,1,0:T(8,128)} %get-tuple-element.39), channel_id=1, source_target_pairs={{0,8},{8,16},{16,24},{24,0},{1,9},{9,17},{17,25},{25,1},{2,10},{10... | collective-permute-start | bytes 3145736 | tf_op jit(solution)/shard_map/ppermute | solution.py:17
  185.8 31.9 %collective-permute-start.18 = (f32[4,256,256]{2,1,0:T(8,128)}, f32[4,256,256]{2,1,0:T(8,128)}, u32[]{:S(2)}, u32[]{:S(2)}) collective-permute-start(f32[4,256,256]{2,1,0:T(8,128)} %get-tuple-element.38), channel_id=1, source_target_pairs={{0,24},{8,0},{16,8},{24,16},{1,25},{9,1},{17,9},{25,17},{2,26},{10... | collective-permute-start | bytes 3145736 | tf_op jit(solution)/shard_map/ppermute | solution.py:17
  196.0 8.8 %collective-permute-start.12 = (f32[264,256]{1,0:T(8,128)}, f32[264,256]{1,0:T(8,128)S(1)}, u32[]{:S(2)}, u32[]{:S(2)}) collective-permute-start(f32[264,256]{1,0:T(8,128)} %get-tuple-element.31), channel_id=1, source_target_pairs={{0,1},{1,0},{2,3},{3,2},{4,5},{5,4},{6,7},{7,6},{8,9},{9,8},{10,11... | collective-permute-start | bytes 811016 | tf_op jit(solution)/shard_map/ppermute | solution.py:17
  196.7 10.5 %collective-permute-start.13 = (f32[264,256]{1,0:T(8,128)}, f32[264,256]{1,0:T(8,128)S(1)}, u32[]{:S(2)}, u32[]{:S(2)}) collective-permute-start(f32[264,256]{1,0:T(8,128)} %get-tuple-element.32), channel_id=1, source_target_pairs={{0,2},{1,3},{2,0},{3,1},{4,6},{5,7},{6,4},{7,5},{8,10},{9,11},{10,... | collective-permute-start | bytes 811016 | tf_op jit(solution)/shard_map/ppermute | solution.py:17
  197.0 14.8 %collective-permute-start.14 = (f32[264,256]{1,0:T(8,128)}, f32[264,256]{1,0:T(8,128)S(1)}, u32[]{:S(2)}, u32[]{:S(2)}) collective-permute-start(f32[264,256]{1,0:T(8,128)} %get-tuple-element.33), channel_id=1, source_target_pairs={{0,3},{1,2},{2,1},{3,0},{4,7},{5,6},{6,5},{7,4},{8,11},{9,10},{10,... | collective-permute-start | bytes 811016 | tf_op jit(solution)/shard_map/ppermute | solution.py:17
  204.8 11.1 %collective-permute-start.15 = (f32[4,8,128]{2,1,0:T(8,128)S(1)}, f32[4,8,128]{2,1,0:T(8,128)S(1)}, u32[]{:S(2)}, u32[]{:S(2)}) collective-permute-start(f32[4,8,128]{2,1,0:T(8,128)S(1)} %slice.16), channel_id=1, source_target_pairs={{0,4},{1,5},{2,6},{3,7},{4,0},{5,1},{6,2},{7,3},{8,12},{9,13},{10,... | collective-permute-start | bytes 49160 | tf_op jit(solution)/shard_map/ppermute | solution.py:17
  212.9 4.8 %copy-start.10 = (f32[4,264,256]{2,1,0:T(8,128)}, f32[4,264,256]{2,1,0:T(8,128)S(1)}, u32[]{:S(2)}) copy-start(f32[4,264,256]{2,1,0:T(8,128)S(1)} %pad_maximum_fusion.1.refs_1_) | copy-start | bytes 3244036
  213.0 4.7 %collective-permute-start.16 = (f32[4,8,128]{2,1,0:T(8,128)S(1)}, f32[4,8,128]{2,1,0:T(8,128)S(1)}, u32[]{:S(2)}, u32[]{:S(2)}) collective-permute-start(f32[4,8,128]{2,1,0:T(8,128)S(1)} %slice.17), channel_id=1, source_target_pairs={{0,4},{1,5},{2,6},{3,7},{4,0},{5,1},{6,2},{7,3},{8,12},{9,13},{10,... | collective-permute-start | bytes 49160 | tf_op jit(solution)/shard_map/ppermute | solution.py:17
  215.8 1.9 copy-start.11
  (2 other events, 1.2 us)

commit v4 on v3

--- a/solution.py
+++ b/solution.py
@@ -120,8 +120,8 @@
     )(places, *[piece for pieces in sets for piece in pieces])
 
 
-def turn(blocks, high, low, occ, scale):
-    count, rows, cols = blocks.shape
+def turn(blocks, first, rows, high, low, occ, scale):
+    count, _, cols = blocks.shape
     group, depth, _ = high.shape
     lines = rows // NZ
 
@@ -180,7 +180,7 @@
     return pl.pallas_call(
         body,
         grid=(group,),
-        in_specs=[pl.BlockSpec(blocks.shape, lambda s: (0, 0, 0)), weight, weight, pl.BlockSpec((1, EXTRA, cols), lambda s: (s, 0, 0))],
+        in_specs=[pl.BlockSpec((count, rows, cols), lambda s: (0, first // rows, 0)), weight, weight, pl.BlockSpec((1, EXTRA, cols), lambda s: (s, 0, 0))],
         out_specs=[pl.BlockSpec((rows + EXTRA, cols), lambda s: (0, 0))] * group + [pl.BlockSpec((EXTRA, NZ), lambda s: (0, 0))],
         out_shape=[out] * group + [jax.ShapeDtypeStruct((EXTRA, NZ), jnp.float32)],
         scratch_shapes=[
@@ -307,30 +307,29 @@
     high, low, occ_rows = split_rot(list(zip(firsts, seconds, thirds, fourths)), places)
 
     lines = NY // group
-    ends = [(0, 0, lines), (planes - 1, 0, lines)]
-    chunks = [ends] + [[(p, 0, lines)] for p in range(1, planes - 1)]
-    gates = [[], [high]] + [[] for _ in chunks]
+    lots = [[(0, 0, lines), (planes - 1, 0, lines)], [(p, 0, lines) for p in range(1, planes - 1)]]
     where = [[None] * lines for _ in range(planes)]
-    near, far = [], []
-    for index, chunk in enumerate(chunks):
-        height = 0
-        lot = []
-        for p, h, count in chunk:
+    near, far, edges = [], [], []
+    gate = []
+    for lot in lots:
+        height = sum(count for _, _, count in lot) * NZ
+        rows = load(psi, [((p * NY + h) // count, count * NZ, lines // count) for p, h, count in lot], group)
+        rows = after(rows.reshape(n * height, cols), gate)
+        rows = lax.all_to_all(rows, "orb", split_axis=0, concat_axis=0, tiled=True).reshape(n, height, cols)
+        at = 0
+        for p, h, count in lot:
             for k in range(count):
-                where[p][h + k] = (index, height + k)
-            height += count
-            lot.append(((p * NY + h) // count, count * NZ, lines // count))
-        lot = load(psi, lot, group).reshape(n * height * NZ, cols)
-        lot = lax.all_to_all(after(lot, gates[index]), "orb", split_axis=0, concat_axis=0, tiled=True)
-        gates[index + 1].append(lot)
-        if index == 1:
-            lot = after(lot, near)
-        *outs, dens = turn(lot.reshape(n, height * NZ, cols), high, low, occ_rows, 1.0 / depth)
-        near.append(jnp.stack([outs[0]] + [swap(outs[s], s) for s in range(1, group)]))
-        far.append(swap(near[-1][:, -EXTRA:, :NZ], group))
-        if index == 0:
-            first, last = near[0][:, : lines * NZ], near[0][:, lines * NZ : 2 * lines * NZ]
-            edges = [send(last, "dom", doms, lambda a: (a + 1) % doms), send(first, "dom", doms, lambda a: (a - 1) % doms)]
+                where[p][h + k] = (len(near), k)
+            *outs, _ = turn(rows, at, count * NZ, high, low, occ_rows, 1.0 / depth)
+            at += count * NZ
+            if not near:
+                gate = [rows, high]
+            near.append(jnp.stack([outs[0]] + [swap(outs[s], s) for s in range(1, group)]))
+            far.append(swap(near[-1][:, -EXTRA:, :NZ], group))
+            if p == 0:
+                edges.append(send(near[-1], "dom", doms, lambda a: (a - 1) % doms))
+            if p == planes - 1:
+                edges.insert(0, send(near[-1], "dom", doms, lambda a: (a + 1) % doms))
 
     rotated, density, hpsi, band = finish(
         near, far, where, *edges, v_loc, shares, 1.0 / (points * doms)

time: 232 us -> 228 us (0.983)
  waiting for transfers between devices: 132 us -> 120 us
  starting transfers between devices: 32.4 us -> 38.6 us
  Pallas kernels: 36.7 us -> 41 us
  local copies, waits for them, and re-layouts: 19.5 us -> 16.8 us
    ppermute x19 -> x23, waiting for transfers between devices: 123 us -> 110 us  [send(): return lax.ppermute(block, axis, [(a, step(a)) for a in range(size)])]
    ppermute x19 -> x23, starting transfers between devices: 21.8 us -> 28 us  [send(): return lax.ppermute(block, axis, [(a, step(a)) for a in range(size)])]
    pallas_call x2 -> x3, Pallas kernels: 21.2 us -> 25.3 us  [turn(): pl.pallas_call(body, grid=(group,), in_specs=[pl.BlockSpec((count, rows,...]
    unnamed x26 -> x36, local copies, waits for them, and re-layouts: 16.6 us -> 16 us
  transfers between devices with their start and end apart: 21 -> 25, of which waited for: 11 -> 13; matrix products, arithmetic and copies ran while one was open for 2% -> 2% of each run, Pallas kernels for 13% -> 15%
where the time goes in v4:
time: 228 us; the launch traced here: 227 us
  waiting for transfers between devices  120 us (53%)
  Pallas kernels  41 us (18%)
  starting transfers between devices  38.6 us (17%)
  local copies, waits for them, and re-layouts  16.8 us (7%)
  blocking collectives  6.35 us (3%)
  other arithmetic  4.11 us (2%)
    ppermute x23, waiting for transfers between devices, send(): return lax.ppermute(block, axis, [(a, step(a)) for a in range(size)])  110 us
    ppermute x23, starting transfers between devices, send(): return lax.ppermute(block, axis, [(a, step(a)) for a in range(size)])  28 us
    pallas_call x3, Pallas kernels, turn(): pl.pallas_call(body, grid=(group,), in_specs=[pl.BlockSpec((count, rows,...  25.3 us
    unnamed x36, local copies, waits for them, and re-layouts  16 us
    all_to_all x2, starting transfers between devices, shards(): lax.all_to_all(rows, 'orb', split_axis=0, concat_axis=0, tiled=True)  10.6 us
    all_to_all x2, waiting for transfers between devices, shards(): lax.all_to_all(rows, 'orb', split_axis=0, concat_axis=0, tiled=True)  9.18 us
    pallas_call x1, Pallas kernels, finish(): pl.pallas_call(body, grid_spec=pltpu.PrefetchScalarGridSpec(num_scalar_pr...  6.75 us
    psum x1, blocking collectives, shards(): lax.psum(band.reshape(cols), 'dom')  6.35 us
  transfers between devices with their start and end apart: 25, of which 13 were waited for; matrix products, arithmetic and copies ran while one was open for 2% of the time, Pallas kernels for 15%

profile of v4, /device:TPU:0, one launch (start us, length us, event | category | flops | bytes accessed | tf_op | source)
XLA Modules:
  0.0 227.3 jit_solution(13232709930026090047)
XLA Ops:
  2.4 3.0 %collective-permute-start.3 = (f32[520,256]{1,0:T(8,128)S(1)}, f32[520,256]{1,0:T(8,128)}, u32[]{:S(2)}, u32[]{:S(2)}) collective-permute-start(f32[520,256]{1,0:T(8,128)S(1)} %get-tuple-element.44), channel_id=1, source_target_pairs={{0,1},{1,0},{2,3},{3,2},{4,5},{5,4},{6,7},{7,6},{8,9},{9,8},{10,11... | collective-permute-start | bytes 1597448 | tf_op jit(solution)/shard_map/ppermute | solution.py:17
  9.5 1.9 copy-done.5
  11.4 6.2 %all-to-all-start = ((f32[8,512,256]{2,1,0:T(8,128)}), f32[8,512,256]{2,1,0:T(8,128)}, u32[]{:S(2)}, u32[]{:S(2)}) async-start(f32[8,512,256]{2,1,0:T(8,128)} %bitcast.28), calls=%async_computation | async-start | bytes 8388608 | tf_op jit(solution)/shard_map/all_to_all | solution.py:318
  17.6 2.9 %collective-permute-done.4.refs_1_ = f32[520,256]{1,0:T(8,128)} collective-permute-done((f32[520,256]{1,0:T(8,128)S(1)}, f32[520,256]{1,0:T(8,128)}, u32[]{:S(2)}, u32[]{:S(2)}) %collective-permute-start.4) | collective-permute-done | bytes 532512 | tf_op jit(solution)/shard_map/ppermute | solution.py:17
  20.5 21.2 %collective-permute-done.5.refs_2_ = f32[520,256]{1,0:T(8,128)} collective-permute-done((f32[520,256]{1,0:T(8,128)S(1)}, f32[520,256]{1,0:T(8,128)}, u32[]{:S(2)}, u32[]{:S(2)}) %collective-permute-start.5) | collective-permute-done | bytes 532512 | tf_op jit(solution)/shard_map/ppermute | solution.py:17
  41.7 3.0 %collect.1.refs_4_ = f32[3,520,256]{2,1,0:T(8,128)} custom-call(f32[520,256]{1,0:T(8,128)} %collective-permute-done.3.refs_0_, f32[520,256]{1,0:T(8,128)} %collective-permute-done.4.refs_1_, f32[520,256]{1,0:T(8,128)} %collective-permute-done.5.refs_2_), custom_call_target="tpu_custom_call" | custom-call | flops 40000000000 | bytes 3194880 | tf_op jit(solution)/shard_map/collect/pallas_call | solution.py:66
  44.7 2.0 collective-permute-start.6
  46.7 33.0 %collective-permute-done.6.refs_5_ = f32[3,520,256]{2,1,0:T(8,128)} collective-permute-done((f32[3,520,256]{2,1,0:T(8,128)}, f32[3,520,256]{2,1,0:T(8,128)}, u32[]{:S(2)}, u32[]{:S(2)}) %collective-permute-start.6) | collective-permute-done | bytes 1597472 | tf_op jit(solution)/shard_map/ppermute | solution.py:17
  81.3 12.9 %collective-permute-done.refs_1_ = f32[1,520,256]{2,1,0:T(8,128)S(1)} collective-permute-done((f32[1,520,256]{2,1,0:T(8,128)S(1)}, f32[1,520,256]{2,1,0:T(8,128)S(1)}, u32[]{:S(2)}, u32[]{:S(2)}) %collective-permute-start) | collective-permute-done | bytes 532512 | tf_op jit(solution)/shard_map/ppermute | solution.py:17
  94.2 1.9 copy-done.2
  99.3 5.0 %split_rot.1 = (bf16[4,2048,256]{2,1,0:T(8,128)(2,1)S(1)}, bf16[4,2048,256]{2,1,0:T(8,128)(2,1)S(1)}, f32[4,8,256]{2,1,0:T(8,128)S(1)}) custom-call(s32[4]{0:T(128)S(1)} %pad_add_fusion.1.place, f32[1,520,256]{2,1,0:T(8,128)S(1)} %get-tuple-element.45.refs_0_, f32[1,520,256]{2,1,0:T(8,128)S(1)} %collective-permute-done.refs_1_, ...), custom_call_target="tpu_custom_call" | custom-call | tf_op jit(solution)/shard_map/split_rot/pallas_call | solution.py:105
  104.3 2.0 copy-done.3
  106.3 2.1 copy-done.4
  109.0 9.2 %all-to-all-done.x_ref = f32[8,512,256]{2,1,0:T(8,128)} async-done(((f32[8,512,256]{2,1,0:T(8,128)}), f32[8,512,256]{2,1,0:T(8,128)}, u32[]{:S(2)}, u32[]{:S(2)}) %all-to-all-start) | async-done | bytes 4194336 | tf_op jit(solution)/shard_map/all_to_all | solution.py:318
  118.1 4.4 %all-to-all-start.1 = ((f32[8,256,256]{2,1,0:T(8,128)}), f32[8,256,256]{2,1,0:T(8,128)}, u32[]{:S(2)}, u32[]{:S(2)}) async-start(f32[8,256,256]{2,1,0:T(8,128)} %bitcast.29), calls=%async_computation.1 | async-start | bytes 4194304 | tf_op jit(solution)/shard_map/all_to_all | solution.py:318
  122.5 8.5 %turn.4 = (f32[264,256]{1,0:T(8,128)}, f32[264,256]{1,0:T(8,128)}, f32[264,256]{1,0:T(8,128)}, f32[264,256]{1,0:T(8,128)}, f32[8,128]{1,0:T(8,128)}) custom-call(f32[8,512,256]{2,1,0:T(8,128)} %all-to-all-done.x_ref, bf16[4,2048,256]{2,1,0:T(8,128)(2,1)} %copy-done.3, bf16[4,2048,256]{2,1,0:T(8,128)(2,1)} %copy-done.4, f32[4,8,256]{2,1,0:T(8,128)} %copy-done.8), custom_call_target="tpu_custom_call" | custom-call | flops 3221225472 | bytes 12582912 | tf_op jit(solution)/shard_map/turn/pallas_call | solution.py:180
  131.0 1.9 collective-permute-start.12
  134.5 8.4 %turn.3 = (f32[264,256]{1,0:T(8,128)}, f32[264,256]{1,0:T(8,128)}, f32[264,256]{1,0:T(8,128)}, f32[264,256]{1,0:T(8,128)}, f32[8,128]{1,0:T(8,128)}) custom-call(f32[8,512,256]{2,1,0:T(8,128)} %all-to-all-done.x_ref, bf16[4,2048,256]{2,1,0:T(8,128)(2,1)} %copy-done.3, bf16[4,2048,256]{2,1,0:T(8,128)(2,1)} %copy-done.4, f32[4,8,256]{2,1,0:T(8,128)} %copy-done.8), custom_call_target="tpu_custom_call" | custom-call | flops 3221225472 | bytes 12582912 | tf_op jit(solution)/shard_map/turn/pallas_call | solution.py:180
  143.0 1.9 collective-permute-start.9
  147.2 3.5 %collective-permute-start.11 = (f32[264,256]{1,0:T(8,128)}, f32[264,256]{1,0:T(8,128)S(1)}, u32[]{:S(2)}, u32[]{:S(2)}) collective-permute-start(f32[264,256]{1,0:T(8,128)} %get-tuple-element.30), channel_id=1, source_target_pairs={{0,3},{1,2},{2,1},{3,0},{4,7},{5,6},{6,5},{7,4},{8,11},{9,10},{10,... | collective-permute-start | bytes 811016 | tf_op jit(solution)/shard_map/ppermute | solution.py:17
  150.7 12.7 %collective-permute-done.13 = f32[264,256]{1,0:T(8,128)S(1)} collective-permute-done((f32[264,256]{1,0:T(8,128)}, f32[264,256]{1,0:T(8,128)S(1)}, u32[]{:S(2)}, u32[]{:S(2)}) %collective-permute-start.13) | collective-permute-done | bytes 270368 | tf_op jit(solution)/shard_map/ppermute | solution.py:17
  163.4 8.0 %collective-permute-done.14 = f32[264,256]{1,0:T(8,128)S(1)} collective-permute-done((f32[264,256]{1,0:T(8,128)}, f32[264,256]{1,0:T(8,128)S(1)}, u32[]{:S(2)}, u32[]{:S(2)}) %collective-permute-start.14) | collective-permute-done | bytes 270368 | tf_op jit(solution)/shard_map/ppermute | solution.py:17
  173.3 4.0 %collective-permute-done.10 = f32[264,256]{1,0:T(8,128)S(1)} collective-permute-done((f32[264,256]{1,0:T(8,128)}, f32[264,256]{1,0:T(8,128)S(1)}, u32[]{:S(2)}, u32[]{:S(2)}) %collective-permute-start.10) | collective-permute-done | bytes 270368 | tf_op jit(solution)/shard_map/ppermute | solution.py:17
  177.3 3.9 %collective-permute-done.11 = f32[264,256]{1,0:T(8,128)S(1)} collective-permute-done((f32[264,256]{1,0:T(8,128)}, f32[264,256]{1,0:T(8,128)S(1)}, u32[]{:S(2)}, u32[]{:S(2)}) %collective-permute-start.11) | collective-permute-done | bytes 270368 | tf_op jit(solution)/shard_map/ppermute | solution.py:17
  182.3 8.4 %turn.5 = (f32[264,256]{1,0:T(8,128)}, f32[264,256]{1,0:T(8,128)}, f32[264,256]{1,0:T(8,128)}, f32[264,256]{1,0:T(8,128)}, f32[8,128]{1,0:T(8,128)}) custom-call(f32[8,256,256]{2,1,0:T(8,128)} %all-to-all-done.1.x_ref, bf16[4,2048,256]{2,1,0:T(8,128)(2,1)} %copy-done.3, bf16[4,2048,256]{2,1,0:T(8,128)(2,1)} %copy-done.4, f32[4,8,256]{2,1,0:T(8,128)} %copy-done.8), custom_call_target="tpu_custom_call" | custom-call | flops 3221225472 | bytes 12582912 | tf_op jit(solution)/shard_map/turn/pallas_call | solution.py:180
  191.8 2.5 %collective-permute-start.17 = (f32[264,256]{1,0:T(8,128)}, f32[264,256]{1,0:T(8,128)}, u32[]{:S(2)}, u32[]{:S(2)}) collective-permute-start(f32[264,256]{1,0:T(8,128)} %get-tuple-element.39), channel_id=1, source_target_pairs={{0,3},{1,2},{2,1},{3,0},{4,7},{5,6},{6,5},{7,4},{8,11},{9,10},{10,... | collective-permute-start | bytes 811016 | tf_op jit(solution)/shard_map/ppermute | solution.py:17
  195.0 4.9 %collective-permute-done.15 = f32[264,256]{1,0:T(8,128)S(1)} collective-permute-done((f32[264,256]{1,0:T(8,128)}, f32[264,256]{1,0:T(8,128)S(1)}, u32[]{:S(2)}, u32[]{:S(2)}) %collective-permute-start.15) | collective-permute-done | bytes 270368 | tf_op jit(solution)/shard_map/ppermute | solution.py:17
  199.9 2.4 %collective-permute-start.19 = (f32[4,8,128]{2,1,0:T(8,128)S(1)}, f32[4,8,128]{2,1,0:T(8,128)S(1)}, u32[]{:S(2)}, u32[]{:S(2)}) collective-permute-start(f32[4,8,128]{2,1,0:T(8,128)S(1)} %slice.13), channel_id=1, source_target_pairs={{0,4},{1,5},{2,6},{3,7},{4,0},{5,1},{6,2},{7,3},{8,12},{9,13},{10,... | collective-permute-start | bytes 49160 | tf_op jit(solution)/shard_map/ppermute | solution.py:17
  203.4 4.2 %collective-permute-done.17 = f32[264,256]{1,0:T(8,128)} collective-permute-done((f32[264,256]{1,0:T(8,128)}, f32[264,256]{1,0:T(8,128)}, u32[]{:S(2)}, u32[]{:S(2)}) %collective-permute-start.17) | collective-permute-done | bytes 270368 | tf_op jit(solution)/shard_map/ppermute | solution.py:17
  208.9 2.2 collective-permute-start.20
  214.2 6.8 %finish.1 = (f32[3072,256]{1,0:T(8,128)}, f32[24,128]{1,0:T(8,128)}, f32[3072,256]{1,0:T(8,128)}, f32[1,256]{1,0:T(1,128)}) custom-call(s32[4]{0:T(128)} %pad_add_fusion.place, f32[4,264,256]{2,1,0:T(8,128)} %pad_maximum_fusion.refs_0_, f32[4,264,256]{2,1,0:T(8,128)} %copy-done.9, f32[4,264,256]{2,1,0:T(8,128)} %copy-done.10, f32[4,8,128]{2,1,0:T(8,128)} %copy-done.15, ...), custom_call_target="tpu_custom_call" | custom-call | tf_op jit(solution)/shard_map/finish/pallas_call | solution.py:252
  221.0 6.3 %psum.7 = f32[256]{0:T(256)} all-reduce(f32[256]{0:T(256)} %bitcast.41), channel_id=1, replica_groups=mesh['dom'=4,'orb'=8] {'dom'}, use_global_device_ids=true, to_apply=%region_0.1 | all-reduce | flops 256 | bytes 2048 | tf_op jit(solution)/shard_map/psum | solution.py:337
  (74 shorter events, 25.1 us)
Async XLA Ops:
  2.4 15.2 %collective-permute-start.3 = (f32[520,256]{1,0:T(8,128)S(1)}, f32[520,256]{1,0:T(8,128)}, u32[]{:S(2)}, u32[]{:S(2)}) collective-permute-start(f32[520,256]{1,0:T(8,128)S(1)} %get-tuple-element.44), channel_id=1, source_target_pairs={{0,1},{1,0},{2,3},{3,2},{4,5},{5,4},{6,7},{7,6},{8,9},{9,8},{10,11... | collective-permute-start | bytes 1597448 | tf_op jit(solution)/shard_map/ppermute | solution.py:17
  5.4 15.1 %collective-permute-start.4 = (f32[520,256]{1,0:T(8,128)S(1)}, f32[520,256]{1,0:T(8,128)}, u32[]{:S(2)}, u32[]{:S(2)}) collective-permute-start(f32[520,256]{1,0:T(8,128)S(1)} %get-tuple-element.44), channel_id=1, source_target_pairs={{0,2},{1,3},{2,0},{3,1},{4,6},{5,7},{6,4},{7,5},{8,10},{9,11},{10,... | collective-permute-start | bytes 1597448 | tf_op jit(solution)/shard_map/ppermute | solution.py:17
  6.9 34.7 %collective-permute-start.5 = (f32[520,256]{1,0:T(8,128)S(1)}, f32[520,256]{1,0:T(8,128)}, u32[]{:S(2)}, u32[]{:S(2)}) collective-permute-start(f32[520,256]{1,0:T(8,128)S(1)} %get-tuple-element.44), channel_id=1, source_target_pairs={{0,3},{1,2},{2,1},{3,0},{4,7},{5,6},{6,5},{7,4},{8,11},{9,10},{10,... | collective-permute-start | bytes 1597448 | tf_op jit(solution)/shard_map/ppermute | solution.py:17
  11.4 106.8 %all-to-all-start = ((f32[8,512,256]{2,1,0:T(8,128)}), f32[8,512,256]{2,1,0:T(8,128)}, u32[]{:S(2)}, u32[]{:S(2)}) async-start(f32[8,512,256]{2,1,0:T(8,128)} %bitcast.28), calls=%async_computation | async-start | bytes 8388608 | tf_op jit(solution)/shard_map/all_to_all | solution.py:318
  44.7 35.0 %collective-permute-start.6 = (f32[3,520,256]{2,1,0:T(8,128)}, f32[3,520,256]{2,1,0:T(8,128)}, u32[]{:S(2)}, u32[]{:S(2)}) collective-permute-start(f32[3,520,256]{2,1,0:T(8,128)} %collect.1.refs_4_), channel_id=1, source_target_pairs={{0,16},{8,24},{16,0},{24,8},{1,17},{9,25},{17,1},{25,9},{2,18},{10... | collective-permute-start | bytes 4792328 | tf_op jit(solution)/shard_map/ppermute | solution.py:17
  46.7 51.1 %collective-permute-start.7 = (f32[3,520,256]{2,1,0:T(8,128)}, f32[3,520,256]{2,1,0:T(8,128)}, u32[]{:S(2)}, u32[]{:S(2)}) collective-permute-start(f32[3,520,256]{2,1,0:T(8,128)} %collect.1.refs_4_), channel_id=1, source_target_pairs={{0,8},{8,0},{16,24},{24,16},{1,9},{9,1},{17,25},{25,17},{2,10},{10... | collective-permute-start | bytes 4792328 | tf_op jit(solution)/shard_map/ppermute | solution.py:17
  79.7 18.2 %collective-permute-start.8 = (f32[3,520,256]{2,1,0:T(8,128)}, f32[3,520,256]{2,1,0:T(8,128)}, u32[]{:S(2)}, u32[]{:S(2)}) collective-permute-start(f32[3,520,256]{2,1,0:T(8,128)} %collective-permute-done.6.refs_5_), channel_id=1, source_target_pairs={{0,8},{8,0},{16,24},{24,16},{1,9},{9,1},{17,25},{25,17},{2,10},{10... | collective-permute-start | bytes 4792328 | tf_op jit(solution)/shard_map/ppermute | solution.py:17
  79.7 14.5 %collective-permute-start = (f32[1,520,256]{2,1,0:T(8,128)S(1)}, f32[1,520,256]{2,1,0:T(8,128)S(1)}, u32[]{:S(2)}, u32[]{:S(2)}) collective-permute-start(f32[1,520,256]{2,1,0:T(8,128)S(1)} %get-tuple-element.45.refs_0_), channel_id=1, source_target_pairs={{0,16},{8,24},{16,0},{24,8},{1,17},{9,25},{17,1},{25,9},{2,18},{10... | collective-permute-start | bytes 1597448 | tf_op jit(solution)/shard_map/ppermute | solution.py:17
  81.0 16.8 %collective-permute-start.1 = (f32[1,520,256]{2,1,0:T(8,128)S(1)}, f32[1,520,256]{2,1,0:T(8,128)}, u32[]{:S(2)}, u32[]{:S(2)}) collective-permute-start(f32[1,520,256]{2,1,0:T(8,128)S(1)} %get-tuple-element.45.refs_0_), channel_id=1, source_target_pairs={{0,8},{8,0},{16,24},{24,16},{1,9},{9,1},{17,25},{25,17},{2,10},{10... | collective-permute-start | bytes 1597448 | tf_op jit(solution)/shard_map/ppermute | solution.py:17
  94.2 3.6 %collective-permute-start.2 = (f32[1,520,256]{2,1,0:T(8,128)S(1)}, f32[1,520,256]{2,1,0:T(8,128)}, u32[]{:S(2)}, u32[]{:S(2)}) collective-permute-start(f32[1,520,256]{2,1,0:T(8,128)S(1)} %collective-permute-done.refs_1_), channel_id=1, source_target_pairs={{0,8},{8,0},{16,24},{24,16},{1,9},{9,1},{17,25},{25,17},{2,10},{10... | collective-permute-start | bytes 1597448 | tf_op jit(solution)/shard_map/ppermute | solution.py:17
  104.3 2.0 copy-start.3
  106.3 2.1 copy-start.4
  118.1 64.2 %all-to-all-start.1 = ((f32[8,256,256]{2,1,0:T(8,128)}), f32[8,256,256]{2,1,0:T(8,128)}, u32[]{:S(2)}, u32[]{:S(2)}) async-start(f32[8,256,256]{2,1,0:T(8,128)} %bitcast.29), calls=%async_computation.1 | async-start | bytes 4194304 | tf_op jit(solution)/shard_map/all_to_all | solution.py:318
  131.0 16.2 %collective-permute-start.12 = (f32[264,256]{1,0:T(8,128)}, f32[264,256]{1,0:T(8,128)S(1)}, u32[]{:S(2)}, u32[]{:S(2)}) collective-permute-start(f32[264,256]{1,0:T(8,128)} %get-tuple-element.32), channel_id=1, source_target_pairs={{0,1},{1,0},{2,3},{3,2},{4,5},{5,4},{6,7},{7,6},{8,9},{9,8},{10,11... | collective-permute-start | bytes 811016 | tf_op jit(solution)/shard_map/ppermute | solution.py:17
  132.9 30.5 %collective-permute-start.13 = (f32[264,256]{1,0:T(8,128)}, f32[264,256]{1,0:T(8,128)S(1)}, u32[]{:S(2)}, u32[]{:S(2)}) collective-permute-start(f32[264,256]{1,0:T(8,128)} %get-tuple-element.33), channel_id=1, source_target_pairs={{0,2},{1,3},{2,0},{3,1},{4,6},{5,7},{6,4},{7,5},{8,10},{9,11},{10,... | collective-permute-start | bytes 811016 | tf_op jit(solution)/shard_map/ppermute | solution.py:17
  134.4 37.7 %copy-start.12 = (f32[264,256]{1,0:T(8,128)S(1)}, f32[264,256]{1,0:T(8,128)}, u32[]{:S(2)}) copy-start(f32[264,256]{1,0:T(8,128)} %get-tuple-element.31) | copy-start | bytes 811012
  134.4 37.0 %collective-permute-start.14 = (f32[264,256]{1,0:T(8,128)}, f32[264,256]{1,0:T(8,128)S(1)}, u32[]{:S(2)}, u32[]{:S(2)}) collective-permute-start(f32[264,256]{1,0:T(8,128)} %get-tuple-element.34), channel_id=1, source_target_pairs={{0,3},{1,2},{2,1},{3,0},{4,7},{5,6},{6,5},{7,4},{8,11},{9,10},{10,... | collective-permute-start | bytes 811016 | tf_op jit(solution)/shard_map/ppermute | solution.py:17
  143.0 30.3 %collective-permute-start.9 = (f32[264,256]{1,0:T(8,128)}, f32[264,256]{1,0:T(8,128)S(1)}, u32[]{:S(2)}, u32[]{:S(2)}) collective-permute-start(f32[264,256]{1,0:T(8,128)} %get-tuple-element.28), channel_id=1, source_target_pairs={{0,1},{1,0},{2,3},{3,2},{4,5},{5,4},{6,7},{7,6},{8,9},{9,8},{10,11... | collective-permute-start | bytes 811016 | tf_op jit(solution)/shard_map/ppermute | solution.py:17
  144.9 32.4 %collective-permute-start.10 = (f32[264,256]{1,0:T(8,128)}, f32[264,256]{1,0:T(8,128)S(1)}, u32[]{:S(2)}, u32[]{:S(2)}) collective-permute-start(f32[264,256]{1,0:T(8,128)} %get-tuple-element.29), channel_id=1, source_target_pairs={{0,2},{1,3},{2,0},{3,1},{4,6},{5,7},{6,4},{7,5},{8,10},{9,11},{10,... | collective-permute-start | bytes 811016 | tf_op jit(solution)/shard_map/ppermute | solution.py:17
  147.2 34.1 %collective-permute-start.11 = (f32[264,256]{1,0:T(8,128)}, f32[264,256]{1,0:T(8,128)S(1)}, u32[]{:S(2)}, u32[]{:S(2)}) collective-permute-start(f32[264,256]{1,0:T(8,128)} %get-tuple-element.30), channel_id=1, source_target_pairs={{0,3},{1,2},{2,1},{3,0},{4,7},{5,6},{6,5},{7,4},{8,11},{9,10},{10,... | collective-permute-start | bytes 811016 | tf_op jit(solution)/shard_map/ppermute | solution.py:17
  172.1 9.1 %copy-start.11 = (f32[264,256]{1,0:T(8,128)S(1)}, f32[264,256]{1,0:T(8,128)}, u32[]{:S(2)}) copy-start(f32[264,256]{1,0:T(8,128)} %get-tuple-element.27) | copy-start | bytes 811012
  173.2 21.1 %copy-start.9 = (f32[4,264,256]{2,1,0:T(8,128)}, f32[4,264,256]{2,1,0:T(8,128)S(1)}, u32[]{:S(2)}) copy-start(f32[4,264,256]{2,1,0:T(8,128)S(1)} %pad_maximum_fusion.1.refs_1_) | copy-start | bytes 3244036
  173.2 38.5 %collective-permute-start.21 = (f32[4,264,256]{2,1,0:T(8,128)S(1)}, f32[4,264,256]{2,1,0:T(8,128)}, u32[]{:S(2)}, u32[]{:S(2)}) collective-permute-start(f32[4,264,256]{2,1,0:T(8,128)S(1)} %pad_maximum_fusion.1.refs_1_), channel_id=1, source_target_pairs={{0,8},{8,16},{16,24},{24,0},{1,9},{9,17},{17,25},{25,1},{2,10},{10... | collective-permute-start | bytes 3244040 | tf_op jit(solution)/shard_map/ppermute | solution.py:17
  182.3 29.4 %collective-permute-start.22 = (f32[4,264,256]{2,1,0:T(8,128)}, f32[4,264,256]{2,1,0:T(8,128)}, u32[]{:S(2)}, u32[]{:S(2)}) collective-permute-start(f32[4,264,256]{2,1,0:T(8,128)} %pad_maximum_fusion.refs_0_), channel_id=1, source_target_pairs={{0,24},{8,0},{16,8},{24,16},{1,25},{9,1},{17,9},{25,17},{2,26},{10... | collective-permute-start | bytes 3244040 | tf_op jit(solution)/shard_map/ppermute | solution.py:17
  190.7 9.2 %collective-permute-start.15 = (f32[264,256]{1,0:T(8,128)}, f32[264,256]{1,0:T(8,128)S(1)}, u32[]{:S(2)}, u32[]{:S(2)}) collective-permute-start(f32[264,256]{1,0:T(8,128)} %get-tuple-element.37), channel_id=1, source_target_pairs={{0,1},{1,0},{2,3},{3,2},{4,5},{5,4},{6,7},{7,6},{8,9},{9,8},{10,11... | collective-permute-start | bytes 811016 | tf_op jit(solution)/shard_map/ppermute | solution.py:17
  191.4 10.9 %collective-permute-start.16 = (f32[264,256]{1,0:T(8,128)}, f32[264,256]{1,0:T(8,128)}, u32[]{:S(2)}, u32[]{:S(2)}) collective-permute-start(f32[264,256]{1,0:T(8,128)} %get-tuple-element.38), channel_id=1, source_target_pairs={{0,2},{1,3},{2,0},{3,1},{4,6},{5,7},{6,4},{7,5},{8,10},{9,11},{10,... | collective-permute-start | bytes 811016 | tf_op jit(solution)/shard_map/ppermute | solution.py:17
  191.8 15.9 %collective-permute-start.17 = (f32[264,256]{1,0:T(8,128)}, f32[264,256]{1,0:T(8,128)}, u32[]{:S(2)}, u32[]{:S(2)}) collective-permute-start(f32[264,256]{1,0:T(8,128)} %get-tuple-element.39), channel_id=1, source_target_pairs={{0,3},{1,2},{2,1},{3,0},{4,7},{5,6},{6,5},{7,4},{8,11},{9,10},{10,... | collective-permute-start | bytes 811016 | tf_op jit(solution)/shard_map/ppermute | solution.py:17
  199.9 11.8 %collective-permute-start.19 = (f32[4,8,128]{2,1,0:T(8,128)S(1)}, f32[4,8,128]{2,1,0:T(8,128)S(1)}, u32[]{:S(2)}, u32[]{:S(2)}) collective-permute-start(f32[4,8,128]{2,1,0:T(8,128)S(1)} %slice.13), channel_id=1, source_target_pairs={{0,4},{1,5},{2,6},{3,7},{4,0},{5,1},{6,2},{7,3},{8,12},{9,13},{10,... | collective-permute-start | bytes 49160 | tf_op jit(solution)/shard_map/ppermute | solution.py:17
  202.3 9.4 %collective-permute-start.18 = (f32[4,8,128]{2,1,0:T(8,128)S(1)}, f32[4,8,128]{2,1,0:T(8,128)S(1)}, u32[]{:S(2)}, u32[]{:S(2)}) collective-permute-start(f32[4,8,128]{2,1,0:T(8,128)S(1)} %slice.12), channel_id=1, source_target_pairs={{0,4},{1,5},{2,6},{3,7},{4,0},{5,1},{6,2},{7,3},{8,12},{9,13},{10,... | collective-permute-start | bytes 49160 | tf_op jit(solution)/shard_map/ppermute | solution.py:17
  208.9 2.8 %copy-start.10 = (f32[4,264,256]{2,1,0:T(8,128)}, f32[4,264,256]{2,1,0:T(8,128)S(1)}, u32[]{:S(2)}) copy-start(f32[4,264,256]{2,1,0:T(8,128)S(1)} %pad_maximum_fusion.2.refs_2_) | copy-start | bytes 3244036
  208.9 4.7 %collective-permute-start.20 = (f32[4,8,128]{2,1,0:T(8,128)S(1)}, f32[4,8,128]{2,1,0:T(8,128)S(1)}, u32[]{:S(2)}, u32[]{:S(2)}) collective-permute-start(f32[4,8,128]{2,1,0:T(8,128)S(1)} %slice.14), channel_id=1, source_target_pairs={{0,4},{1,5},{2,6},{3,7},{4,0},{5,1},{6,2},{7,3},{8,12},{9,13},{10,... | collective-permute-start | bytes 49160 | tf_op jit(solution)/shard_map/ppermute | solution.py:17
  211.7 1.9 copy-start.14
  (11 other events, 15.5 us)

commit v5 on v4

--- a/solution.py
+++ b/solution.py
@@ -309,7 +309,7 @@
     lines = NY // group
     lots = [[(0, 0, lines), (planes - 1, 0, lines)], [(p, 0, lines) for p in range(1, planes - 1)]]
     where = [[None] * lines for _ in range(planes)]
-    near, far, edges = [], [], []
+    near, far = [], []
     gate = []
     for lot in lots:
         height = sum(count for _, _, count in lot) * NZ
@@ -324,12 +324,17 @@
             at += count * NZ
             if not near:
                 gate = [rows, high]
-            near.append(jnp.stack([outs[0]] + [swap(outs[s], s) for s in range(1, group)]))
+            back = [outs[0]] + [swap(outs[s], s) for s in range(1, group)]
+            if not near:
+                waiting, near, far = back, [None], [None]
+                continue
+            near.append(jnp.stack(back))
             far.append(swap(near[-1][:, -EXTRA:, :NZ], group))
-            if p == 0:
-                edges.append(send(near[-1], "dom", doms, lambda a: (a - 1) % doms))
             if p == planes - 1:
-                edges.insert(0, send(near[-1], "dom", doms, lambda a: (a + 1) % doms))
+                before = send(near[-1], "dom", doms, lambda a: (a + 1) % doms)
+    near[0] = jnp.stack([waiting[0]] + [after(block, [outs[0]]) for block in waiting[1:]])
+    far[0] = swap(near[0][:, -EXTRA:, :NZ], group)
+    edges = [before, send(near[0], "dom", doms, lambda a: (a - 1) % doms)]
 
     rotated, density, hpsi, band = finish(
         near, far, where, *edges, v_loc, shares, 1.0 / (points * doms)

time: 228 us -> 223 us (0.978)
  waiting for transfers between devices: 120 us -> 109 us
  starting transfers between devices: 38.6 us -> 42.4 us
    ppermute x23, waiting for transfers between devices: 110 us -> 99.5 us  [send(): return lax.ppermute(block, axis, [(a, step(a)) for a in range(size)])]
    ppermute x23, starting transfers between devices: 28 us -> 31.8 us  [send(): return lax.ppermute(block, axis, [(a, step(a)) for a in range(size)])]
    unnamed x36 -> x40, local copies, waits for them, and re-layouts: 16 us -> 16.6 us
  transfers between devices with their start and end apart: 25 -> 25, of which waited for: 13 -> 11; matrix products, arithmetic and copies ran while one was open for 2% -> 3% of each run, Pallas kernels for 15% -> 16%
where the time goes in v5:
time: 223 us
  waiting for transfers between devices  109 us (49%)
  starting transfers between devices  42.4 us (19%)
  Pallas kernels  41.4 us (19%)
  local copies, waits for them, and re-layouts  17.4 us (8%)
  blocking collectives  6.35 us (3%)
  other arithmetic  5.4 us (2%)
    ppermute x23, waiting for transfers between devices, send(): return lax.ppermute(block, axis, [(a, step(a)) for a in range(size)])  99.5 us
    ppermute x23, starting transfers between devices, send(): return lax.ppermute(block, axis, [(a, step(a)) for a in range(size)])  31.8 us
    pallas_call x3, Pallas kernels, turn(): pl.pallas_call(body, grid=(group,), in_specs=[pl.BlockSpec((count, rows,...  25.7 us
    unnamed x40, local copies, waits for them, and re-layouts  16.6 us
    all_to_all x2, starting transfers between devices, shards(): lax.all_to_all(rows, 'orb', split_axis=0, concat_axis=0, tiled=True)  10.6 us
    all_to_all x2, waiting for transfers between devices, shards(): lax.all_to_all(rows, 'orb', split_axis=0, concat_axis=0, tiled=True)  9.17 us
    pallas_call x1, Pallas kernels, finish(): pl.pallas_call(body, grid_spec=pltpu.PrefetchScalarGridSpec(num_scalar_pr...  6.71 us
    psum x1, blocking collectives, shards(): lax.psum(band.reshape(cols), 'dom')  6.35 us
  transfers between devices with their start and end apart: 25, of which 11 were waited for; matrix products, arithmetic and copies ran while one was open for 3% of the time, Pallas kernels for 16%

profile of v5, /device:TPU:0, one launch (start us, length us, event | category | flops | bytes accessed | tf_op | source)
XLA Modules:
  0.0 222.6 jit_solution(2842439308001471199)
XLA Ops:
  2.4 3.0 %collective-permute-start.3 = (f32[520,256]{1,0:T(8,128)S(1)}, f32[520,256]{1,0:T(8,128)}, u32[]{:S(2)}, u32[]{:S(2)}) collective-permute-start(f32[520,256]{1,0:T(8,128)S(1)} %get-tuple-element.50), channel_id=1, source_target_pairs={{0,1},{1,0},{2,3},{3,2},{4,5},{5,4},{6,7},{7,6},{8,9},{9,8},{10,11... | collective-permute-start | bytes 1597448 | tf_op jit(solution)/shard_map/ppermute | solution.py:17
  7.0 1.9 copy-done.1
  9.5 1.9 copy-done.5
  11.4 6.2 %all-to-all-start = ((f32[8,512,256]{2,1,0:T(8,128)}), f32[8,512,256]{2,1,0:T(8,128)}, u32[]{:S(2)}, u32[]{:S(2)}) async-start(f32[8,512,256]{2,1,0:T(8,128)} %bitcast.28), calls=%async_computation | async-start | bytes 8388608 | tf_op jit(solution)/shard_map/all_to_all | solution.py:318
  17.6 2.9 %collective-permute-done.4.refs_1_ = f32[520,256]{1,0:T(8,128)} collective-permute-done((f32[520,256]{1,0:T(8,128)S(1)}, f32[520,256]{1,0:T(8,128)}, u32[]{:S(2)}, u32[]{:S(2)}) %collective-permute-start.4) | collective-permute-done | bytes 532512 | tf_op jit(solution)/shard_map/ppermute | solution.py:17
  20.5 21.2 %collective-permute-done.5.refs_2_ = f32[520,256]{1,0:T(8,128)} collective-permute-done((f32[520,256]{1,0:T(8,128)S(1)}, f32[520,256]{1,0:T(8,128)}, u32[]{:S(2)}, u32[]{:S(2)}) %collective-permute-start.5) | collective-permute-done | bytes 532512 | tf_op jit(solution)/shard_map/ppermute | solution.py:17
  41.7 3.0 %collect.1.refs_4_ = f32[3,520,256]{2,1,0:T(8,128)} custom-call(f32[520,256]{1,0:T(8,128)} %collective-permute-done.3.refs_0_, f32[520,256]{1,0:T(8,128)} %collective-permute-done.4.refs_1_, f32[520,256]{1,0:T(8,128)} %collective-permute-done.5.refs_2_), custom_call_target="tpu_custom_call" | custom-call | flops 40000000000 | bytes 3194880 | tf_op jit(solution)/shard_map/collect/pallas_call | solution.py:66
  44.7 2.0 collective-permute-start.6
  46.7 32.9 %collective-permute-done.6.refs_5_ = f32[3,520,256]{2,1,0:T(8,128)} collective-permute-done((f32[3,520,256]{2,1,0:T(8,128)}, f32[3,520,256]{2,1,0:T(8,128)}, u32[]{:S(2)}, u32[]{:S(2)}) %collective-permute-start.6) | collective-permute-done | bytes 1597472 | tf_op jit(solution)/shard_map/ppermute | solution.py:17
  81.3 12.9 %collective-permute-done.refs_1_ = f32[1,520,256]{2,1,0:T(8,128)S(1)} collective-permute-done((f32[1,520,256]{2,1,0:T(8,128)S(1)}, f32[1,520,256]{2,1,0:T(8,128)S(1)}, u32[]{:S(2)}, u32[]{:S(2)}) %collective-permute-start) | collective-permute-done | bytes 532512 | tf_op jit(solution)/shard_map/ppermute | solution.py:17
  94.2 1.9 copy-done.2
  99.3 5.0 %split_rot.1 = (bf16[4,2048,256]{2,1,0:T(8,128)(2,1)S(1)}, bf16[4,2048,256]{2,1,0:T(8,128)(2,1)S(1)}, f32[4,8,256]{2,1,0:T(8,128)S(1)}) custom-call(s32[4]{0:T(128)S(1)} %pad_add_fusion.1.place, f32[1,520,256]{2,1,0:T(8,128)S(1)} %get-tuple-element.51.refs_0_, f32[1,520,256]{2,1,0:T(8,128)S(1)} %collective-permute-done.refs_1_, ...), custom_call_target="tpu_custom_call" | custom-call | tf_op jit(solution)/shard_map/split_rot/pallas_call | solution.py:105
  104.3 2.0 copy-done.3
  106.3 2.1 copy-done.4
  109.0 9.2 %all-to-all-done.x_ref = f32[8,512,256]{2,1,0:T(8,128)} async-done(((f32[8,512,256]{2,1,0:T(8,128)}), f32[8,512,256]{2,1,0:T(8,128)}, u32[]{:S(2)}, u32[]{:S(2)}) %all-to-all-start) | async-done | bytes 4194336 | tf_op jit(solution)/shard_map/all_to_all | solution.py:318
  118.1 4.4 %all-to-all-start.1 = ((f32[8,256,256]{2,1,0:T(8,128)}), f32[8,256,256]{2,1,0:T(8,128)}, u32[]{:S(2)}, u32[]{:S(2)}) async-start(f32[8,256,256]{2,1,0:T(8,128)} %bitcast.29), calls=%async_computation.1 | async-start | bytes 4194304 | tf_op jit(solution)/shard_map/all_to_all | solution.py:318
  122.5 8.5 %turn.5 = (f32[264,256]{1,0:T(8,128)}, f32[264,256]{1,0:T(8,128)}, f32[264,256]{1,0:T(8,128)}, f32[264,256]{1,0:T(8,128)}, f32[8,128]{1,0:T(8,128)}) custom-call(f32[8,512,256]{2,1,0:T(8,128)} %all-to-all-done.x_ref, bf16[4,2048,256]{2,1,0:T(8,128)(2,1)} %copy-done.3, bf16[4,2048,256]{2,1,0:T(8,128)(2,1)} %copy-done.4, f32[4,8,256]{2,1,0:T(8,128)} %copy-done.8), custom_call_target="tpu_custom_call" | custom-call | flops 3221225472 | bytes 12582912 | tf_op jit(solution)/shard_map/turn/pallas_call | solution.py:180
  131.0 1.9 collective-permute-start.12
  134.5 8.4 %turn.3 = (f32[264,256]{1,0:T(8,128)}, f32[264,256]{1,0:T(8,128)}, f32[264,256]{1,0:T(8,128)}, f32[264,256]{1,0:T(8,128)}, f32[8,128]{1,0:T(8,128)}) custom-call(f32[8,512,256]{2,1,0:T(8,128)} %all-to-all-done.x_ref, bf16[4,2048,256]{2,1,0:T(8,128)(2,1)} %copy-done.3, bf16[4,2048,256]{2,1,0:T(8,128)(2,1)} %copy-done.4, f32[4,8,256]{2,1,0:T(8,128)} %copy-done.8), custom_call_target="tpu_custom_call" | custom-call | flops 3221225472 | bytes 12582912 | tf_op jit(solution)/shard_map/turn/pallas_call | solution.py:180
  143.0 1.9 collective-permute-start.9
  147.1 3.5 %collective-permute-start.11 = (f32[264,256]{1,0:T(8,128)}, f32[264,256]{1,0:T(8,128)}, u32[]{:S(2)}, u32[]{:S(2)}) collective-permute-start(f32[264,256]{1,0:T(8,128)} %get-tuple-element.37), channel_id=1, source_target_pairs={{0,3},{1,2},{2,1},{3,0},{4,7},{5,6},{6,5},{7,4},{8,11},{9,10},{10,... | collective-permute-start | bytes 811016 | tf_op jit(solution)/shard_map/ppermute | solution.py:17
  150.7 12.7 %collective-permute-done.13 = f32[264,256]{1,0:T(8,128)S(1)} collective-permute-done((f32[264,256]{1,0:T(8,128)}, f32[264,256]{1,0:T(8,128)S(1)}, u32[]{:S(2)}, u32[]{:S(2)}) %collective-permute-start.13) | collective-permute-done | bytes 270368 | tf_op jit(solution)/shard_map/ppermute | solution.py:17
  163.4 8.0 %collective-permute-done.14 = f32[264,256]{1,0:T(8,128)S(1)} collective-permute-done((f32[264,256]{1,0:T(8,128)}, f32[264,256]{1,0:T(8,128)S(1)}, u32[]{:S(2)}, u32[]{:S(2)}) %collective-permute-start.14) | collective-permute-done | bytes 270368 | tf_op jit(solution)/shard_map/ppermute | solution.py:17
  173.3 8.8 %turn.4 = (f32[264,256]{1,0:T(8,128)}, f32[264,256]{1,0:T(8,128)}, f32[264,256]{1,0:T(8,128)}, f32[264,256]{1,0:T(8,128)}, f32[8,128]{1,0:T(8,128)}) custom-call(f32[8,256,256]{2,1,0:T(8,128)} %all-to-all-done.1.x_ref, bf16[4,2048,256]{2,1,0:T(8,128)(2,1)} %copy-done.3, bf16[4,2048,256]{2,1,0:T(8,128)(2,1)} %copy-done.4, f32[4,8,256]{2,1,0:T(8,128)} %copy-done.8), custom_call_target="tpu_custom_call" | custom-call | flops 3221225472 | bytes 12582912 | tf_op jit(solution)/shard_map/turn/pallas_call | solution.py:180
  182.8 2.3 %pad_maximum_fusion.refs_0_ = f32[4,264,256]{2,1,0:T(8,128)} fusion(f32[1,264,256]{2,1,0:T(8,128)} %bitcast.15, f32[1,264,256]{2,1,0:T(8,128)} %bitcast.14, f32[1,264,256]{2,1,0:T(8,128)} %bitcast.32, f32[1,264,256]{2,1,0:T(8,128)} %bitcast.31), kind=kLoop, calls=%fused_computation | loop fusion | flops 811008 | bytes 2162688 | tf_op jit(solution)/shard_map/stack | solution.py:335
  188.2 1.8 collective-permute-start.17
  190.8 4.6 %collective-permute-done.15 = f32[264,256]{1,0:T(8,128)} collective-permute-done((f32[264,256]{1,0:T(8,128)}, f32[264,256]{1,0:T(8,128)}, u32[]{:S(2)}, u32[]{:S(2)}) %collective-permute-start.15) | collective-permute-done | bytes 270368 | tf_op jit(solution)/shard_map/ppermute | solution.py:17
  195.4 3.4 %collective-permute-start.19 = (f32[4,8,128]{2,1,0:T(8,128)S(1)}, f32[4,8,128]{2,1,0:T(8,128)S(1)}, u32[]{:S(2)}, u32[]{:S(2)}) collective-permute-start(f32[4,8,128]{2,1,0:T(8,128)S(1)} %slice.13), channel_id=1, source_target_pairs={{0,4},{1,5},{2,6},{3,7},{4,0},{5,1},{6,2},{7,3},{8,12},{9,13},{10,... | collective-permute-start | bytes 49160 | tf_op jit(solution)/shard_map/ppermute | solution.py:17
  200.2 2.4 %collective-permute-done.17 = f32[264,256]{1,0:T(8,128)} collective-permute-done((f32[264,256]{1,0:T(8,128)}, f32[264,256]{1,0:T(8,128)}, u32[]{:S(2)}, u32[]{:S(2)}) %collective-permute-start.17) | collective-permute-done | bytes 270368 | tf_op jit(solution)/shard_map/ppermute | solution.py:17
  203.9 3.3 %collective-permute-start.20 = (f32[4,8,128]{2,1,0:T(8,128)S(1)}, f32[4,8,128]{2,1,0:T(8,128)S(1)}, u32[]{:S(2)}, u32[]{:S(2)}) collective-permute-start(f32[4,8,128]{2,1,0:T(8,128)S(1)} %slice.14), channel_id=1, source_target_pairs={{0,4},{1,5},{2,6},{3,7},{4,0},{5,1},{6,2},{7,3},{8,12},{9,13},{10,... | collective-permute-start | bytes 49160 | tf_op jit(solution)/shard_map/ppermute | solution.py:17
  209.5 6.7 %finish.1 = (f32[3072,256]{1,0:T(8,128)}, f32[24,128]{1,0:T(8,128)}, f32[3072,256]{1,0:T(8,128)}, f32[1,256]{1,0:T(1,128)}) custom-call(s32[4]{0:T(128)} %pad_add_fusion.place, f32[4,264,256]{2,1,0:T(8,128)} %pad_maximum_fusion.refs_0_, f32[4,264,256]{2,1,0:T(8,128)} %copy-done.9, f32[4,264,256]{2,1,0:T(8,128)} %copy-done.10, f32[4,8,128]{2,1,0:T(8,128)} %copy-done.17, ...), custom_call_target="tpu_custom_call" | custom-call | tf_op jit(solution)/shard_map/finish/pallas_call | solution.py:252
  216.2 6.3 %psum.7 = f32[256]{0:T(256)} all-reduce(f32[256]{0:T(256)} %bitcast.38), channel_id=1, replica_groups=mesh['dom'=4,'orb'=8] {'dom'}, use_global_device_ids=true, to_apply=%region_0.1 | all-reduce | flops 256 | bytes 2048 | tf_op jit(solution)/shard_map/psum | solution.py:342
  (78 shorter events, 24.4 us)
Async XLA Ops:
  2.4 15.2 %collective-permute-start.3 = (f32[520,256]{1,0:T(8,128)S(1)}, f32[520,256]{1,0:T(8,128)}, u32[]{:S(2)}, u32[]{:S(2)}) collective-permute-start(f32[520,256]{1,0:T(8,128)S(1)} %get-tuple-element.50), channel_id=1, source_target_pairs={{0,1},{1,0},{2,3},{3,2},{4,5},{5,4},{6,7},{7,6},{8,9},{9,8},{10,11... | collective-permute-start | bytes 1597448 | tf_op jit(solution)/shard_map/ppermute | solution.py:17
  5.4 15.1 %collective-permute-start.4 = (f32[520,256]{1,0:T(8,128)S(1)}, f32[520,256]{1,0:T(8,128)}, u32[]{:S(2)}, u32[]{:S(2)}) collective-permute-start(f32[520,256]{1,0:T(8,128)S(1)} %get-tuple-element.50), channel_id=1, source_target_pairs={{0,2},{1,3},{2,0},{3,1},{4,6},{5,7},{6,4},{7,5},{8,10},{9,11},{10,... | collective-permute-start | bytes 1597448 | tf_op jit(solution)/shard_map/ppermute | solution.py:17
  6.9 34.7 %collective-permute-start.5 = (f32[520,256]{1,0:T(8,128)S(1)}, f32[520,256]{1,0:T(8,128)}, u32[]{:S(2)}, u32[]{:S(2)}) collective-permute-start(f32[520,256]{1,0:T(8,128)S(1)} %get-tuple-element.50), channel_id=1, source_target_pairs={{0,3},{1,2},{2,1},{3,0},{4,7},{5,6},{6,5},{7,4},{8,11},{9,10},{10,... | collective-permute-start | bytes 1597448 | tf_op jit(solution)/shard_map/ppermute | solution.py:17
  11.4 106.8 %all-to-all-start = ((f32[8,512,256]{2,1,0:T(8,128)}), f32[8,512,256]{2,1,0:T(8,128)}, u32[]{:S(2)}, u32[]{:S(2)}) async-start(f32[8,512,256]{2,1,0:T(8,128)} %bitcast.28), calls=%async_computation | async-start | bytes 8388608 | tf_op jit(solution)/shard_map/all_to_all | solution.py:318
  44.7 35.0 %collective-permute-start.6 = (f32[3,520,256]{2,1,0:T(8,128)}, f32[3,520,256]{2,1,0:T(8,128)}, u32[]{:S(2)}, u32[]{:S(2)}) collective-permute-start(f32[3,520,256]{2,1,0:T(8,128)} %collect.1.refs_4_), channel_id=1, source_target_pairs={{0,16},{8,24},{16,0},{24,8},{1,17},{9,25},{17,1},{25,9},{2,18},{10... | collective-permute-start | bytes 4792328 | tf_op jit(solution)/shard_map/ppermute | solution.py:17
  46.7 51.1 %collective-permute-start.7 = (f32[3,520,256]{2,1,0:T(8,128)}, f32[3,520,256]{2,1,0:T(8,128)}, u32[]{:S(2)}, u32[]{:S(2)}) collective-permute-start(f32[3,520,256]{2,1,0:T(8,128)} %collect.1.refs_4_), channel_id=1, source_target_pairs={{0,8},{8,0},{16,24},{24,16},{1,9},{9,1},{17,25},{25,17},{2,10},{10... | collective-permute-start | bytes 4792328 | tf_op jit(solution)/shard_map/ppermute | solution.py:17
  79.7 18.2 %collective-permute-start.8 = (f32[3,520,256]{2,1,0:T(8,128)}, f32[3,520,256]{2,1,0:T(8,128)}, u32[]{:S(2)}, u32[]{:S(2)}) collective-permute-start(f32[3,520,256]{2,1,0:T(8,128)} %collective-permute-done.6.refs_5_), channel_id=1, source_target_pairs={{0,8},{8,0},{16,24},{24,16},{1,9},{9,1},{17,25},{25,17},{2,10},{10... | collective-permute-start | bytes 4792328 | tf_op jit(solution)/shard_map/ppermute | solution.py:17
  79.7 14.5 %collective-permute-start = (f32[1,520,256]{2,1,0:T(8,128)S(1)}, f32[1,520,256]{2,1,0:T(8,128)S(1)}, u32[]{:S(2)}, u32[]{:S(2)}) collective-permute-start(f32[1,520,256]{2,1,0:T(8,128)S(1)} %get-tuple-element.51.refs_0_), channel_id=1, source_target_pairs={{0,16},{8,24},{16,0},{24,8},{1,17},{9,25},{17,1},{25,9},{2,18},{10... | collective-permute-start | bytes 1597448 | tf_op jit(solution)/shard_map/ppermute | solution.py:17
  81.1 16.8 %collective-permute-start.1 = (f32[1,520,256]{2,1,0:T(8,128)S(1)}, f32[1,520,256]{2,1,0:T(8,128)}, u32[]{:S(2)}, u32[]{:S(2)}) collective-permute-start(f32[1,520,256]{2,1,0:T(8,128)S(1)} %get-tuple-element.51.refs_0_), channel_id=1, source_target_pairs={{0,8},{8,0},{16,24},{24,16},{1,9},{9,1},{17,25},{25,17},{2,10},{10... | collective-permute-start | bytes 1597448 | tf_op jit(solution)/shard_map/ppermute | solution.py:17
  94.2 3.6 %collective-permute-start.2 = (f32[1,520,256]{2,1,0:T(8,128)S(1)}, f32[1,520,256]{2,1,0:T(8,128)}, u32[]{:S(2)}, u32[]{:S(2)}) collective-permute-start(f32[1,520,256]{2,1,0:T(8,128)S(1)} %collective-permute-done.refs_1_), channel_id=1, source_target_pairs={{0,8},{8,0},{16,24},{24,16},{1,9},{9,1},{17,25},{25,17},{2,10},{10... | collective-permute-start | bytes 1597448 | tf_op jit(solution)/shard_map/ppermute | solution.py:17
  104.3 2.0 copy-start.3
  106.3 2.1 copy-start.4
  118.1 55.2 %all-to-all-start.1 = ((f32[8,256,256]{2,1,0:T(8,128)}), f32[8,256,256]{2,1,0:T(8,128)}, u32[]{:S(2)}, u32[]{:S(2)}) async-start(f32[8,256,256]{2,1,0:T(8,128)} %bitcast.29), calls=%async_computation.1 | async-start | bytes 4194304 | tf_op jit(solution)/shard_map/all_to_all | solution.py:318
  131.0 16.2 %collective-permute-start.12 = (f32[264,256]{1,0:T(8,128)}, f32[264,256]{1,0:T(8,128)S(1)}, u32[]{:S(2)}, u32[]{:S(2)}) collective-permute-start(f32[264,256]{1,0:T(8,128)} %get-tuple-element.40), channel_id=1, source_target_pairs={{0,1},{1,0},{2,3},{3,2},{4,5},{5,4},{6,7},{7,6},{8,9},{9,8},{10,11... | collective-permute-start | bytes 811016 | tf_op jit(solution)/shard_map/ppermute | solution.py:17
  132.9 30.5 %collective-permute-start.13 = (f32[264,256]{1,0:T(8,128)}, f32[264,256]{1,0:T(8,128)S(1)}, u32[]{:S(2)}, u32[]{:S(2)}) collective-permute-start(f32[264,256]{1,0:T(8,128)} %get-tuple-element.41), channel_id=1, source_target_pairs={{0,2},{1,3},{2,0},{3,1},{4,6},{5,7},{6,4},{7,5},{8,10},{9,11},{10,... | collective-permute-start | bytes 811016 | tf_op jit(solution)/shard_map/ppermute | solution.py:17
  134.4 37.7 %copy-start.13 = (f32[264,256]{1,0:T(8,128)S(1)}, f32[264,256]{1,0:T(8,128)}, u32[]{:S(2)}) copy-start(f32[264,256]{1,0:T(8,128)} %get-tuple-element.39) | copy-start | bytes 811012
  134.4 37.0 %collective-permute-start.14 = (f32[264,256]{1,0:T(8,128)}, f32[264,256]{1,0:T(8,128)S(1)}, u32[]{:S(2)}, u32[]{:S(2)}) collective-permute-start(f32[264,256]{1,0:T(8,128)} %get-tuple-element.42), channel_id=1, source_target_pairs={{0,3},{1,2},{2,1},{3,0},{4,7},{5,6},{6,5},{7,4},{8,11},{9,10},{10,... | collective-permute-start | bytes 811016 | tf_op jit(solution)/shard_map/ppermute | solution.py:17
  143.0 39.1 %collective-permute-start.9 = (f32[264,256]{1,0:T(8,128)}, f32[264,256]{1,0:T(8,128)S(1)}, u32[]{:S(2)}, u32[]{:S(2)}) collective-permute-start(f32[264,256]{1,0:T(8,128)} %get-tuple-element.31), channel_id=1, source_target_pairs={{0,1},{1,0},{2,3},{3,2},{4,5},{5,4},{6,7},{7,6},{8,9},{9,8},{10,11... | collective-permute-start | bytes 811016 | tf_op jit(solution)/shard_map/ppermute | solution.py:17
  144.9 37.2 %collective-permute-start.10 = (f32[264,256]{1,0:T(8,128)}, f32[264,256]{1,0:T(8,128)}, u32[]{:S(2)}, u32[]{:S(2)}) collective-permute-start(f32[264,256]{1,0:T(8,128)} %get-tuple-element.35), channel_id=1, source_target_pairs={{0,2},{1,3},{2,0},{3,1},{4,6},{5,7},{6,4},{7,5},{8,10},{9,11},{10,... | collective-permute-start | bytes 811016 | tf_op jit(solution)/shard_map/ppermute | solution.py:17
  147.1 35.0 %collective-permute-start.11 = (f32[264,256]{1,0:T(8,128)}, f32[264,256]{1,0:T(8,128)}, u32[]{:S(2)}, u32[]{:S(2)}) collective-permute-start(f32[264,256]{1,0:T(8,128)} %get-tuple-element.37), channel_id=1, source_target_pairs={{0,3},{1,2},{2,1},{3,0},{4,7},{5,6},{6,5},{7,4},{8,11},{9,10},{10,... | collective-permute-start | bytes 811016 | tf_op jit(solution)/shard_map/ppermute | solution.py:17
  163.4 8.0 %copy-start.14 = (f32[264,256]{1,0:T(8,128)}, f32[264,256]{1,0:T(8,128)S(1)}, u32[]{:S(2)}) copy-start(f32[264,256]{1,0:T(8,128)S(1)} %collective-permute-done.13) | copy-start | bytes 811012
  173.2 16.8 %copy-start.9 = (f32[4,264,256]{2,1,0:T(8,128)}, f32[4,264,256]{2,1,0:T(8,128)S(1)}, u32[]{:S(2)}) copy-start(f32[4,264,256]{2,1,0:T(8,128)S(1)} %pad_maximum_fusion.1.refs_1_) | copy-start | bytes 3244036
  173.2 34.5 %collective-permute-start.21 = (f32[4,264,256]{2,1,0:T(8,128)S(1)}, f32[4,264,256]{2,1,0:T(8,128)}, u32[]{:S(2)}, u32[]{:S(2)}) collective-permute-start(f32[4,264,256]{2,1,0:T(8,128)S(1)} %pad_maximum_fusion.1.refs_1_), channel_id=1, source_target_pairs={{0,8},{8,16},{16,24},{24,0},{1,9},{9,17},{17,25},{25,1},{2,10},{10... | collective-permute-start | bytes 3244040 | tf_op jit(solution)/shard_map/ppermute | solution.py:17
  182.8 19.8 %copy-start.11 = (f32[264,256]{1,0:T(8,128)S(1)}, f32[264,256]{1,0:T(8,128)}, u32[]{:S(2)}) copy-start(f32[264,256]{1,0:T(8,128)} %get-tuple-element.33) | copy-start | bytes 811012
  185.1 23.8 %collective-permute-start.22 = (f32[4,264,256]{2,1,0:T(8,128)}, f32[4,264,256]{2,1,0:T(8,128)}, u32[]{:S(2)}, u32[]{:S(2)}) collective-permute-start(f32[4,264,256]{2,1,0:T(8,128)} %pad_maximum_fusion.refs_0_), channel_id=1, source_target_pairs={{0,24},{8,0},{16,8},{24,16},{1,25},{9,1},{17,9},{25,17},{2,26},{10... | collective-permute-start | bytes 3244040 | tf_op jit(solution)/shard_map/ppermute | solution.py:17
  186.5 8.8 %collective-permute-start.15 = (f32[264,256]{1,0:T(8,128)}, f32[264,256]{1,0:T(8,128)}, u32[]{:S(2)}, u32[]{:S(2)}) collective-permute-start(f32[264,256]{1,0:T(8,128)} %get-tuple-element.43), channel_id=1, source_target_pairs={{0,1},{1,0},{2,3},{3,2},{4,5},{5,4},{6,7},{7,6},{8,9},{9,8},{10,11... | collective-permute-start | bytes 811016 | tf_op jit(solution)/shard_map/ppermute | solution.py:17
  188.1 10.7 %collective-permute-start.16 = (f32[264,256]{1,0:T(8,128)}, f32[264,256]{1,0:T(8,128)}, u32[]{:S(2)}, u32[]{:S(2)}) collective-permute-start(f32[264,256]{1,0:T(8,128)} %get-tuple-element.44), channel_id=1, source_target_pairs={{0,2},{1,3},{2,0},{3,1},{4,6},{5,7},{6,4},{7,5},{8,10},{9,11},{10,... | collective-permute-start | bytes 811016 | tf_op jit(solution)/shard_map/ppermute | solution.py:17
  188.2 14.4 %collective-permute-start.17 = (f32[264,256]{1,0:T(8,128)}, f32[264,256]{1,0:T(8,128)}, u32[]{:S(2)}, u32[]{:S(2)}) collective-permute-start(f32[264,256]{1,0:T(8,128)} %get-tuple-element.45), channel_id=1, source_target_pairs={{0,3},{1,2},{2,1},{3,0},{4,7},{5,6},{6,5},{7,4},{8,11},{9,10},{10,... | collective-permute-start | bytes 811016 | tf_op jit(solution)/shard_map/ppermute | solution.py:17
  195.4 12.4 %collective-permute-start.19 = (f32[4,8,128]{2,1,0:T(8,128)S(1)}, f32[4,8,128]{2,1,0:T(8,128)S(1)}, u32[]{:S(2)}, u32[]{:S(2)}) collective-permute-start(f32[4,8,128]{2,1,0:T(8,128)S(1)} %slice.13), channel_id=1, source_target_pairs={{0,4},{1,5},{2,6},{3,7},{4,0},{5,1},{6,2},{7,3},{8,12},{9,13},{10,... | collective-permute-start | bytes 49160 | tf_op jit(solution)/shard_map/ppermute | solution.py:17
  198.8 9.0 %collective-permute-start.18 = (f32[4,8,128]{2,1,0:T(8,128)S(1)}, f32[4,8,128]{2,1,0:T(8,128)S(1)}, u32[]{:S(2)}, u32[]{:S(2)}) collective-permute-start(f32[4,8,128]{2,1,0:T(8,128)S(1)} %slice.12), channel_id=1, source_target_pairs={{0,4},{1,5},{2,6},{3,7},{4,0},{5,1},{6,2},{7,3},{8,12},{9,13},{10,... | collective-permute-start | bytes 49160 | tf_op jit(solution)/shard_map/ppermute | solution.py:17
  203.9 3.9 %copy-start.10 = (f32[4,264,256]{2,1,0:T(8,128)}, f32[4,264,256]{2,1,0:T(8,128)S(1)}, u32[]{:S(2)}) copy-start(f32[4,264,256]{2,1,0:T(8,128)S(1)} %pad_maximum_fusion.2.refs_2_) | copy-start | bytes 3244036
  203.9 5.0 %collective-permute-start.20 = (f32[4,8,128]{2,1,0:T(8,128)S(1)}, f32[4,8,128]{2,1,0:T(8,128)S(1)}, u32[]{:S(2)}, u32[]{:S(2)}) collective-permute-start(f32[4,8,128]{2,1,0:T(8,128)S(1)} %slice.14), channel_id=1, source_target_pairs={{0,4},{1,5},{2,6},{3,7},{4,0},{5,1},{6,2},{7,3},{8,12},{9,13},{10,... | collective-permute-start | bytes 49160 | tf_op jit(solution)/shard_map/ppermute | solution.py:17
  (13 other events, 16.5 us)

commit v6 on v5

--- a/solution.py
+++ b/solution.py
@@ -320,7 +320,7 @@
         for p, h, count in lot:
             for k in range(count):
                 where[p][h + k] = (len(near), k)
-            *outs, _ = turn(rows, at, count * NZ, high, low, occ_rows, 1.0 / depth)
+            *outs, dens = turn(rows, at, count * NZ, high, low, occ_rows, 1.0 / depth)
             at += count * NZ
             if not near:
                 gate = [rows, high]
@@ -329,7 +329,10 @@
                 waiting, near, far = back, [None], [None]
                 continue
             near.append(jnp.stack(back))
-            far.append(swap(near[-1][:, -EXTRA:, :NZ], group))
+            if lot is lots[-1]:
+                far.append(jnp.stack([swap(dens, group + s) for s in range(group)]))
+            else:
+                far.append(swap(near[-1][:, -EXTRA:, :NZ], group))
             if p == planes - 1:
                 before = send(near[-1], "dom", doms, lambda a: (a + 1) % doms)
     near[0] = jnp.stack([waiting[0]] + [after(block, [outs[0]]) for block in waiting[1:]])

time: 223 us -> 227 us (1.018)
    ppermute x23 -> x26, waiting for transfers between devices: 99.5 us -> 102 us  [send(): return lax.ppermute(block, axis, [(a, step(a)) for a in range(size)])]
    ppermute x23 -> x26, starting transfers between devices: 31.8 us -> 31.6 us  [send(): return lax.ppermute(block, axis, [(a, step(a)) for a in range(size)])]
    unnamed x40 -> x38, local copies, waits for them, and re-layouts: 16.6 us -> 16.7 us
  transfers between devices with their start and end apart: 25 -> 28, of which waited for: 11 -> 13; matrix products, arithmetic and copies ran while one was open for 3% -> 3% of each run, Pallas kernels for 16% -> 15%
where the time goes in v6:
time: 227 us; the launch traced here: 226 us
  waiting for transfers between devices  111 us (49%)
  starting transfers between devices  42.2 us (19%)
  Pallas kernels  41.3 us (18%)
  local copies, waits for them, and re-layouts  17.4 us (8%)
  other arithmetic  7.1 us (3%)
  blocking collectives  6.35 us (3%)
    ppermute x26, waiting for transfers between devices, send(): return lax.ppermute(block, axis, [(a, step(a)) for a in range(size)])  102 us
    ppermute x26, starting transfers between devices, send(): return lax.ppermute(block, axis, [(a, step(a)) for a in range(size)])  31.6 us
    pallas_call x3, Pallas kernels, turn(): pl.pallas_call(body, grid=(group,), in_specs=[pl.BlockSpec((count, rows,...  25.7 us
    unnamed x38, local copies, waits for them, and re-layouts  16.7 us
    all_to_all x2, starting transfers between devices, shards(): lax.all_to_all(rows, 'orb', split_axis=0, concat_axis=0, tiled=True)  10.6 us
    all_to_all x2, waiting for transfers between devices, shards(): lax.all_to_all(rows, 'orb', split_axis=0, concat_axis=0, tiled=True)  9.19 us
    pallas_call x1, Pallas kernels, finish(): pl.pallas_call(body, grid_spec=pltpu.PrefetchScalarGridSpec(num_scalar_pr...  6.71 us
    psum x1, blocking collectives, shards(): lax.psum(band.reshape(cols), 'dom')  6.35 us
  transfers between devices with their start and end apart: 28, of which 13 were waited for; matrix products, arithmetic and copies ran while one was open for 3% of the time, Pallas kernels for 15%

profile of v6, /device:TPU:0, one launch (start us, length us, event | category | flops | bytes accessed | tf_op | source)
XLA Modules:
  0.0 226.0 jit_solution(3261699319503463703)
XLA Ops:
  2.4 3.0 %collective-permute-start.3 = (f32[520,256]{1,0:T(8,128)S(1)}, f32[520,256]{1,0:T(8,128)}, u32[]{:S(2)}, u32[]{:S(2)}) collective-permute-start(f32[520,256]{1,0:T(8,128)S(1)} %get-tuple-element.52), channel_id=1, source_target_pairs={{0,1},{1,0},{2,3},{3,2},{4,5},{5,4},{6,7},{7,6},{8,9},{9,8},{10,11... | collective-permute-start | bytes 1597448 | tf_op jit(solution)/shard_map/ppermute | solution.py:17
  7.0 1.9 copy-done.1
  9.5 1.9 copy-done.5
  11.4 6.2 %all-to-all-start = ((f32[8,512,256]{2,1,0:T(8,128)}), f32[8,512,256]{2,1,0:T(8,128)}, u32[]{:S(2)}, u32[]{:S(2)}) async-start(f32[8,512,256]{2,1,0:T(8,128)} %bitcast.32), calls=%async_computation | async-start | bytes 8388608 | tf_op jit(solution)/shard_map/all_to_all | solution.py:318
  17.6 2.9 %collective-permute-done.4.refs_1_ = f32[520,256]{1,0:T(8,128)} collective-permute-done((f32[520,256]{1,0:T(8,128)S(1)}, f32[520,256]{1,0:T(8,128)}, u32[]{:S(2)}, u32[]{:S(2)}) %collective-permute-start.4) | collective-permute-done | bytes 532512 | tf_op jit(solution)/shard_map/ppermute | solution.py:17
  20.5 21.2 %collective-permute-done.5.refs_2_ = f32[520,256]{1,0:T(8,128)} collective-permute-done((f32[520,256]{1,0:T(8,128)S(1)}, f32[520,256]{1,0:T(8,128)}, u32[]{:S(2)}, u32[]{:S(2)}) %collective-permute-start.5) | collective-permute-done | bytes 532512 | tf_op jit(solution)/shard_map/ppermute | solution.py:17
  41.7 3.0 %collect.1.refs_4_ = f32[3,520,256]{2,1,0:T(8,128)} custom-call(f32[520,256]{1,0:T(8,128)} %collective-permute-done.3.refs_0_, f32[520,256]{1,0:T(8,128)} %collective-permute-done.4.refs_1_, f32[520,256]{1,0:T(8,128)} %collective-permute-done.5.refs_2_), custom_call_target="tpu_custom_call" | custom-call | flops 40000000000 | bytes 3194880 | tf_op jit(solution)/shard_map/collect/pallas_call | solution.py:66
  44.7 2.0 collective-permute-start.6
  46.7 32.9 %collective-permute-done.6.refs_5_ = f32[3,520,256]{2,1,0:T(8,128)} collective-permute-done((f32[3,520,256]{2,1,0:T(8,128)}, f32[3,520,256]{2,1,0:T(8,128)}, u32[]{:S(2)}, u32[]{:S(2)}) %collective-permute-start.6) | collective-permute-done | bytes 1597472 | tf_op jit(solution)/shard_map/ppermute | solution.py:17
  81.3 12.9 %collective-permute-done.refs_1_ = f32[1,520,256]{2,1,0:T(8,128)S(1)} collective-permute-done((f32[1,520,256]{2,1,0:T(8,128)S(1)}, f32[1,520,256]{2,1,0:T(8,128)S(1)}, u32[]{:S(2)}, u32[]{:S(2)}) %collective-permute-start) | collective-permute-done | bytes 532512 | tf_op jit(solution)/shard_map/ppermute | solution.py:17
  94.2 1.9 copy-done.2
  99.3 5.0 %split_rot.1 = (bf16[4,2048,256]{2,1,0:T(8,128)(2,1)S(1)}, bf16[4,2048,256]{2,1,0:T(8,128)(2,1)S(1)}, f32[4,8,256]{2,1,0:T(8,128)S(1)}) custom-call(s32[4]{0:T(128)S(1)} %pad_add_fusion.1.place, f32[1,520,256]{2,1,0:T(8,128)S(1)} %get-tuple-element.53.refs_0_, f32[1,520,256]{2,1,0:T(8,128)S(1)} %collective-permute-done.refs_1_, ...), custom_call_target="tpu_custom_call" | custom-call | tf_op jit(solution)/shard_map/split_rot/pallas_call | solution.py:105
  104.3 2.0 copy-done.3
  106.3 2.0 copy-done.4
  109.0 9.2 %all-to-all-done.x_ref = f32[8,512,256]{2,1,0:T(8,128)} async-done(((f32[8,512,256]{2,1,0:T(8,128)}), f32[8,512,256]{2,1,0:T(8,128)}, u32[]{:S(2)}, u32[]{:S(2)}) %all-to-all-start) | async-done | bytes 4194336 | tf_op jit(solution)/shard_map/all_to_all | solution.py:318
  118.1 4.4 %all-to-all-start.1 = ((f32[8,256,256]{2,1,0:T(8,128)}), f32[8,256,256]{2,1,0:T(8,128)}, u32[]{:S(2)}, u32[]{:S(2)}) async-start(f32[8,256,256]{2,1,0:T(8,128)} %bitcast.33), calls=%async_computation.1 | async-start | bytes 4194304 | tf_op jit(solution)/shard_map/all_to_all | solution.py:318
  122.5 8.5 %turn.5 = (f32[264,256]{1,0:T(8,128)}, f32[264,256]{1,0:T(8,128)}, f32[264,256]{1,0:T(8,128)}, f32[264,256]{1,0:T(8,128)}, f32[8,128]{1,0:T(8,128)}) custom-call(f32[8,512,256]{2,1,0:T(8,128)} %all-to-all-done.x_ref, bf16[4,2048,256]{2,1,0:T(8,128)(2,1)} %copy-done.3, bf16[4,2048,256]{2,1,0:T(8,128)(2,1)} %copy-done.4, f32[4,8,256]{2,1,0:T(8,128)} %copy-done.8), custom_call_target="tpu_custom_call" | custom-call | flops 3221225472 | bytes 12582912 | tf_op jit(solution)/shard_map/turn/pallas_call | solution.py:180
  131.0 1.9 collective-permute-start.12
  134.6 8.4 %turn.3 = (f32[264,256]{1,0:T(8,128)}, f32[264,256]{1,0:T(8,128)}, f32[264,256]{1,0:T(8,128)}, f32[264,256]{1,0:T(8,128)}, f32[8,128]{1,0:T(8,128)}) custom-call(f32[8,512,256]{2,1,0:T(8,128)} %all-to-all-done.x_ref, bf16[4,2048,256]{2,1,0:T(8,128)(2,1)} %copy-done.3, bf16[4,2048,256]{2,1,0:T(8,128)(2,1)} %copy-done.4, f32[4,8,256]{2,1,0:T(8,128)} %copy-done.8), custom_call_target="tpu_custom_call" | custom-call | flops 3221225472 | bytes 12582912 | tf_op jit(solution)/shard_map/turn/pallas_call | solution.py:180
  143.0 1.9 collective-permute-start.9
  147.2 3.5 %collective-permute-start.11 = (f32[264,256]{1,0:T(8,128)}, f32[264,256]{1,0:T(8,128)}, u32[]{:S(2)}, u32[]{:S(2)}) collective-permute-start(f32[264,256]{1,0:T(8,128)} %get-tuple-element.38), channel_id=1, source_target_pairs={{0,3},{1,2},{2,1},{3,0},{4,7},{5,6},{6,5},{7,4},{8,11},{9,10},{10,... | collective-permute-start | bytes 811016 | tf_op jit(solution)/shard_map/ppermute | solution.py:17
  150.7 12.7 %collective-permute-done.13 = f32[264,256]{1,0:T(8,128)S(1)} collective-permute-done((f32[264,256]{1,0:T(8,128)}, f32[264,256]{1,0:T(8,128)S(1)}, u32[]{:S(2)}, u32[]{:S(2)}) %collective-permute-start.13) | collective-permute-done | bytes 270368 | tf_op jit(solution)/shard_map/ppermute | solution.py:17
  163.5 8.0 %collective-permute-done.14 = f32[264,256]{1,0:T(8,128)S(1)} collective-permute-done((f32[264,256]{1,0:T(8,128)}, f32[264,256]{1,0:T(8,128)S(1)}, u32[]{:S(2)}, u32[]{:S(2)}) %collective-permute-start.14) | collective-permute-done | bytes 270368 | tf_op jit(solution)/shard_map/ppermute | solution.py:17
  173.4 8.8 %turn.4 = (f32[264,256]{1,0:T(8,128)}, f32[264,256]{1,0:T(8,128)}, f32[264,256]{1,0:T(8,128)}, f32[264,256]{1,0:T(8,128)}, f32[8,128]{1,0:T(8,128)}) custom-call(f32[8,256,256]{2,1,0:T(8,128)} %all-to-all-done.1.x_ref, bf16[4,2048,256]{2,1,0:T(8,128)(2,1)} %copy-done.3, bf16[4,2048,256]{2,1,0:T(8,128)(2,1)} %copy-done.4, f32[4,8,256]{2,1,0:T(8,128)} %copy-done.8), custom_call_target="tpu_custom_call" | custom-call | flops 3221225472 | bytes 12582912 | tf_op jit(solution)/shard_map/turn/pallas_call | solution.py:180
  182.9 2.3 %pad_maximum_fusion.refs_0_ = f32[4,264,256]{2,1,0:T(8,128)} fusion(f32[1,264,256]{2,1,0:T(8,128)} %bitcast.15, f32[1,264,256]{2,1,0:T(8,128)} %bitcast.14, f32[1,264,256]{2,1,0:T(8,128)} %bitcast.36, f32[1,264,256]{2,1,0:T(8,128)} %bitcast.35), kind=kLoop, calls=%fused_computation | loop fusion | flops 811008 | bytes 2162688 | tf_op jit(solution)/shard_map/stack | solution.py:338
  186.6 3.4 %collective-permute-start.20 = (f32[8,128]{1,0:T(8,128)S(1)}, f32[8,128]{1,0:T(8,128)S(1)}, u32[]{:S(2)}, u32[]{:S(2)}) collective-permute-start(f32[8,128]{1,0:T(8,128)S(1)} %copy-done.18), channel_id=1, source_target_pairs={{0,4},{1,5},{2,6},{3,7},{4,0},{5,1},{6,2},{7,3},{8,12},{9,13},{10,... | collective-permute-start | bytes 12296 | tf_op jit(solution)/shard_map/ppermute | solution.py:17
  192.0 2.7 %collective-permute-start.23 = (f32[8,128]{1,0:T(8,128)S(1)}, f32[8,128]{1,0:T(8,128)S(1)}, u32[]{:S(2)}, u32[]{:S(2)}) collective-permute-start(f32[8,128]{1,0:T(8,128)S(1)} %copy-done.18), channel_id=1, source_target_pairs={{0,7},{1,6},{2,5},{3,4},{4,3},{5,2},{6,1},{7,0},{8,15},{9,14},{10,... | collective-permute-start | bytes 12296 | tf_op jit(solution)/shard_map/ppermute | solution.py:17
  201.0 3.2 %collective-permute-done.15 = f32[264,256]{1,0:T(8,128)} collective-permute-done((f32[264,256]{1,0:T(8,128)}, f32[264,256]{1,0:T(8,128)}, u32[]{:S(2)}, u32[]{:S(2)}) %collective-permute-start.15) | collective-permute-done | bytes 270368 | tf_op jit(solution)/shard_map/ppermute | solution.py:17
  207.1 3.0 %collective-permute-done.17 = f32[264,256]{1,0:T(8,128)} collective-permute-done((f32[264,256]{1,0:T(8,128)}, f32[264,256]{1,0:T(8,128)}, u32[]{:S(2)}, u32[]{:S(2)}) %collective-permute-start.17) | collective-permute-done | bytes 270368 | tf_op jit(solution)/shard_map/ppermute | solution.py:17
  210.1 2.2 pad_maximum_fusion.2.refs_2_
  213.0 6.7 %finish.1 = (f32[3072,256]{1,0:T(8,128)}, f32[24,128]{1,0:T(8,128)}, f32[3072,256]{1,0:T(8,128)}, f32[1,256]{1,0:T(1,128)}) custom-call(s32[4]{0:T(128)} %pad_add_fusion.place, f32[4,264,256]{2,1,0:T(8,128)} %pad_maximum_fusion.refs_0_, f32[4,264,256]{2,1,0:T(8,128)} %copy-done.9, f32[4,264,256]{2,1,0:T(8,128)} %pad_maximum_fusion.2.refs_2_, ...), custom_call_target="tpu_custom_call" | custom-call | tf_op jit(solution)/shard_map/finish/pallas_call | solution.py:252
  219.7 6.3 %psum.7 = f32[256]{0:T(256)} all-reduce(f32[256]{0:T(256)} %bitcast.46), channel_id=1, replica_groups=mesh['dom'=4,'orb'=8] {'dom'}, use_global_device_ids=true, to_apply=%region_0.1 | all-reduce | flops 256 | bytes 2048 | tf_op jit(solution)/shard_map/psum | solution.py:345
  (82 shorter events, 28.9 us)
Async XLA Ops:
  2.4 15.2 %collective-permute-start.3 = (f32[520,256]{1,0:T(8,128)S(1)}, f32[520,256]{1,0:T(8,128)}, u32[]{:S(2)}, u32[]{:S(2)}) collective-permute-start(f32[520,256]{1,0:T(8,128)S(1)} %get-tuple-element.52), channel_id=1, source_target_pairs={{0,1},{1,0},{2,3},{3,2},{4,5},{5,4},{6,7},{7,6},{8,9},{9,8},{10,11... | collective-permute-start | bytes 1597448 | tf_op jit(solution)/shard_map/ppermute | solution.py:17
  5.4 15.1 %collective-permute-start.4 = (f32[520,256]{1,0:T(8,128)S(1)}, f32[520,256]{1,0:T(8,128)}, u32[]{:S(2)}, u32[]{:S(2)}) collective-permute-start(f32[520,256]{1,0:T(8,128)S(1)} %get-tuple-element.52), channel_id=1, source_target_pairs={{0,2},{1,3},{2,0},{3,1},{4,6},{5,7},{6,4},{7,5},{8,10},{9,11},{10,... | collective-permute-start | bytes 1597448 | tf_op jit(solution)/shard_map/ppermute | solution.py:17
  6.9 34.7 %collective-permute-start.5 = (f32[520,256]{1,0:T(8,128)S(1)}, f32[520,256]{1,0:T(8,128)}, u32[]{:S(2)}, u32[]{:S(2)}) collective-permute-start(f32[520,256]{1,0:T(8,128)S(1)} %get-tuple-element.52), channel_id=1, source_target_pairs={{0,3},{1,2},{2,1},{3,0},{4,7},{5,6},{6,5},{7,4},{8,11},{9,10},{10,... | collective-permute-start | bytes 1597448 | tf_op jit(solution)/shard_map/ppermute | solution.py:17
  11.4 106.8 %all-to-all-start = ((f32[8,512,256]{2,1,0:T(8,128)}), f32[8,512,256]{2,1,0:T(8,128)}, u32[]{:S(2)}, u32[]{:S(2)}) async-start(f32[8,512,256]{2,1,0:T(8,128)} %bitcast.32), calls=%async_computation | async-start | bytes 8388608 | tf_op jit(solution)/shard_map/all_to_all | solution.py:318
  44.7 35.0 %collective-permute-start.6 = (f32[3,520,256]{2,1,0:T(8,128)}, f32[3,520,256]{2,1,0:T(8,128)}, u32[]{:S(2)}, u32[]{:S(2)}) collective-permute-start(f32[3,520,256]{2,1,0:T(8,128)} %collect.1.refs_4_), channel_id=1, source_target_pairs={{0,16},{8,24},{16,0},{24,8},{1,17},{9,25},{17,1},{25,9},{2,18},{10... | collective-permute-start | bytes 4792328 | tf_op jit(solution)/shard_map/ppermute | solution.py:17
  46.7 51.1 %collective-permute-start.7 = (f32[3,520,256]{2,1,0:T(8,128)}, f32[3,520,256]{2,1,0:T(8,128)}, u32[]{:S(2)}, u32[]{:S(2)}) collective-permute-start(f32[3,520,256]{2,1,0:T(8,128)} %collect.1.refs_4_), channel_id=1, source_target_pairs={{0,8},{8,0},{16,24},{24,16},{1,9},{9,1},{17,25},{25,17},{2,10},{10... | collective-permute-start | bytes 4792328 | tf_op jit(solution)/shard_map/ppermute | solution.py:17
  79.7 18.2 %collective-permute-start.8 = (f32[3,520,256]{2,1,0:T(8,128)}, f32[3,520,256]{2,1,0:T(8,128)}, u32[]{:S(2)}, u32[]{:S(2)}) collective-permute-start(f32[3,520,256]{2,1,0:T(8,128)} %collective-permute-done.6.refs_5_), channel_id=1, source_target_pairs={{0,8},{8,0},{16,24},{24,16},{1,9},{9,1},{17,25},{25,17},{2,10},{10... | collective-permute-start | bytes 4792328 | tf_op jit(solution)/shard_map/ppermute | solution.py:17
  79.7 14.5 %collective-permute-start = (f32[1,520,256]{2,1,0:T(8,128)S(1)}, f32[1,520,256]{2,1,0:T(8,128)S(1)}, u32[]{:S(2)}, u32[]{:S(2)}) collective-permute-start(f32[1,520,256]{2,1,0:T(8,128)S(1)} %get-tuple-element.53.refs_0_), channel_id=1, source_target_pairs={{0,16},{8,24},{16,0},{24,8},{1,17},{9,25},{17,1},{25,9},{2,18},{10... | collective-permute-start | bytes 1597448 | tf_op jit(solution)/shard_map/ppermute | solution.py:17
  81.1 16.8 %collective-permute-start.1 = (f32[1,520,256]{2,1,0:T(8,128)S(1)}, f32[1,520,256]{2,1,0:T(8,128)}, u32[]{:S(2)}, u32[]{:S(2)}) collective-permute-start(f32[1,520,256]{2,1,0:T(8,128)S(1)} %get-tuple-element.53.refs_0_), channel_id=1, source_target_pairs={{0,8},{8,0},{16,24},{24,16},{1,9},{9,1},{17,25},{25,17},{2,10},{10... | collective-permute-start | bytes 1597448 | tf_op jit(solution)/shard_map/ppermute | solution.py:17
  94.2 3.6 %collective-permute-start.2 = (f32[1,520,256]{2,1,0:T(8,128)S(1)}, f32[1,520,256]{2,1,0:T(8,128)}, u32[]{:S(2)}, u32[]{:S(2)}) collective-permute-start(f32[1,520,256]{2,1,0:T(8,128)S(1)} %collective-permute-done.refs_1_), channel_id=1, source_target_pairs={{0,8},{8,0},{16,24},{24,16},{1,9},{9,1},{17,25},{25,17},{2,10},{10... | collective-permute-start | bytes 1597448 | tf_op jit(solution)/shard_map/ppermute | solution.py:17
  118.1 55.2 %all-to-all-start.1 = ((f32[8,256,256]{2,1,0:T(8,128)}), f32[8,256,256]{2,1,0:T(8,128)}, u32[]{:S(2)}, u32[]{:S(2)}) async-start(f32[8,256,256]{2,1,0:T(8,128)} %bitcast.33), calls=%async_computation.1 | async-start | bytes 4194304 | tf_op jit(solution)/shard_map/all_to_all | solution.py:318
  131.0 16.2 %collective-permute-start.12 = (f32[264,256]{1,0:T(8,128)}, f32[264,256]{1,0:T(8,128)S(1)}, u32[]{:S(2)}, u32[]{:S(2)}) collective-permute-start(f32[264,256]{1,0:T(8,128)} %get-tuple-element.41), channel_id=1, source_target_pairs={{0,1},{1,0},{2,3},{3,2},{4,5},{5,4},{6,7},{7,6},{8,9},{9,8},{10,11... | collective-permute-start | bytes 811016 | tf_op jit(solution)/shard_map/ppermute | solution.py:17
  133.0 30.5 %collective-permute-start.13 = (f32[264,256]{1,0:T(8,128)}, f32[264,256]{1,0:T(8,128)S(1)}, u32[]{:S(2)}, u32[]{:S(2)}) collective-permute-start(f32[264,256]{1,0:T(8,128)} %get-tuple-element.42), channel_id=1, source_target_pairs={{0,2},{1,3},{2,0},{3,1},{4,6},{5,7},{6,4},{7,5},{8,10},{9,11},{10,... | collective-permute-start | bytes 811016 | tf_op jit(solution)/shard_map/ppermute | solution.py:17
  134.4 37.7 %copy-start.12 = (f32[264,256]{1,0:T(8,128)S(1)}, f32[264,256]{1,0:T(8,128)}, u32[]{:S(2)}) copy-start(f32[264,256]{1,0:T(8,128)} %get-tuple-element.40) | copy-start | bytes 811012
  134.4 37.0 %collective-permute-start.14 = (f32[264,256]{1,0:T(8,128)}, f32[264,256]{1,0:T(8,128)S(1)}, u32[]{:S(2)}, u32[]{:S(2)}) collective-permute-start(f32[264,256]{1,0:T(8,128)} %get-tuple-element.43), channel_id=1, source_target_pairs={{0,3},{1,2},{2,1},{3,0},{4,7},{5,6},{6,5},{7,4},{8,11},{9,10},{10,... | collective-permute-start | bytes 811016 | tf_op jit(solution)/shard_map/ppermute | solution.py:17
  143.0 39.1 %collective-permute-start.9 = (f32[264,256]{1,0:T(8,128)}, f32[264,256]{1,0:T(8,128)S(1)}, u32[]{:S(2)}, u32[]{:S(2)}) collective-permute-start(f32[264,256]{1,0:T(8,128)} %get-tuple-element.32), channel_id=1, source_target_pairs={{0,1},{1,0},{2,3},{3,2},{4,5},{5,4},{6,7},{7,6},{8,9},{9,8},{10,11... | collective-permute-start | bytes 811016 | tf_op jit(solution)/shard_map/ppermute | solution.py:17
  144.9 37.2 %collective-permute-start.10 = (f32[264,256]{1,0:T(8,128)}, f32[264,256]{1,0:T(8,128)}, u32[]{:S(2)}, u32[]{:S(2)}) collective-permute-start(f32[264,256]{1,0:T(8,128)} %get-tuple-element.36), channel_id=1, source_target_pairs={{0,2},{1,3},{2,0},{3,1},{4,6},{5,7},{6,4},{7,5},{8,10},{9,11},{10,... | collective-permute-start | bytes 811016 | tf_op jit(solution)/shard_map/ppermute | solution.py:17
  147.2 35.0 %collective-permute-start.11 = (f32[264,256]{1,0:T(8,128)}, f32[264,256]{1,0:T(8,128)}, u32[]{:S(2)}, u32[]{:S(2)}) collective-permute-start(f32[264,256]{1,0:T(8,128)} %get-tuple-element.38), channel_id=1, source_target_pairs={{0,3},{1,2},{2,1},{3,0},{4,7},{5,6},{6,5},{7,4},{8,11},{9,10},{10,... | collective-permute-start | bytes 811016 | tf_op jit(solution)/shard_map/ppermute | solution.py:17
  163.5 8.0 %copy-start.13 = (f32[264,256]{1,0:T(8,128)}, f32[264,256]{1,0:T(8,128)S(1)}, u32[]{:S(2)}) copy-start(f32[264,256]{1,0:T(8,128)S(1)} %collective-permute-done.13) | copy-start | bytes 811012
  173.3 26.4 %copy-start.9 = (f32[4,264,256]{2,1,0:T(8,128)}, f32[4,264,256]{2,1,0:T(8,128)S(1)}, u32[]{:S(2)}) copy-start(f32[4,264,256]{2,1,0:T(8,128)S(1)} %pad_maximum_fusion.1.refs_1_) | copy-start | bytes 3244036
  173.3 39.0 %collective-permute-start.24 = (f32[4,264,256]{2,1,0:T(8,128)S(1)}, f32[4,264,256]{2,1,0:T(8,128)}, u32[]{:S(2)}, u32[]{:S(2)}) collective-permute-start(f32[4,264,256]{2,1,0:T(8,128)S(1)} %pad_maximum_fusion.1.refs_1_), channel_id=1, source_target_pairs={{0,8},{8,16},{16,24},{24,0},{1,9},{9,17},{17,25},{25,1},{2,10},{10... | collective-permute-start | bytes 3244040 | tf_op jit(solution)/shard_map/ppermute | solution.py:17
  182.9 27.2 %copy-start.10 = (f32[264,256]{1,0:T(8,128)S(1)}, f32[264,256]{1,0:T(8,128)}, u32[]{:S(2)}) copy-start(f32[264,256]{1,0:T(8,128)} %get-tuple-element.34) | copy-start | bytes 811012
  185.2 27.2 %collective-permute-start.25 = (f32[4,264,256]{2,1,0:T(8,128)}, f32[4,264,256]{2,1,0:T(8,128)}, u32[]{:S(2)}, u32[]{:S(2)}) collective-permute-start(f32[4,264,256]{2,1,0:T(8,128)} %pad_maximum_fusion.refs_0_), channel_id=1, source_target_pairs={{0,24},{8,0},{16,8},{24,16},{1,25},{9,1},{17,9},{25,17},{2,26},{10... | collective-permute-start | bytes 3244040 | tf_op jit(solution)/shard_map/ppermute | solution.py:17
  186.6 5.4 %collective-permute-start.20 = (f32[8,128]{1,0:T(8,128)S(1)}, f32[8,128]{1,0:T(8,128)S(1)}, u32[]{:S(2)}, u32[]{:S(2)}) collective-permute-start(f32[8,128]{1,0:T(8,128)S(1)} %copy-done.18), channel_id=1, source_target_pairs={{0,4},{1,5},{2,6},{3,7},{4,0},{5,1},{6,2},{7,3},{8,12},{9,13},{10,... | collective-permute-start | bytes 12296 | tf_op jit(solution)/shard_map/ppermute | solution.py:17
  190.0 5.4 %collective-permute-start.21 = (f32[8,128]{1,0:T(8,128)S(1)}, f32[8,128]{1,0:T(8,128)S(1)}, u32[]{:S(2)}, u32[]{:S(2)}) collective-permute-start(f32[8,128]{1,0:T(8,128)S(1)} %copy-done.18), channel_id=1, source_target_pairs={{0,5},{1,4},{2,7},{3,6},{4,1},{5,0},{6,3},{7,2},{8,13},{9,12},{10,... | collective-permute-start | bytes 12296 | tf_op jit(solution)/shard_map/ppermute | solution.py:17
  190.5 5.4 %collective-permute-start.22 = (f32[8,128]{1,0:T(8,128)S(1)}, f32[8,128]{1,0:T(8,128)S(1)}, u32[]{:S(2)}, u32[]{:S(2)}) collective-permute-start(f32[8,128]{1,0:T(8,128)S(1)} %copy-done.18), channel_id=1, source_target_pairs={{0,6},{1,7},{2,4},{3,5},{4,2},{5,3},{6,0},{7,1},{8,14},{9,15},{10,... | collective-permute-start | bytes 12296 | tf_op jit(solution)/shard_map/ppermute | solution.py:17
  192.0 6.4 %collective-permute-start.23 = (f32[8,128]{1,0:T(8,128)S(1)}, f32[8,128]{1,0:T(8,128)S(1)}, u32[]{:S(2)}, u32[]{:S(2)}) collective-permute-start(f32[8,128]{1,0:T(8,128)S(1)} %copy-done.18), channel_id=1, source_target_pairs={{0,7},{1,6},{2,5},{3,4},{4,3},{5,2},{6,1},{7,0},{8,15},{9,14},{10,... | collective-permute-start | bytes 12296 | tf_op jit(solution)/shard_map/ppermute | solution.py:17
  195.4 8.8 %collective-permute-start.15 = (f32[264,256]{1,0:T(8,128)}, f32[264,256]{1,0:T(8,128)}, u32[]{:S(2)}, u32[]{:S(2)}) collective-permute-start(f32[264,256]{1,0:T(8,128)} %get-tuple-element.44), channel_id=1, source_target_pairs={{0,1},{1,0},{2,3},{3,2},{4,5},{5,4},{6,7},{7,6},{8,9},{9,8},{10,11... | collective-permute-start | bytes 811016 | tf_op jit(solution)/shard_map/ppermute | solution.py:17
  195.9 9.6 %collective-permute-start.16 = (f32[264,256]{1,0:T(8,128)}, f32[264,256]{1,0:T(8,128)}, u32[]{:S(2)}, u32[]{:S(2)}) collective-permute-start(f32[264,256]{1,0:T(8,128)} %get-tuple-element.45), channel_id=1, source_target_pairs={{0,2},{1,3},{2,0},{3,1},{4,6},{5,7},{6,4},{7,5},{8,10},{9,11},{10,... | collective-permute-start | bytes 811016 | tf_op jit(solution)/shard_map/ppermute | solution.py:17
  198.4 11.7 %collective-permute-start.17 = (f32[264,256]{1,0:T(8,128)}, f32[264,256]{1,0:T(8,128)}, u32[]{:S(2)}, u32[]{:S(2)}) collective-permute-start(f32[264,256]{1,0:T(8,128)} %get-tuple-element.46), channel_id=1, source_target_pairs={{0,3},{1,2},{2,1},{3,0},{4,7},{5,6},{6,5},{7,4},{8,11},{9,10},{10,... | collective-permute-start | bytes 811016 | tf_op jit(solution)/shard_map/ppermute | solution.py:17
  204.2 8.1 %collective-permute-start.19 = (f32[4,8,128]{2,1,0:T(8,128)S(1)}, f32[4,8,128]{2,1,0:T(8,128)S(1)}, u32[]{:S(2)}, u32[]{:S(2)}) collective-permute-start(f32[4,8,128]{2,1,0:T(8,128)S(1)} %slice.9), channel_id=1, source_target_pairs={{0,4},{1,5},{2,6},{3,7},{4,0},{5,1},{6,2},{7,3},{8,12},{9,13},{10,... | collective-permute-start | bytes 49160 | tf_op jit(solution)/shard_map/ppermute | solution.py:17
  205.5 6.8 %collective-permute-start.18 = (f32[4,8,128]{2,1,0:T(8,128)S(1)}, f32[4,8,128]{2,1,0:T(8,128)S(1)}, u32[]{:S(2)}, u32[]{:S(2)}) collective-permute-start(f32[4,8,128]{2,1,0:T(8,128)S(1)} %slice.8), channel_id=1, source_target_pairs={{0,4},{1,5},{2,6},{3,7},{4,0},{5,1},{6,2},{7,3},{8,12},{9,13},{10,... | collective-permute-start | bytes 49160 | tf_op jit(solution)/shard_map/ppermute | solution.py:17
  (15 other events, 22.7 us)
